TPU v7x, 32 devices: a whole 2x2x4 slice. The times are simulated.
32 devices in a mesh: section: 4 (over y, x), dp: 8 (over z, core).
Axes of the slice: x: 2, y: 2, z: 4, core: 2. Of those that a mesh axis runs over, the one named last changes fastest.
Arguments:
- enc_in: bfloat16 [4, 2, 4096, 1152], P('section', None, 'dp'), may hold values from -6 to 6
- dec_in: bfloat16 [4, 2, 4096, 1152], P('section', None, 'dp'), may hold values from -6 to 6
- cotangent: bfloat16 [4, 2, 4096, 1152], P('section', None, 'dp'), may hold values from -0.23925781 to 0.23925781
- w_proj: float32 [4, 1152, 1152], P('section', 'dp'), may hold values from -0.1875 to 0.1875
- w_skip: float32 [4, 2304, 1152], P('section', 'dp'), may hold values from -0.125 to 0.125
- m_proj: float32 [4, 1152, 1152], P('section', 'dp'), may hold values from -3 to 3
- v_proj: float32 [4, 1152, 1152], P('section', 'dp'), may hold values from 0.05 to 1
- m_skip: float32 [4, 2304, 1152], P('section', 'dp'), may hold values from -3 to 3
- v_skip: float32 [4, 2304, 1152], P('section', 'dp'), may hold values from 0.05 to 1
Outputs:
- dec_out: bfloat16 [4, 2, 4096, 1152], P('section', None, 'dp')
- enc_grad: bfloat16 [4, 2, 4096, 1152], P('section', None, 'dp')
- dec_grad: bfloat16 [4, 2, 4096, 1152], P('section', None, 'dp')
- new_w_proj: float32 [4, 1152, 1152], P('section', 'dp')
- new_m_proj: float32 [4, 1152, 1152], P('section', 'dp')
- new_v_proj: float32 [4, 1152, 1152], P('section', 'dp')
- new_w_skip: float32 [4, 2304, 1152], P('section', 'dp')
- new_m_skip: float32 [4, 2304, 1152], P('section', 'dp')
- new_v_skip: float32 [4, 2304, 1152], P('section', 'dp')
All inputs are finite; a program needn't handle non-finite values.
Results may differ from a plain program's by a relative error of at most 0.025.
Values may be sent and summed in bfloat16 or wider, within the bound.
No kernel may reach another device: no remote copies, remote signals or barrier semaphores. Data moves between devices by JAX's collectives and lax.ppermute only.
A program may use at most 128 MiB of HBM per device.

v0:
```python
import jax
import jax.numpy as jnp
from jax import lax
from jax.sharding import PartitionSpec as P

half_root = 0.7071067811865476
gauss_norm = 0.3989422804014327
beta_one = 0.9
beta_two = 0.95
learn_rate = 0.002
adam_eps = 1e-08
correct_one = 1.0 - 0.9**10
correct_two = 1.0 - 0.95**10


def swapped(value, axis, bit):
    mask = 2**bit
    pairs = [(source, source ^ mask) for source in range(lax.axis_size(axis))]
    return lax.ppermute(value, axis, pairs)


def gelu_parts(preact):
    normal_cdf = 0.5 * (1.0 + lax.erf(preact * half_root))
    density = jnp.exp(-0.5 * preact * preact) * gauss_norm
    return (preact * normal_cdf, normal_cdf + preact * density)


def adam_update(weight, moment, second, grad):
    new_moment = beta_one * moment + (1.0 - beta_one) * grad
    new_second = beta_two * second + (1.0 - beta_two) * grad * grad
    step_size = new_moment / correct_one / (jnp.sqrt(new_second / correct_two) + adam_eps)
    return (weight - learn_rate * step_size, new_moment, new_second)


def top_bit():
    return lax.axis_size("section").bit_length() - 2


def send_forward(value):
    return swapped(value, "section", top_bit())


def send_backward(value):
    return swapped(value, "section", top_bit())


def layer_pass(enc_rows, dec_rows, out_grad, proj_full, skip_full):
    width = enc_rows.shape[1]
    skip_local = jnp.dot(enc_rows, proj_full, preferred_element_type=jnp.float32).astype(
        jnp.bfloat16
    )
    skip_remote = send_forward(skip_local)
    joined = jnp.concatenate([dec_rows, skip_remote], axis=1)
    preact = jnp.dot(joined, skip_full, preferred_element_type=jnp.float32)
    activated, gelu_slope = gelu_parts(preact)
    dec_out = activated.astype(jnp.bfloat16)
    pre_grad = (out_grad.astype(jnp.float32) * gelu_slope).astype(jnp.bfloat16)
    input_grad = jnp.einsum("rk,jk->rj", pre_grad, skip_full, preferred_element_type=jnp.float32)
    dec_grad = input_grad[:, :width].astype(jnp.bfloat16)
    skip_sent = input_grad[:, width:].astype(jnp.bfloat16)
    skip_grad = send_backward(skip_sent)
    enc_grad = jnp.einsum(
        "rk,jk->rj", skip_grad, proj_full, preferred_element_type=jnp.float32
    ).astype(jnp.bfloat16)
    grad_proj = jnp.einsum("rj,rk->jk", enc_rows, skip_grad, preferred_element_type=jnp.float32)
    grad_skip = jnp.einsum("rj,rk->jk", joined, pre_grad, preferred_element_type=jnp.float32)
    return (dec_out, enc_grad, dec_grad, grad_proj, grad_skip)


def body(enc_in, dec_in, cotangent, w_proj, w_skip, m_proj, v_proj, m_skip, v_skip):
    proj_all, skip_all = (
        lax.all_gather(w_proj.astype(jnp.bfloat16), "dp", axis=1, tiled=True),
        lax.all_gather(w_skip.astype(jnp.bfloat16), "dp", axis=1, tiled=True),
    )
    proj_full = proj_all[0]
    skip_full = skip_all[0]
    micro = enc_in.shape[1]
    tokens_here = enc_in.shape[2]
    width = enc_in.shape[3]
    rows = micro * tokens_here
    result = layer_pass(
        enc_in[0].reshape(rows, width),
        dec_in[0].reshape(rows, width),
        cotangent[0].reshape(rows, width),
        proj_full,
        skip_full,
    )
    dec_out = result[0].reshape(micro, tokens_here, width)
    enc_grad = result[1].reshape(micro, tokens_here, width)
    dec_grad = result[2].reshape(micro, tokens_here, width)
    proj_sum, skip_sum = (
        lax.psum_scatter(
            result[3].astype(jnp.bfloat16), "dp", scatter_dimension=0, tiled=True
        ).astype(jnp.float32),
        lax.psum_scatter(
            result[4].astype(jnp.bfloat16), "dp", scatter_dimension=0, tiled=True
        ).astype(jnp.float32),
    )
    new_w_proj, new_m_proj, new_v_proj = adam_update(w_proj[0], m_proj[0], v_proj[0], proj_sum)
    new_w_skip, new_m_skip, new_v_skip = adam_update(w_skip[0], m_skip[0], v_skip[0], skip_sum)
    return (
        dec_out[None],
        enc_grad[None],
        dec_grad[None],
        new_w_proj[None],
        new_m_proj[None],
        new_v_proj[None],
        new_w_skip[None],
        new_m_skip[None],
        new_v_skip[None],
    )


def solution(mesh):
    in_specs = (
        P("section", None, "dp", None),
        P("section", None, "dp", None),
        P("section", None, "dp", None),
        P("section", "dp", None),
        P("section", "dp", None),
        P("section", "dp", None),
        P("section", "dp", None),
        P("section", "dp", None),
        P("section", "dp", None),
    )
    out_specs = (
        P("section", None, "dp", None),
        P("section", None, "dp", None),
        P("section", None, "dp", None),
        P("section", "dp", None),
        P("section", "dp", None),
        P("section", "dp", None),
        P("section", "dp", None),
        P("section", "dp", None),
        P("section", "dp", None),
    )
    return jax.shard_map(body, mesh=mesh, in_specs=in_specs, out_specs=out_specs, check_vma=False)
```

profile of v0, /device:TPU:0, one launch (start us, length us, event | category | flops | bytes accessed | tf_op | source)
XLA Modules:
  0.0 301.6 jit_solution(14259255035393955461)
XLA Ops:
  7.2 2.0 convert_element_type.41
  9.3 0.0 all-gather.5.cloned.1.call-start
  9.3 2.2 convert_element_type.43
  11.6 0.0 reduce-scatter.7.cloned.1.call-start
  11.6 35.5 %all-gather.3.cloned.1.call-done = bf16[1,1152,1152]{2,1,0:T(8,128)(2,1)} async-done(((bf16[1,144,1152]{2,1,0:T(8,128)(2,1)}), bf16[1,1152,1152]{2,1,0:T(8,128)(2,1)}) %all-gather.3.cloned.1.call-update) | async-done | bytes 2654224 | tf_op jit(solution)/shard_map/all_gather | solution.py:72
  47.1 5.4 %convolution_convert_fusion.4 = bf16[1024,1152]{1,0:T(8,128)(2,1)S(1)} fusion(bf16[1024,1152]{1,0:T(8,128)(2,1)S(1)} %bitcast.73, bf16[1,1152,1152]{2,1,0:T(8,128)(2,1)} %all-gather.3.cloned.1.call-done), kind=kOutput, calls=%fused_computation.18 | convolution fusion | flops 2719088640 | bytes 7372800 | tf_op jit(solution)/shard_map/dot_general | solution.py:49
  52.6 1.5 collective-permute-start
  54.1 52.0 %collective-permute-done = bf16[1024,1152]{1,0:T(8,128)(2,1)} collective-permute-done((bf16[1024,1152]{1,0:T(8,128)(2,1)S(1)}, bf16[1024,1152]{1,0:T(8,128)(2,1)}, u32[]{:S(2)}, u32[]{:S(2)}) %collective-permute-start) | collective-permute-done | bytes 2359328 | tf_op jit(solution)/shard_map/ppermute | solution.py:19
  106.2 12.5 %fusion.9 = (bf16[1024,1152]{1,0:T(8,128)(2,1)S(1)}, bf16[1024,1152]{1,0:T(8,128)(2,1)}) fusion(bf16[1,2,512,1152]{3,2,1,0:T(8,128)(2,1)} %param.11, bf16[1,2304,1152]{2,1,0:T(8,128)(2,1)} %all-gather.5.cloned.1.call-done, bf16[1024,1152]{1,0:T(8,128)(2,1)} %collective-permute-done, bf16[1024,1152]{1,0:T(8,128)(2,1)} %bitcast.76), kind=kOutput, calls=%fused_computation.13 | convolution fusion | flops 5460590592 | bytes 17104896 | tf_op jit(solution)/shard_map/dot_general | solution.py:54
  118.7 6.5 %convolution_convert_fusion.2 = bf16[1024,2304]{1,0:T(8,128)(2,1)S(1)} fusion(bf16[1024,1152]{1,0:T(8,128)(2,1)S(1)} %get-tuple-element.29, bf16[1,2304,1152]{2,1,0:T(8,128)(2,1)S(1)} %copy-done.5), kind=kOutput, calls=%fused_computation.4 | convolution fusion | flops 5438177280 | bytes 12386304 | tf_op jit(solution)/shard_map/rk,jk->rj/dot_general | solution.py:58
  125.2 1.8 fusion.24
  127.0 1.5 collective-permute-start.1
  128.5 51.1 %collective-permute-done.1 = bf16[1024,1152]{1,0:T(8,128)(2,1)S(1)} collective-permute-done((bf16[1024,1152]{1,0:T(8,128)(2,1)S(1)}, bf16[1024,1152]{1,0:T(8,128)(2,1)S(1)}, u32[]{:S(2)}, u32[]{:S(2)}) %collective-permute-start.1) | collective-permute-done | bytes 2359328 | tf_op jit(solution)/shard_map/ppermute | solution.py:19
  179.6 1.5 copy-done.7
  181.1 4.8 %fusion = bf16[1152,1152]{0,1:T(8,128)(2,1)} fusion(bf16[1024,1152]{1,0:T(8,128)(2,1)S(1)} %collective-permute-done.1, bf16[1024,1152]{1,0:T(8,128)(2,1)S(1)} %bitcast.74), kind=kOutput, calls=%fused_computation.3 | convolution fusion | flops 2719236096 | bytes 7372800 | tf_op jit(solution)/shard_map/rj,rk->jk/dot_general | solution.py:65
  185.9 5.2 %copy.30 = bf16[1152,1152]{1,0:T(8,128)(2,1)} copy(bf16[1152,1152]{0,1:T(8,128)(2,1)} %fusion) | data formatting | bytes 5308416
  191.1 0.2 reduce-scatter.5.cloned.1.call-start
  191.4 1.4 copy-done.6
  192.8 9.9 %convolution_convert_fusion = bf16[2304,1152]{1,0:T(8,128)(2,1)} fusion(bf16[1024,1152]{1,0:T(8,128)(2,1)} %copy-done.8, bf16[1024,1152]{1,0:T(8,128)(2,1)} %collective-permute-done, bf16[1024,1152]{1,0:T(8,128)(2,1)S(1)} %bitcast.77), kind=kOutput, calls=%fused_computation | convolution fusion | flops 5447909376 | bytes 12386304 | tf_op jit(solution)/shard_map/rj,rk->jk/dot_general | solution.py:66
  202.7 1.1 copy-done.3
  203.8 0.4 copy.24
  204.1 0.4 copy.26
  204.5 1.5 copy.25
  206.0 7.5 %convolution_convert_fusion.3 = bf16[1024,1152]{1,0:T(8,128)(2,1)} fusion(bf16[1024,1152]{1,0:T(8,128)(2,1)} %copy-done.7, bf16[1,1152,1152]{2,1,0:T(8,128)(2,1)} %all-gather.3.cloned.1.call-done), kind=kOutput, calls=%fused_computation.17 | convolution fusion | flops 2719088640 | bytes 7372800 | tf_op jit(solution)/shard_map/rk,jk->rj/dot_general | solution.py:62
  213.5 14.6 %reduce-scatter.7.cloned.1.call-done = bf16[144,1152]{1,0:T(8,128)(2,1)} async-done(((bf16[1152,1152]{1,0:T(8,128)(2,1)}), bf16[144,1152]{1,0:T(8,128)(2,1)}) %reduce-scatter.7.cloned.1.call-update) | async-done | bytes 331792
  228.0 2.0 copy.31
  230.1 3.7 %fusion.21 = (f32[1,144,1152]{1,2,0:T(8,128)}, f32[1,144,1152]{1,2,0:T(8,128)}, f32[1,144,1152]{1,2,0:T(8,128)}) fusion(bf16[144,1152]{0,1:T(8,128)(2,1)} %copy.31, f32[1,144,1152]{1,2,0:T(8,128)S(1)} %copy.26, f32[1,144,1152]{1,2,0:T(8,128)S(1)} %copy.25, f32[1,144,1152]{1,2,0:T(8,128)S(1)} %copy.24), kind=kLoop, calls=%fused_computation.36 | loop fusion | flops 2322432 | bytes 4313088 | tf_op jit(solution)/shard_map/broadcast_in_dim | solution.py:107
  233.7 2.5 copy.27
  236.3 2.4 copy.28
  238.7 1.2 copy.29
  239.9 50.0 %reduce-scatter.5.cloned.1.call-done = bf16[288,1152]{1,0:T(8,128)(2,1)} async-done(((bf16[2304,1152]{1,0:T(8,128)(2,1)}), bf16[288,1152]{1,0:T(8,128)(2,1)}) %reduce-scatter.5.cloned.1.call-update) | async-done | bytes 663568 | tf_op jit(solution)/shard_map/reduce_scatter | solution.py:95
  289.9 5.2 %fusion.19 = (f32[1,288,1152]{2,1,0:T(8,128)}, f32[1,288,1152]{2,1,0:T(8,128)}, f32[1,288,1152]{2,1,0:T(8,128)}) fusion(bf16[288,1152]{1,0:T(8,128)(2,1)} %reduce-scatter.5.cloned.1.call-done, f32[1,288,1152]{2,1,0:T(8,128)} %param.17, f32[1,288,1152]{2,1,0:T(8,128)} %param.16, f32[1,288,1152]{2,1,0:T(8,128)} %param.13), kind=kLoop, calls=%fused_computation.34 | loop fusion | flops 4644864 | bytes 8626176 | tf_op jit(solution)/shard_map/broadcast_in_dim | solution.py:110
  (21 shorter events, 0.1 us)
Async XLA Ops:
  7.2 40.0 %copy-start = (bf16[1,2,512,1152]{3,2,1,0:T(8,128)(2,1)S(1)}, bf16[1,2,512,1152]{3,2,1,0:T(8,128)(2,1)}, u32[]{:S(2)}) copy-start(bf16[1,2,512,1152]{3,2,1,0:T(8,128)(2,1)} %param.9) | copy-start | bytes 7077892
  7.2 39.9 %all-gather.3.cloned.1.call-start = ((), (), s32[]{:S(2)}) async-start(), calls=%async_computation.2 | async-start | bytes 2985984 | tf_op jit(solution)/shard_map/all_gather | solution.py:72
  9.3 96.9 %all-gather.5.cloned.1.call-start = ((), (), s32[]{:S(2)}) async-start(), calls=%async_computation.3 | async-start | bytes 5971968 | tf_op jit(solution)/shard_map/all_gather | solution.py:73
  11.6 216.5 %reduce-scatter.7.cloned.1.call-start = ((), (), s32[]{:S(2)}) async-start(), calls=%async_computation.5 | async-start | bytes 2985984
  52.6 53.6 %collective-permute-start = (bf16[1024,1152]{1,0:T(8,128)(2,1)S(1)}, bf16[1024,1152]{1,0:T(8,128)(2,1)}, u32[]{:S(2)}, u32[]{:S(2)}) collective-permute-start(bf16[1024,1152]{1,0:T(8,128)(2,1)S(1)} %convolution_convert_fusion.4), channel_id=1, source_target_pairs={{0,16},{8,24},{16,0},{24,8},{1,17},{9,25},{17,1},{25,9},{2,18},{10... | collective-permute-start | bytes 7077896 | tf_op jit(solution)/shard_map/ppermute | solution.py:19
  106.1 12.6 %copy-start.5 = (bf16[1,2304,1152]{2,1,0:T(8,128)(2,1)S(1)}, bf16[1,2304,1152]{2,1,0:T(8,128)(2,1)}, u32[]{:S(2)}) copy-start(bf16[1,2304,1152]{2,1,0:T(8,128)(2,1)} %all-gather.5.cloned.1.call-done) | copy-start | bytes 15925252
  118.7 6.5 %copy-start.8 = (bf16[1024,1152]{1,0:T(8,128)(2,1)}, bf16[1024,1152]{1,0:T(8,128)(2,1)S(1)}, u32[]{:S(2)}) copy-start(bf16[1024,1152]{1,0:T(8,128)(2,1)S(1)} %get-tuple-element.29) | copy-start | bytes 7077892
  127.0 52.6 %collective-permute-start.1 = (bf16[1024,1152]{1,0:T(8,128)(2,1)S(1)}, bf16[1024,1152]{1,0:T(8,128)(2,1)S(1)}, u32[]{:S(2)}, u32[]{:S(2)}) collective-permute-start(bf16[1024,1152]{1,0:T(8,128)(2,1)S(1)} %get-tuple-element.28), channel_id=1, source_target_pairs={{0,16},{8,24},{16,0},{24,8},{1,17},{9,25},{17,1},{25,9},{2,18},{10... | collective-permute-start | bytes 7077896 | tf_op jit(solution)/shard_map/ppermute | solution.py:19
  179.6 1.5 copy-start.7
  191.1 1.7 copy-start.6
  191.1 98.8 %reduce-scatter.5.cloned.1.call-start = ((), (), s32[]{:S(2)}) async-start(), calls=%async_computation.4 | async-start | bytes 5971968 | tf_op jit(solution)/shard_map/reduce_scatter | solution.py:95
  202.7 1.1 copy-start.3
  202.7 1.5 copy-start.4
  233.7 5.0 %copy-start.2 = (f32[1,144,1152]{1,2,0:T(8,128)S(1)}, f32[1,144,1152]{1,2,0:T(8,128)}, u32[]{:S(2)}) copy-start(f32[1,144,1152]{1,2,0:T(8,128)} %get-tuple-element.34) | copy-start | bytes 1990660
  238.7 56.3 %copy-start.1 = (bf16[1,2,512,1152]{3,2,1,0:T(8,128)(2,1)S(1)}, bf16[1,2,512,1152]{3,2,1,0:T(8,128)(2,1)}, u32[]{:S(2)}) copy-start(bf16[1,2,512,1152]{3,2,1,0:T(8,128)(2,1)} %param.9) | copy-start | bytes 7077892
Sparse Core Ops, SparseCore 0:
  10.2 36.8 all-gather.2
  49.3 55.5 all-gather.4
  191.2 36.7 reduce-scatter.6
  230.2 59.6 reduce-scatter.4
where the time goes:
time: 302 us
  waiting for transfers between devices  203 us (67%)
  matrix products  46.7 us (15%)
  local copies, waits for them, and re-layouts  21.4 us (7%)
  between operations  13.9 us (5%)
  other arithmetic  13.1 us (4%)
  starting transfers between devices  3.36 us (1%)
    ppermute x2, waiting for transfers between devices, swapped(): return lax.ppermute(value, axis, pairs)  103 us
    reduce_scatter x1, waiting for transfers between devices, body(): lax.psum_scatter(result[4].astype(jnp.bfloat16), 'dp', scatter_dimension=...  50 us
    all_gather x1, waiting for transfers between devices, body(): lax.all_gather(w_proj.astype(jnp.bfloat16), 'dp', axis=1, tiled=True)  35.5 us
    unnamed x26, local copies, waits for them, and re-layouts  19.6 us
    unnamed x5, waiting for transfers between devices  14.6 us
    dot_general x1, matrix products, layer_pass(): preact = jnp.dot(joined, skip_full, preferred_element_type=jnp.float32)  12.5 us
    dot_general x1, matrix products, layer_pass(): jnp.einsum('rj,rk->jk', joined, pre_grad, preferred_element_type=jnp.floa...  9.9 us
    dot_general x1, matrix products, layer_pass(): jnp.einsum('rk,jk->rj', skip_grad, proj_full, preferred_element_type=jnp....  7.46 us
  transfers between devices with their start and end apart: 6, of which 5 were waited for; matrix products, arithmetic and copies ran while one was open for 13% of the time, Pallas kernels for 0%

commit v1 on v0

v1 whole, which is shorter than its diff:
```python
import jax
import jax.numpy as jnp
from jax import lax
from jax.sharding import PartitionSpec as P

half_root = 0.7071067811865476
gauss_norm = 0.3989422804014327
beta_one = 0.9
beta_two = 0.95
learn_rate = 0.002
adam_eps = 1e-08
correct_one = 1.0 - 0.9**10
correct_two = 1.0 - 0.95**10


def gelu_parts(preact):
    normal_cdf = 0.5 * (1.0 + lax.erf(preact * half_root))
    density = jnp.exp(-0.5 * preact * preact) * gauss_norm
    return (preact * normal_cdf, normal_cdf + preact * density)


def adam_update(weight, moment, second, grad):
    new_moment = beta_one * moment + (1.0 - beta_one) * grad
    new_second = beta_two * second + (1.0 - beta_two) * grad * grad
    step_size = new_moment / correct_one / (jnp.sqrt(new_second / correct_two) + adam_eps)
    return (weight - learn_rate * step_size, new_moment, new_second)


def to_partner(value):
    count = lax.axis_size("section")
    pairs = [(s, (s + count // 2) % count) for s in range(count)]
    return lax.ppermute(value, "section", pairs)


def chip_count():
    return lax.axis_size("dp") // 2


def to_chips(value, pairs):
    return lax.ppermute(value, "dp", [(2 * a + c, 2 * b + c) for a, b in pairs for c in range(2)])


def chip_flip(value, mask):
    return to_chips(value, [(z, z ^ mask) for z in range(chip_count())])


def core_flip(value):
    return lax.ppermute(value, "dp", [(d, d ^ 1) for d in range(lax.axis_size("dp"))])


def gather_chips(piece):
    held = [piece]
    step = chip_count() // 2
    found = {0: piece}
    while step:
        came = {k + step: chip_flip(found[k], step) for k in sorted(found)}
        found.update(came)
        step //= 2
    return [found[k] for k in range(chip_count())]


def plus(*terms):
    total = terms[0].astype(jnp.float32)
    for term in terms[1:]:
        total = total + term.astype(jnp.float32)
    return total


def scatter_chips(blocks):
    chips = chip_count()
    step = 1
    while step < chips // 2:
        came = {k: chip_flip(blocks[k + step], step) for k in range(0, chips, 2 * step) if k}
        for k in came:
            blocks[k] = plus(blocks[k], came[k]).astype(jnp.bfloat16)
        step *= 2
    terms, step = [blocks[0]], 1
    while step < chips:
        terms.append(chip_flip(blocks[step], step))
        step *= 2
    return plus(*terms)


def gather_rows(piece):
    chips = chip_count()
    place = lax.axis_index("dp")
    chip, core = place // 2, place % 2
    mine = gather_chips(piece)
    whole = jnp.zeros((chips, 2) + piece.shape, piece.dtype)
    for k in range(chips):
        whole = lax.dynamic_update_slice(whole, mine[k][None, None], (chip ^ k, core, 0, 0))
        whole = lax.dynamic_update_slice(whole, core_flip(mine[k])[None, None], (chip ^ k, 1 - core, 0, 0))
    return whole.reshape(-1, piece.shape[1])


def scatter_rows(total):
    chips = chip_count()
    place = lax.axis_index("dp")
    chip, core = place // 2, place % 2
    split = total.reshape(chips, 2, -1, total.shape[1])
    keep = lax.dynamic_index_in_dim(split, core, 1, keepdims=False)
    send = lax.dynamic_index_in_dim(split, 1 - core, 1, keepdims=False)
    both = plus(keep, core_flip(send)).astype(jnp.bfloat16)
    return scatter_chips([lax.dynamic_index_in_dim(both, chip ^ k, 0, keepdims=False) for k in range(chips)])


def matmul(left, right):
    return jnp.dot(left, right, preferred_element_type=jnp.float32)


def body(enc_in, dec_in, cotangent, w_proj, w_skip, m_proj, v_proj, m_skip, v_skip):
    micro, tokens_here, width = enc_in.shape[1:]
    rows = micro * tokens_here
    enc_rows = enc_in[0].reshape(rows, width)
    dec_rows = dec_in[0].reshape(rows, width)
    out_grad = cotangent[0].reshape(rows, width)

    proj_other = to_partner(w_proj[0].astype(jnp.bfloat16))
    enc_other = to_partner(enc_rows)
    skip_full = gather_rows(w_skip[0].astype(jnp.bfloat16))
    proj_full = gather_rows(proj_other)
    upper, lower = skip_full[:width], skip_full[width:]

    skip = matmul(enc_other, proj_full).astype(jnp.bfloat16)
    preact = matmul(dec_rows, upper) + matmul(skip, lower)
    activated, gelu_slope = gelu_parts(preact)
    dec_out = activated.astype(jnp.bfloat16)
    pre_grad = (out_grad.astype(jnp.float32) * gelu_slope).astype(jnp.bfloat16)

    skip_grad = jnp.einsum("rk,jk->rj", pre_grad, lower, preferred_element_type=jnp.float32).astype(jnp.bfloat16)
    grad_proj = jnp.einsum("rj,rk->jk", enc_other, skip_grad, preferred_element_type=jnp.float32).astype(jnp.bfloat16)
    proj_sum = to_partner(scatter_rows(grad_proj).astype(jnp.bfloat16)).astype(jnp.float32)
    enc_grad = to_partner(
        jnp.einsum("rk,jk->rj", skip_grad, proj_full, preferred_element_type=jnp.float32).astype(jnp.bfloat16)
    )
    grad_upper = jnp.einsum("rj,rk->jk", dec_rows, pre_grad, preferred_element_type=jnp.float32).astype(jnp.bfloat16)
    grad_lower = jnp.einsum("rj,rk->jk", skip, pre_grad, preferred_element_type=jnp.float32).astype(jnp.bfloat16)
    skip_sum = scatter_rows(jnp.concatenate([grad_upper, grad_lower], axis=0))
    dec_grad = jnp.einsum("rk,jk->rj", pre_grad, upper, preferred_element_type=jnp.float32).astype(jnp.bfloat16)

    new_proj = adam_update(w_proj[0], m_proj[0], v_proj[0], proj_sum)
    new_skip = adam_update(w_skip[0], m_skip[0], v_skip[0], skip_sum)
    streams = tuple(value.reshape(1, micro, tokens_here, width) for value in (dec_out, enc_grad, dec_grad))
    return streams + tuple(value[None] for value in new_proj + new_skip)


def solution(mesh):
    tokens = P("section", None, "dp", None)
    weights = P("section", "dp", None)
    return jax.shard_map(
        body,
        mesh=mesh,
        in_specs=(tokens,) * 3 + (weights,) * 6,
        out_specs=(tokens,) * 3 + (weights,) * 6,
        check_vma=False,
    )
```

time: 302 us -> 216 us (0.72)
  waiting for transfers between devices: 203 us -> 120 us
  starting transfers between devices: 3.36 us -> 20.5 us
  between operations: 13.9 us -> 0.98 us
  matrix products: 46.7 us -> 43.3 us
  local copies, waits for them, and re-layouts: 21.4 us -> 18.3 us
    reduce_scatter x1 -> x0, waiting for transfers between devices: 50 us -> none  [body(): lax.psum_scatter(result[4].astype(jnp.bfloat16), 'dp', scatter_dimension=...]
    all_gather x2 -> x0, waiting for transfers between devices: 35.5 us -> none  [the longest x1 35.5 us: body(): lax.all_gather(w_proj.astype(jnp.bfloat16), 'dp', axis=1, tiled=True)]
    unnamed x26 -> x33, local copies, waits for them, and re-layouts: 19.6 us -> 2 us
    ppermute x2 -> x26, starting transfers between devices: 3.02 us -> 20.5 us  [the longest x12 12.9 us: to_chips(): lax.ppermute(value, 'dp', [(2 * a + c, 2 * b + c) for a, b in pairs for c...]
    ppermute x2 -> x26, waiting for transfers between devices: 103 us -> 120 us  [the longest x12 80.1 us: to_chips(): lax.ppermute(value, 'dp', [(2 * a + c, 2 * b + c) for a, b in pairs for c...]
    unnamed x5 -> x0, waiting for transfers between devices: 14.6 us -> none
    dynamic_update_slice x0 -> x15, local copies, waits for them, and re-layouts: none -> 8.84 us  [the longest x8 4.89 us: gather_rows(): lax.dynamic_update_slice(whole, core_flip(mine[k])[None, None], (chip ^ k...]
    broadcast_in_dim x2, other arithmetic: 8.88 us -> 4.83 us  [body(): return streams + tuple((value[None] for value in new_proj + new_skip))]
  transfers between devices with their start and end apart: 6 -> 26, of which waited for: 5 -> 12; matrix products, arithmetic and copies ran while one was open for 13% -> 16% of each run, Pallas kernels for 0% -> 0%
where the time goes in v1:
time: 216 us
  waiting for transfers between devices  120 us (56%)
  matrix products  43.3 us (20%)
  starting transfers between devices  20.5 us (9%)
  local copies, waits for them, and re-layouts  18.3 us (8%)
  other arithmetic  13.2 us (6%)
    ppermute x12, waiting for transfers between devices, to_chips(): lax.ppermute(value, 'dp', [(2 * a + c, 2 * b + c) for a, b in pairs for c...  80.1 us
    ppermute x4, waiting for transfers between devices, to_partner(): return lax.ppermute(value, 'section', pairs)  37.2 us
    dot_general x3, matrix products, matmul(): return jnp.dot(left, right, preferred_element_type=jnp.float32)  16.4 us
    ppermute x12, starting transfers between devices, to_chips(): lax.ppermute(value, 'dp', [(2 * a + c, 2 * b + c) for a, b in pairs for c...  12.9 us
    ppermute x4, starting transfers between devices, to_partner(): return lax.ppermute(value, 'section', pairs)  5.18 us
    dot_general x1, matrix products, body(): jnp.einsum('rj,rk->jk', enc_other, skip_grad, preferred_element_type=jnp....  5.16 us
    dynamic_update_slice x8, local copies, waits for them, and re-layouts, gather_rows(): lax.dynamic_update_slice(whole, core_flip(mine[k])[None, None], (chip ^ k...  4.89 us
    dot_general x1, matrix products, body(): jnp.einsum('rj,rk->jk', dec_rows, pre_grad, preferred_element_type=jnp.fl...  4.87 us
  transfers between devices with their start and end apart: 26, of which 12 were waited for; matrix products, arithmetic and copies ran while one was open for 16% of the time, Pallas kernels for 0%

profile of v1, /device:TPU:0, one launch (start us, length us, event | category | flops | bytes accessed | tf_op | source)
XLA Modules:
  0.0 215.7 jit_solution(10817548660690006547)
XLA Ops:
  0.7 2.4 %bitcast_convert_fusion = bf16[288,1152]{1,0:T(8,128)(2,1)} fusion(f32[1,288,1152]{2,1,0:T(8,128)} %param.13), kind=kLoop, calls=%fused_computation.32 | loop fusion | flops 331776 | bytes 1990656 | tf_op jit(solution)/shard_map/convert_element_type | solution.py:120
  3.5 2.6 %collective-permute-start.1 = (bf16[288,1152]{1,0:T(8,128)(2,1)}, bf16[288,1152]{1,0:T(8,128)(2,1)}, u32[]{:S(2)}, u32[]{:S(2)}) collective-permute-start(bf16[288,1152]{1,0:T(8,128)(2,1)} %bitcast_convert_fusion), channel_id=1, source_target_pairs={{0,2},{1,3},{2,0},{3,1},{4,6},{5,7},{6,4},{7,5},{8,10},{9,11},{10,... | collective-permute-start | bytes 1990664 | tf_op jit(solution)/shard_map/ppermute | solution.py:40
  6.1 2.6 %collective-permute-start.3 = (bf16[288,1152]{1,0:T(8,128)(2,1)}, bf16[288,1152]{1,0:T(8,128)(2,1)S(1)}, u32[]{:S(2)}, u32[]{:S(2)}) collective-permute-start(bf16[288,1152]{1,0:T(8,128)(2,1)} %bitcast_convert_fusion), channel_id=1, source_target_pairs={{0,4},{1,5},{2,6},{3,7},{4,0},{5,1},{6,2},{7,3},{8,12},{9,13},{10,... | collective-permute-start | bytes 1990664 | tf_op jit(solution)/shard_map/ppermute | solution.py:40
  8.7 1.9 bitcast_convert_fusion.1
  12.5 2.8 %broadcast_in_dim.70 = bf16[4,2,288,1152]{3,2,1,0:T(8,128)(2,1)} broadcast(bf16[]{:T(256)} %constant.99.clone.1), dimensions={} | broadcast | bytes 5308418 | tf_op jit(solution)/shard_map/broadcast_in_dim | solution.py:89
  16.2 5.2 %collective-permute-done.7 = bf16[144,1152]{1,0:T(8,128)(2,1)S(1)} collective-permute-done((bf16[144,1152]{1,0:T(8,128)(2,1)}, bf16[144,1152]{1,0:T(8,128)(2,1)S(1)}, u32[]{:S(2)}, u32[]{:S(2)}) %collective-permute-start.7) | collective-permute-done | bytes 331808 | tf_op jit(solution)/shard_map/ppermute | solution.py:32
  22.1 2.0 bitcast_dynamic-update-slice_fusion.6
  24.1 28.7 %collective-permute-done.11 = bf16[144,1152]{1,0:T(8,128)(2,1)S(1)} collective-permute-done((bf16[144,1152]{1,0:T(8,128)(2,1)S(1)}, bf16[144,1152]{1,0:T(8,128)(2,1)S(1)}, u32[]{:S(2)}, u32[]{:S(2)}) %collective-permute-start.11) | collective-permute-done | bytes 331808 | tf_op jit(solution)/shard_map/ppermute | solution.py:40
  52.8 2.0 bitcast_dynamic-update-slice_fusion.5
  54.8 2.0 collective-permute-start.13
  56.7 6.6 %collective-permute-done.9 = bf16[144,1152]{1,0:T(8,128)(2,1)S(1)} collective-permute-done((bf16[144,1152]{1,0:T(8,128)(2,1)S(1)}, bf16[144,1152]{1,0:T(8,128)(2,1)S(1)}, u32[]{:S(2)}, u32[]{:S(2)}) %collective-permute-start.9) | collective-permute-done | bytes 331808 | tf_op jit(solution)/shard_map/ppermute | solution.py:40
  65.3 5.2 %collective-permute-done.13 = bf16[144,1152]{1,0:T(8,128)(2,1)S(1)} collective-permute-done((bf16[144,1152]{1,0:T(8,128)(2,1)S(1)}, bf16[144,1152]{1,0:T(8,128)(2,1)S(1)}, u32[]{:S(2)}, u32[]{:S(2)}) %collective-permute-start.13) | collective-permute-done | bytes 331808 | tf_op jit(solution)/shard_map/ppermute | solution.py:40
  70.6 13.2 %collective-permute-done.5 = bf16[288,1152]{1,0:T(8,128)(2,1)S(1)} collective-permute-done((bf16[288,1152]{1,0:T(8,128)(2,1)S(1)}, bf16[288,1152]{1,0:T(8,128)(2,1)S(1)}, u32[]{:S(2)}, u32[]{:S(2)}) %collective-permute-start.5) | collective-permute-done | bytes 663584 | tf_op jit(solution)/shard_map/ppermute | solution.py:40
  88.4 3.0 %fusion.23 = (bf16[2,2,288,1152]{3,2,1,0:T(8,128)(2,1)S(1)}, bf16[2,2,288,1152]{3,2,1,0:T(8,128)(2,1)S(1)}) fusion(bf16[4,2,288,1152]{3,2,1,0:T(8,128)(2,1)} %bitcast_dynamic-update-slice_fusion), kind=kLoop, calls=%fused_computation.71 | loop fusion | bytes 10616832 | tf_op jit(solution)/shard_map/slice | solution.py:122
  91.4 3.5 %fusion.24 = f32[1152,1024]{0,1:T(8,128)S(1)} fusion(bf16[1024,1152]{1,0:T(8,128)(2,1)S(1)} %bitcast.158, bf16[1152,1152]{1,0:T(8,128)(2,1)S(1)} %bitcast.164), kind=kOutput, calls=%fused_computation.72 | convolution fusion | flops 2717908992 | bytes 9732096 | tf_op jit(solution)/shard_map/dot_general | solution.py:108
  94.9 5.1 %convolution_convert_fusion.6 = bf16[1152,1024]{1,0:T(8,128)(2,1)S(1)} fusion(bf16[1152,1152]{1,0:T(8,128)(2,1)S(1)} %bitcast.162, bf16[1024,1152]{1,0:T(8,128)(2,1)} %collective-permute-done.15), kind=kOutput, calls=%fused_computation.20 | convolution fusion | flops 2719088640 | bytes 7372800 | tf_op jit(solution)/shard_map/dot_general | solution.py:108
  100.0 7.8 %fusion.7 = (bf16[1024,1152]{1,0:T(8,128)(2,1)S(1)}, bf16[1024,1152]{1,0:T(8,128)(2,1)}) fusion(bf16[1,2,512,1152]{3,2,1,0:T(8,128)(2,1)S(1)} %copy-done.11, bf16[1152,1024]{1,0:T(8,128)(2,1)S(1)} %convolution_convert_fusion.6, bf16[1152,1152]{1,0:T(8,128)(2,1)S(1)} %bitcast.168, f32[1152,1024]{0,1:T(8,128)S(1)} %fusion.24), kind=kOutput, calls=%fused_computation.13 | convolution fusion | flops 2734424064 | bytes 16809984 | tf_op jit(solution)/shard_map/dot_general | solution.py:108
  107.8 3.8 %convolution_convert_fusion.5 = bf16[1024,1152]{1,0:T(8,128)(2,1)S(1)} fusion(bf16[1024,1152]{1,0:T(8,128)(2,1)S(1)} %get-tuple-element.14, bf16[1152,1152]{1,0:T(8,128)(2,1)S(1)} %bitcast.169), kind=kOutput, calls=%fused_computation.19 | convolution fusion | flops 2719088640 | bytes 7372800 | tf_op jit(solution)/shard_map/rk,jk->rj/dot_general | solution.py:130
  111.6 4.5 %convolution_convert_fusion = bf16[1152,1152]{1,0:T(8,128)(2,1)} fusion(bf16[1152,1024]{1,0:T(8,128)(2,1)S(1)} %convolution_convert_fusion.6, bf16[1024,1152]{1,0:T(8,128)(2,1)S(1)} %get-tuple-element.14), kind=kOutput, calls=%fused_computation | convolution fusion | flops 2719236096 | bytes 7372800 | tf_op jit(solution)/shard_map/rj,rk->jk/dot_general | solution.py:137
  116.1 4.9 %fusion = bf16[1152,1152]{1,0:T(8,128)(2,1)} fusion(bf16[1024,1152]{1,0:T(8,128)(2,1)S(1)} %get-tuple-element.14, bf16[1024,1152]{1,0:T(8,128)(2,1)S(1)} %bitcast.159), kind=kOutput, calls=%fused_computation.4 | convolution fusion | flops 2719236096 | bytes 7372800 | tf_op jit(solution)/shard_map/rj,rk->jk/dot_general | solution.py:136
  121.0 5.2 %convolution_convert_fusion.2 = bf16[1152,1152]{0,1:T(8,128)(2,1)S(1)} fusion(bf16[1024,1152]{1,0:T(8,128)(2,1)S(1)} %convolution_convert_fusion.5, bf16[1024,1152]{1,0:T(8,128)(2,1)} %collective-permute-done.15), kind=kOutput, calls=%fused_computation.2 | convolution fusion | flops 2719236096 | bytes 7372800 | tf_op jit(solution)/shard_map/rj,rk->jk/dot_general | solution.py:131
  132.9 1.8 collective-permute-start.18
  134.7 8.6 %collective-permute-done.19 = bf16[144,1152]{1,0:T(8,128)(2,1)S(1)} collective-permute-done((bf16[144,1152]{1,0:T(8,128)(2,1)S(1)}, bf16[144,1152]{1,0:T(8,128)(2,1)S(1)}, u32[]{:S(2)}, u32[]{:S(2)}) %collective-permute-start.19) | collective-permute-done | bytes 331808 | tf_op jit(solution)/shard_map/ppermute | solution.py:40
  145.0 1.8 collective-permute-start.24
  146.8 3.8 %convolution_convert_fusion.4 = bf16[1024,1152]{1,0:T(8,128)(2,1)S(1)} fusion(bf16[1024,1152]{1,0:T(8,128)(2,1)S(1)} %copy-done.15, bf16[1152,1152]{1,0:T(8,128)(2,1)S(1)} %bitcast.163), kind=kOutput, calls=%fused_computation.18 | convolution fusion | flops 2719088640 | bytes 7372800 | tf_op jit(solution)/shard_map/rk,jk->rj/dot_general | solution.py:134
  152.2 2.2 %collective-permute-done.18 = bf16[144,1152]{1,0:T(8,128)(2,1)S(1)} collective-permute-done((bf16[144,1152]{1,0:T(8,128)(2,1)S(1)}, bf16[144,1152]{1,0:T(8,128)(2,1)S(1)}, u32[]{:S(2)}, u32[]{:S(2)}) %collective-permute-start.18) | collective-permute-done | bytes 331808 | tf_op jit(solution)/shard_map/ppermute | solution.py:40
  154.4 5.9 %collective-permute-done.20 = bf16[144,1152]{1,0:T(8,128)(2,1)S(1)} collective-permute-done((bf16[144,1152]{1,0:T(8,128)(2,1)S(1)}, bf16[144,1152]{1,0:T(8,128)(2,1)S(1)}, u32[]{:S(2)}, u32[]{:S(2)}) %collective-permute-start.20) | collective-permute-done | bytes 331808 | tf_op jit(solution)/shard_map/ppermute | solution.py:40
  162.0 9.7 %collective-permute-done.24 = bf16[288,1152]{1,0:T(8,128)(2,1)S(1)} collective-permute-done((bf16[288,1152]{1,0:T(8,128)(2,1)S(1)}, bf16[288,1152]{1,0:T(8,128)(2,1)S(1)}, u32[]{:S(2)}, u32[]{:S(2)}) %collective-permute-start.24) | collective-permute-done | bytes 663584 | tf_op jit(solution)/shard_map/ppermute | solution.py:40
  172.6 4.8 %convolution_convert_fusion.3 = bf16[1024,1152]{1,0:T(8,128)(2,1)} fusion(bf16[1024,1152]{1,0:T(8,128)(2,1)S(1)} %copy-done.13, bf16[1152,1152]{1,0:T(8,128)(2,1)S(1)} %bitcast.165), kind=kOutput, calls=%fused_computation.17 | convolution fusion | flops 2719088640 | bytes 7372800 | tf_op jit(solution)/shard_map/rk,jk->rj/dot_general | solution.py:139
  177.4 32.0 %collective-permute-done.21 = bf16[144,1152]{1,0:T(8,128)(2,1)S(1)} collective-permute-done((bf16[144,1152]{1,0:T(8,128)(2,1)S(1)}, bf16[144,1152]{1,0:T(8,128)(2,1)S(1)}, u32[]{:S(2)}, u32[]{:S(2)}) %collective-permute-start.21) | collective-permute-done | bytes 331808 | tf_op jit(solution)/shard_map/ppermute | solution.py:32
  209.4 1.8 fusion.20
  211.2 3.1 %fusion.22 = (f32[1,288,1152]{2,1,0:T(8,128)}, f32[1,288,1152]{2,1,0:T(8,128)}, f32[1,288,1152]{2,1,0:T(8,128)}) fusion(bf16[288,1152]{1,0:T(8,128)(2,1)S(1)} %collective-permute-done.25, bf16[288,1152]{1,0:T(8,128)(2,1)S(1)} %collective-permute-done.23, bf16[4,288,1152]{2,1,0:T(8,128)(2,1)S(1)} %fusion.1, s32[]{:T(128)S(6)} %select_n.81, ...), kind=kLoop, calls=%fused_computation.70 | loop fusion | flops 5971968 | bytes 9953284 | tf_op jit(solution)/shard_map/broadcast_in_dim | solution.py:144
  (95 shorter events, 24.7 us)
Async XLA Ops:
  0.6 90.7 %copy-start = (bf16[1,2,512,1152]{3,2,1,0:T(8,128)(2,1)S(1)}, bf16[1,2,512,1152]{3,2,1,0:T(8,128)(2,1)}, u32[]{:S(2)}) copy-start(bf16[1,2,512,1152]{3,2,1,0:T(8,128)(2,1)} %param.10) | copy-start | bytes 7077892
  3.0 18.6 %collective-permute-start = (bf16[288,1152]{1,0:T(8,128)(2,1)}, bf16[288,1152]{1,0:T(8,128)(2,1)}, u32[]{:S(2)}, u32[]{:S(2)}) collective-permute-start(bf16[288,1152]{1,0:T(8,128)(2,1)} %bitcast_convert_fusion), channel_id=1, source_target_pairs={{0,1},{1,0},{2,3},{3,2},{4,5},{5,4},{6,7},{7,6},{8,9},{9,8},{10,11... | collective-permute-start | bytes 1990664 | tf_op jit(solution)/shard_map/ppermute | solution.py:48
  3.5 49.2 %collective-permute-start.1 = (bf16[288,1152]{1,0:T(8,128)(2,1)}, bf16[288,1152]{1,0:T(8,128)(2,1)}, u32[]{:S(2)}, u32[]{:S(2)}) collective-permute-start(bf16[288,1152]{1,0:T(8,128)(2,1)} %bitcast_convert_fusion), channel_id=1, source_target_pairs={{0,2},{1,3},{2,0},{3,1},{4,6},{5,7},{6,4},{7,5},{8,10},{9,11},{10,... | collective-permute-start | bytes 1990664 | tf_op jit(solution)/shard_map/ppermute | solution.py:40
  6.1 57.4 %collective-permute-start.3 = (bf16[288,1152]{1,0:T(8,128)(2,1)}, bf16[288,1152]{1,0:T(8,128)(2,1)S(1)}, u32[]{:S(2)}, u32[]{:S(2)}) collective-permute-start(bf16[288,1152]{1,0:T(8,128)(2,1)} %bitcast_convert_fusion), channel_id=1, source_target_pairs={{0,4},{1,5},{2,6},{3,7},{4,0},{5,1},{6,2},{7,3},{8,12},{9,13},{10,... | collective-permute-start | bytes 1990664 | tf_op jit(solution)/shard_map/ppermute | solution.py:40
  10.5 10.9 %collective-permute-start.7 = (bf16[144,1152]{1,0:T(8,128)(2,1)}, bf16[144,1152]{1,0:T(8,128)(2,1)S(1)}, u32[]{:S(2)}, u32[]{:S(2)}) collective-permute-start(bf16[144,1152]{1,0:T(8,128)(2,1)} %bitcast_convert_fusion.1), channel_id=1, source_target_pairs={{0,16},{8,24},{16,0},{24,8},{1,17},{9,25},{17,1},{25,9},{2,18},{10... | collective-permute-start | bytes 995336 | tf_op jit(solution)/shard_map/ppermute | solution.py:32
  12.0 82.8 %collective-permute-start.15 = (bf16[1024,1152]{1,0:T(8,128)(2,1)}, bf16[1024,1152]{1,0:T(8,128)(2,1)}, u32[]{:S(2)}, u32[]{:S(2)}) collective-permute-start(bf16[1024,1152]{1,0:T(8,128)(2,1)} %bitcast.22), channel_id=1, source_target_pairs={{0,16},{8,24},{16,0},{24,8},{1,17},{9,25},{17,1},{25,9},{2,18},{10... | collective-permute-start | bytes 7077896 | tf_op jit(solution)/shard_map/ppermute | solution.py:32
  21.4 33.4 %collective-permute-start.8 = (bf16[144,1152]{1,0:T(8,128)(2,1)S(1)}, bf16[144,1152]{1,0:T(8,128)(2,1)S(1)}, u32[]{:S(2)}, u32[]{:S(2)}) collective-permute-start(bf16[144,1152]{1,0:T(8,128)(2,1)S(1)} %collective-permute-done.7), channel_id=1, source_target_pairs={{0,1},{1,0},{2,3},{3,2},{4,5},{5,4},{6,7},{7,6},{8,9},{9,8},{10,11... | collective-permute-start | bytes 995336 | tf_op jit(solution)/shard_map/ppermute | solution.py:48
  21.7 31.1 %collective-permute-start.11 = (bf16[144,1152]{1,0:T(8,128)(2,1)S(1)}, bf16[144,1152]{1,0:T(8,128)(2,1)S(1)}, u32[]{:S(2)}, u32[]{:S(2)}) collective-permute-start(bf16[144,1152]{1,0:T(8,128)(2,1)S(1)} %collective-permute-done.7), channel_id=1, source_target_pairs={{0,4},{1,5},{2,6},{3,7},{4,0},{5,1},{6,2},{7,3},{8,12},{9,13},{10,... | collective-permute-start | bytes 995336 | tf_op jit(solution)/shard_map/ppermute | solution.py:40
  52.7 10.7 %collective-permute-start.9 = (bf16[144,1152]{1,0:T(8,128)(2,1)S(1)}, bf16[144,1152]{1,0:T(8,128)(2,1)S(1)}, u32[]{:S(2)}, u32[]{:S(2)}) collective-permute-start(bf16[144,1152]{1,0:T(8,128)(2,1)S(1)} %collective-permute-done.7), channel_id=1, source_target_pairs={{0,2},{1,3},{2,0},{3,1},{4,6},{5,7},{6,4},{7,5},{8,10},{9,11},{10,... | collective-permute-start | bytes 995336 | tf_op jit(solution)/shard_map/ppermute | solution.py:40
  52.7 12.5 %collective-permute-start.12 = (bf16[144,1152]{1,0:T(8,128)(2,1)S(1)}, bf16[144,1152]{1,0:T(8,128)(2,1)S(1)}, u32[]{:S(2)}, u32[]{:S(2)}) collective-permute-start(bf16[144,1152]{1,0:T(8,128)(2,1)S(1)} %collective-permute-done.11), channel_id=1, source_target_pairs={{0,1},{1,0},{2,3},{3,2},{4,5},{5,4},{6,7},{7,6},{8,9},{9,8},{10,11... | collective-permute-start | bytes 995336 | tf_op jit(solution)/shard_map/ppermute | solution.py:48
  54.8 15.7 %collective-permute-start.13 = (bf16[144,1152]{1,0:T(8,128)(2,1)S(1)}, bf16[144,1152]{1,0:T(8,128)(2,1)S(1)}, u32[]{:S(2)}, u32[]{:S(2)}) collective-permute-start(bf16[144,1152]{1,0:T(8,128)(2,1)S(1)} %collective-permute-done.11), channel_id=1, source_target_pairs={{0,2},{1,3},{2,0},{3,1},{4,6},{5,7},{6,4},{7,5},{8,10},{9,11},{10,... | collective-permute-start | bytes 995336 | tf_op jit(solution)/shard_map/ppermute | solution.py:40
  63.4 1.6 collective-permute-start.10
  63.5 20.3 %collective-permute-start.2 = (bf16[288,1152]{1,0:T(8,128)(2,1)}, bf16[288,1152]{1,0:T(8,128)(2,1)S(1)}, u32[]{:S(2)}, u32[]{:S(2)}) collective-permute-start(bf16[288,1152]{1,0:T(8,128)(2,1)} %collective-permute-done.1), channel_id=1, source_target_pairs={{0,1},{1,0},{2,3},{3,2},{4,5},{5,4},{6,7},{7,6},{8,9},{9,8},{10,11... | collective-permute-start | bytes 1990664 | tf_op jit(solution)/shard_map/ppermute | solution.py:48
  65.0 20.6 %collective-permute-start.4 = (bf16[288,1152]{1,0:T(8,128)(2,1)S(1)}, bf16[288,1152]{1,0:T(8,128)(2,1)S(1)}, u32[]{:S(2)}, u32[]{:S(2)}) collective-permute-start(bf16[288,1152]{1,0:T(8,128)(2,1)S(1)} %collective-permute-done.3), channel_id=1, source_target_pairs={{0,1},{1,0},{2,3},{3,2},{4,5},{5,4},{6,7},{7,6},{8,9},{9,8},{10,11... | collective-permute-start | bytes 1990664 | tf_op jit(solution)/shard_map/ppermute | solution.py:48
  65.2 18.6 %collective-permute-start.5 = (bf16[288,1152]{1,0:T(8,128)(2,1)S(1)}, bf16[288,1152]{1,0:T(8,128)(2,1)S(1)}, u32[]{:S(2)}, u32[]{:S(2)}) collective-permute-start(bf16[288,1152]{1,0:T(8,128)(2,1)S(1)} %collective-permute-done.3), channel_id=1, source_target_pairs={{0,2},{1,3},{2,0},{3,1},{4,6},{5,7},{6,4},{7,5},{8,10},{9,11},{10,... | collective-permute-start | bytes 1990664 | tf_op jit(solution)/shard_map/ppermute | solution.py:40
  70.5 16.9 %collective-permute-start.14 = (bf16[144,1152]{1,0:T(8,128)(2,1)S(1)}, bf16[144,1152]{1,0:T(8,128)(2,1)S(1)}, u32[]{:S(2)}, u32[]{:S(2)}) collective-permute-start(bf16[144,1152]{1,0:T(8,128)(2,1)S(1)} %collective-permute-done.13), channel_id=1, source_target_pairs={{0,1},{1,0},{2,3},{3,2},{4,5},{5,4},{6,7},{7,6},{8,9},{9,8},{10,11... | collective-permute-start | bytes 995336 | tf_op jit(solution)/shard_map/ppermute | solution.py:48
  83.8 3.6 %collective-permute-start.6 = (bf16[288,1152]{1,0:T(8,128)(2,1)S(1)}, bf16[288,1152]{1,0:T(8,128)(2,1)S(1)}, u32[]{:S(2)}, u32[]{:S(2)}) collective-permute-start(bf16[288,1152]{1,0:T(8,128)(2,1)S(1)} %collective-permute-done.5), channel_id=1, source_target_pairs={{0,1},{1,0},{2,3},{3,2},{4,5},{5,4},{6,7},{7,6},{8,9},{9,8},{10,11... | collective-permute-start | bytes 1990664 | tf_op jit(solution)/shard_map/ppermute | solution.py:48
  127.3 3.6 %collective-permute-start.17 = (bf16[4,144,1152]{2,1,0:T(8,128)(2,1)}, bf16[4,144,1152]{2,1,0:T(8,128)(2,1)}, u32[]{:S(2)}, u32[]{:S(2)}) collective-permute-start(bf16[4,144,1152]{2,1,0:T(8,128)(2,1)} %dynamic-slice_bitcast_fusion.1), channel_id=1, source_target_pairs={{0,1},{1,0},{2,3},{3,2},{4,5},{5,4},{6,7},{7,6},{8,9},{9,8},{10,11... | collective-permute-start | bytes 3981320 | tf_op jit(solution)/shard_map/ppermute | solution.py:48
  129.0 15.1 %collective-permute-start.22 = (bf16[4,288,1152]{2,1,0:T(8,128)(2,1)S(1)}, bf16[4,288,1152]{2,1,0:T(8,128)(2,1)S(1)}, u32[]{:S(2)}, u32[]{:S(2)}) collective-permute-start(bf16[4,288,1152]{2,1,0:T(8,128)(2,1)S(1)} %dynamic-slice_bitcast_fusion), channel_id=1, source_target_pairs={{0,1},{1,0},{2,3},{3,2},{4,5},{5,4},{6,7},{7,6},{8,9},{9,8},{10,11... | collective-permute-start | bytes 7962632 | tf_op jit(solution)/shard_map/ppermute | solution.py:48
  132.6 10.7 %collective-permute-start.19 = (bf16[144,1152]{1,0:T(8,128)(2,1)S(1)}, bf16[144,1152]{1,0:T(8,128)(2,1)S(1)}, u32[]{:S(2)}, u32[]{:S(2)}) collective-permute-start(bf16[144,1152]{1,0:T(8,128)(2,1)S(1)} %get-tuple-element.19), channel_id=1, source_target_pairs={{0,2},{1,3},{2,0},{3,1},{4,6},{5,7},{6,4},{7,5},{8,10},{9,11},{10,... | collective-permute-start | bytes 995336 | tf_op jit(solution)/shard_map/ppermute | solution.py:40
  132.9 21.5 %collective-permute-start.18 = (bf16[144,1152]{1,0:T(8,128)(2,1)S(1)}, bf16[144,1152]{1,0:T(8,128)(2,1)S(1)}, u32[]{:S(2)}, u32[]{:S(2)}) collective-permute-start(bf16[144,1152]{1,0:T(8,128)(2,1)S(1)} %get-tuple-element.18), channel_id=1, source_target_pairs={{0,2},{1,3},{2,0},{3,1},{4,6},{5,7},{6,4},{7,5},{8,10},{9,11},{10,... | collective-permute-start | bytes 995336 | tf_op jit(solution)/shard_map/ppermute | solution.py:40
  143.4 16.9 %collective-permute-start.20 = (bf16[144,1152]{1,0:T(8,128)(2,1)S(1)}, bf16[144,1152]{1,0:T(8,128)(2,1)S(1)}, u32[]{:S(2)}, u32[]{:S(2)}) collective-permute-start(bf16[144,1152]{1,0:T(8,128)(2,1)S(1)} %fusion.15), channel_id=1, source_target_pairs={{0,4},{1,5},{2,6},{3,7},{4,0},{5,1},{6,2},{7,3},{8,12},{9,13},{10,... | collective-permute-start | bytes 995336 | tf_op jit(solution)/shard_map/ppermute | solution.py:40
  145.0 26.8 %collective-permute-start.24 = (bf16[288,1152]{1,0:T(8,128)(2,1)S(1)}, bf16[288,1152]{1,0:T(8,128)(2,1)S(1)}, u32[]{:S(2)}, u32[]{:S(2)}) collective-permute-start(bf16[288,1152]{1,0:T(8,128)(2,1)S(1)} %get-tuple-element.17), channel_id=1, source_target_pairs={{0,2},{1,3},{2,0},{3,1},{4,6},{5,7},{6,4},{7,5},{8,10},{9,11},{10,... | collective-permute-start | bytes 1990664 | tf_op jit(solution)/shard_map/ppermute | solution.py:40
  150.6 60.6 %collective-permute-start.16 = (bf16[1024,1152]{1,0:T(8,128)(2,1)S(1)}, bf16[1024,1152]{1,0:T(8,128)(2,1)S(1)}, u32[]{:S(2)}, u32[]{:S(2)}) collective-permute-start(bf16[1024,1152]{1,0:T(8,128)(2,1)S(1)} %convolution_convert_fusion.4), channel_id=1, source_target_pairs={{0,16},{8,24},{16,0},{24,8},{1,17},{9,25},{17,1},{25,9},{2,18},{10... | collective-permute-start | bytes 7077896 | tf_op jit(solution)/shard_map/ppermute | solution.py:32
  160.4 48.9 %collective-permute-start.21 = (bf16[144,1152]{1,0:T(8,128)(2,1)S(1)}, bf16[144,1152]{1,0:T(8,128)(2,1)S(1)}, u32[]{:S(2)}, u32[]{:S(2)}) collective-permute-start(bf16[144,1152]{1,0:T(8,128)(2,1)S(1)} %fusion.17), channel_id=1, source_target_pairs={{0,16},{8,24},{16,0},{24,8},{1,17},{9,25},{17,1},{25,9},{2,18},{10... | collective-permute-start | bytes 995336 | tf_op jit(solution)/shard_map/ppermute | solution.py:32
  162.0 49.1 %collective-permute-start.23 = (bf16[288,1152]{1,0:T(8,128)(2,1)S(1)}, bf16[288,1152]{1,0:T(8,128)(2,1)S(1)}, u32[]{:S(2)}, u32[]{:S(2)}) collective-permute-start(bf16[288,1152]{1,0:T(8,128)(2,1)S(1)} %get-tuple-element.16), channel_id=1, source_target_pairs={{0,2},{1,3},{2,0},{3,1},{4,6},{5,7},{6,4},{7,5},{8,10},{9,11},{10,... | collective-permute-start | bytes 1990664 | tf_op jit(solution)/shard_map/ppermute | solution.py:40
  171.9 37.5 %copy-start.4 = (f32[1,144,1152]{2,1,0:T(8,128)S(1)}, f32[1,144,1152]{2,1,0:T(8,128)}, u32[]{:S(2)}) copy-start(f32[1,144,1152]{2,1,0:T(8,128)} %param.12) | copy-start | bytes 1990660
  171.9 37.5 %copy-start.9 = (f32[1,144,1152]{2,1,0:T(8,128)S(1)}, f32[1,144,1152]{2,1,0:T(8,128)}, u32[]{:S(2)}) copy-start(f32[1,144,1152]{2,1,0:T(8,128)} %param.15) | copy-start | bytes 1990660
  171.9 37.5 %copy-start.10 = (f32[1,144,1152]{2,1,0:T(8,128)S(1)}, f32[1,144,1152]{2,1,0:T(8,128)}, u32[]{:S(2)}) copy-start(f32[1,144,1152]{2,1,0:T(8,128)} %param.14) | copy-start | bytes 1990660
  171.9 39.2 %collective-permute-start.25 = (bf16[288,1152]{1,0:T(8,128)(2,1)S(1)}, bf16[288,1152]{1,0:T(8,128)(2,1)S(1)}, u32[]{:S(2)}, u32[]{:S(2)}) collective-permute-start(bf16[288,1152]{1,0:T(8,128)(2,1)S(1)} %fusion.10), channel_id=1, source_target_pairs={{0,4},{1,5},{2,6},{3,7},{4,0},{5,1},{6,2},{7,3},{8,12},{9,13},{10,... | collective-permute-start | bytes 1990664 | tf_op jit(solution)/shard_map/ppermute | solution.py:40
  177.4 33.8 %copy-start.7 = (f32[1,288,1152]{2,1,0:T(8,128)S(1)}, f32[1,288,1152]{2,1,0:T(8,128)}, u32[]{:S(2)}) copy-start(f32[1,288,1152]{2,1,0:T(8,128)} %param.17) | copy-start | bytes 3981316
  177.4 33.8 %copy-start.8 = (f32[1,288,1152]{2,1,0:T(8,128)S(1)}, f32[1,288,1152]{2,1,0:T(8,128)}, u32[]{:S(2)}) copy-start(f32[1,288,1152]{2,1,0:T(8,128)} %param.16) | copy-start | bytes 3981316
  (10 other events, 96.9 us)

commit v2 on v1

v2 whole, which is shorter than its diff:
```python
import math

import jax
import jax.numpy as jnp
from jax import lax
from jax.experimental import pallas as pl
from jax.experimental.pallas import tpu as pltpu
from jax.sharding import PartitionSpec as P

half_root = 0.7071067811865476
gauss_norm = 0.3989422804014327
beta_one = 0.9
beta_two = 0.95
learn_rate = 0.002
adam_eps = 1e-08
correct_one = 1.0 - 0.9**10
correct_two = 1.0 - 0.95**10


def gelu_parts(preact):
    normal_cdf = 0.5 * (1.0 + lax.erf(preact * half_root))
    density = jnp.exp(-0.5 * preact * preact) * gauss_norm
    return (preact * normal_cdf, normal_cdf + preact * density)


def adam_update(weight, moment, second, grad):
    new_moment = beta_one * moment + (1.0 - beta_one) * grad
    new_second = beta_two * second + (1.0 - beta_two) * grad * grad
    step_size = new_moment / correct_one / (jnp.sqrt(new_second / correct_two) + adam_eps)
    return (weight - learn_rate * step_size, new_moment, new_second)


def to_partner(value):
    count = lax.axis_size("section")
    pairs = [(s, (s + count // 2) % count) for s in range(count)]
    return lax.ppermute(value, "section", pairs)


def chip_count():
    return lax.axis_size("dp") // 2


def to_chips(value, pairs):
    return lax.ppermute(value, "dp", [(2 * a + c, 2 * b + c) for a, b in pairs for c in range(2)])


def chip_flip(value, mask):
    return to_chips(value, [(z, z ^ mask) for z in range(chip_count())])


def core_flip(value):
    return lax.ppermute(value, "dp", [(d, d ^ 1) for d in range(lax.axis_size("dp"))])


def gather_first(piece):
    found = {0: piece}
    step = chip_count() // 2
    while step > 1:
        found.update({k + step: chip_flip(found[k], step) for k in sorted(found)})
        step //= 2
    found[1] = chip_flip(piece, 1)
    return found


def gather_last(found):
    for k in range(2, chip_count(), 2):
        found[k + 1] = chip_flip(found[k], 1)
    return [found[k] for k in range(chip_count())]


def plus(*terms):
    total = terms[0].astype(jnp.float32)
    for term in terms[1:]:
        total = total + term.astype(jnp.float32)
    return total


def scatter_near(blocks):
    return {k: chip_flip(blocks[k + 1], 1) for k in range(2, len(blocks), 2)}


def scatter_on(blocks, came):
    held = {k: plus(blocks[k], came[k]).astype(jnp.bfloat16) for k in came}
    step = 2
    while step < len(blocks) // 2:
        for k in range(2 * step, len(blocks), 2 * step):
            held[k] = plus(held[k], chip_flip(held[k + step], step)).astype(jnp.bfloat16)
        step *= 2
    return [chip_flip(held[2**n], 2**n) for n in range(1, len(blocks).bit_length() - 1)]


def assemble(found):
    place = lax.axis_index("dp")
    chip, core = place // 2, place % 2
    rows, width = found[0].shape
    whole = jnp.zeros((chip_count(), 2, rows, width), found[0].dtype)
    for k, piece in enumerate(found):
        whole = lax.dynamic_update_slice(whole, piece[None, None], (chip ^ k, core, 0, 0))
        whole = lax.dynamic_update_slice(whole, core_flip(piece)[None, None], (chip ^ k, 1 - core, 0, 0))
    return whole.reshape(-1, width)


def interleave(parts, refs, target, sems):
    copies = []
    for (rows, start, stride), ref in zip(parts, refs):
        if rows == stride:
            copies.append(pltpu.make_async_copy(ref, target, sems.at[len(copies)]))
            continue
        for d in range(ref.shape[0] // rows):
            copies.append(
                pltpu.make_async_copy(
                    ref.at[pl.ds(d * rows, rows)], target.at[pl.ds(d * stride + start, rows)], sems.at[len(copies)]
                )
            )
    for copy in copies:
        copy.start()
    for copy in copies:
        copy.wait()


def copy_count(weights, parts):
    return sum(1 if rows == stride else w.shape[0] // rows for w, (rows, _, stride) in zip(weights, parts))


def row_call(compute, row_arrays, weights, parts, out_count, tile_rows, vmem_mib, start=0, rows=None):
    width = row_arrays[0].shape[1]
    rows = rows or row_arrays[0].shape[0]
    tile = math.gcd(math.gcd(rows, start), tile_rows)
    count = copy_count(weights, parts)

    def kernel(*refs):
        ins = refs[: len(row_arrays)]
        weight_refs = refs[len(row_arrays) : len(row_arrays) + len(weights)]
        outs = refs[len(row_arrays) + len(weights) :][:out_count]
        whole, sems = refs[-2:]

        @pl.when(pl.program_id(0) == 0)
        def _():
            interleave(parts, weight_refs, whole, sems)

        compute(ins, whole, outs)

    block = pl.BlockSpec((tile, width), lambda i: (i, 0))
    taken = pl.BlockSpec((tile, width), lambda i: (i + start // tile, 0))
    return pl.pallas_call(
        kernel,
        grid=(rows // tile,),
        in_specs=[taken] * len(row_arrays) + [pl.BlockSpec(memory_space=pl.ANY)] * len(weights),
        out_specs=[block] * out_count,
        out_shape=[jax.ShapeDtypeStruct((rows, width), jnp.bfloat16)] * out_count,
        scratch_shapes=[
            pltpu.VMEM((sum(w.shape[0] for w in weights), width), jnp.bfloat16),
            pltpu.SemaphoreType.DMA((count,)),
        ],
        compiler_params=pltpu.CompilerParams(vmem_limit_bytes=vmem_mib * 2**20),
        cost_estimate=pl.CostEstimate(flops=COST, bytes_accessed=COST, transcendentals=0),
    )(*row_arrays, *weights)


COST = 1000


def dot_nn(left, right):
    return jnp.dot(left, right, preferred_element_type=jnp.float32)


def dot_nt(left, right):
    return lax.dot_general(left, right, (((1,), (1,)), ((), ())), preferred_element_type=jnp.float32)


def dot_tn(left, right):
    return lax.dot_general(left, right, (((0,), (0,)), ((), ())), preferred_element_type=jnp.float32)


def project(parts, weight, vmem_mib):
    width = weight.shape[1]
    rows = sum(part.shape[0] for part in parts)

    def kernel(*refs):
        at = 0
        for ref, part in zip(refs, parts):
            refs[-1][at : at + part.shape[0]] = dot_nn(ref[...], refs[-2][...]).astype(jnp.bfloat16)
            at += part.shape[0]

    return pl.pallas_call(
        kernel,
        out_shape=jax.ShapeDtypeStruct((rows, width), jnp.bfloat16),
        compiler_params=pltpu.CompilerParams(vmem_limit_bytes=vmem_mib * 2**20),
        cost_estimate=pl.CostEstimate(flops=COST, bytes_accessed=COST, transcendentals=0),
    )(*parts, weight)


def project_back(ins, whole, outs):
    outs[0][...] = dot_nt(ins[0][...], whole[...]).astype(jnp.bfloat16)


def upper_back(ins, whole, outs):
    width = ins[0].shape[1]
    outs[0][...] = dot_nt(ins[0][...], whole[:width]).astype(jnp.bfloat16)


def middle(ins, whole, outs):
    dec, skip, out_grad = ins
    rows, width = dec.shape
    part = math.gcd(rows, 256)
    for at in range(0, rows, part):
        here = slice(at, at + part)
        preact = dot_nn(dec[here], whole[:width]) + dot_nn(skip[here], whole[width:])
        activated, gelu_slope = gelu_parts(preact)
        outs[0][here] = activated.astype(jnp.bfloat16)
        pre_grad = (out_grad[here].astype(jnp.float32) * gelu_slope).astype(jnp.bfloat16)
        outs[1][here] = pre_grad
        outs[2][here] = dot_nt(pre_grad, whole[width:]).astype(jnp.bfloat16)


def weight_grad(lefts, right):
    rows, width = right.shape
    tile = math.gcd(width, 384)
    steps = width // tile
    parts = [(n, part) for n, left in enumerate(lefts) for part in left]

    def kernel(*refs):
        step = pl.program_id(0)
        right_ref, out_ref = refs[-2:]
        for n in range(len(lefts)):

            @pl.when(step // steps == n)
            def _(n=n):
                total, at = 0.0, 0
                for ref, (owner, part) in zip(refs, parts):
                    if owner == n:
                        total = total + dot_tn(ref[...], right_ref[at : at + part.shape[0]])
                        at += part.shape[0]
                out_ref[...] = total.astype(jnp.bfloat16)

    def spec(n, part):
        return pl.BlockSpec((part.shape[0], tile), lambda i: (0, jnp.clip(i - n * steps, 0, steps - 1)))

    return pl.pallas_call(
        kernel,
        grid=(len(lefts) * steps,),
        in_specs=[spec(n, part) for n, part in parts]
        + [pl.BlockSpec((rows, width), lambda i: (0, 0), pipeline_mode=pl.Buffered(1))],
        out_specs=pl.BlockSpec((tile, width), lambda i: (i, 0)),
        out_shape=jax.ShapeDtypeStruct((len(lefts) * width, width), jnp.bfloat16),
        compiler_params=pltpu.CompilerParams(vmem_limit_bytes=16 * 2**20),
        cost_estimate=pl.CostEstimate(flops=COST, bytes_accessed=COST, transcendentals=0),
    )(*[part for _, part in parts], right)


def pair_split(total):
    core = lax.axis_index("dp") % 2
    split = total.reshape(chip_count(), 2, -1, total.shape[1])
    keep = lax.dynamic_index_in_dim(split, core, 1, keepdims=False)
    return keep, lax.dynamic_index_in_dim(split, 1 - core, 1, keepdims=False)


def pair_send(total):
    keep, send = pair_split(total)
    return keep, core_flip(send)


def pair_sum(keep, came):
    chip = lax.axis_index("dp") // 2
    both = plus(keep, came).astype(jnp.bfloat16)
    return [lax.dynamic_index_in_dim(both, chip ^ k, 0, keepdims=False) for k in range(chip_count())]


def body(enc_in, dec_in, cotangent, w_proj, w_skip, m_proj, v_proj, m_skip, v_skip):
    micro, tokens_here, width = enc_in.shape[1:]
    rows = micro * tokens_here
    enc_rows = enc_in[0].reshape(rows, width)
    dec_rows = dec_in[0].reshape(rows, width)
    out_grad = cotangent[0].reshape(rows, width)
    together = lax.optimization_barrier

    enc_cuts = [rows * n // 8 for n in (5, 6)]
    proj_half, skip_half = w_proj[0].astype(jnp.bfloat16), w_skip[0].astype(jnp.bfloat16)
    stride = skip_half.shape[0]
    cut = stride // 48 * 16
    proj_piece = to_partner(proj_half)
    head = gather_first(skip_half[:cut])
    proj_piece, head, tail, enc0 = together((proj_piece, head, skip_half[cut:], enc_rows[: enc_cuts[0]]))
    enc0 = to_partner(enc0)
    proj_found = gather_first(proj_piece)
    tail = gather_first(tail)
    enc0, proj_found, tail, head, enc1 = together((enc0, proj_found, tail, head, enc_rows[enc_cuts[0] : enc_cuts[1]]))
    enc1 = to_partner(enc1)
    proj_found = gather_last(proj_found)
    head = gather_last(head)
    enc1, proj_found, tail, head, enc2 = together((enc1, proj_found, tail, head, enc_rows[enc_cuts[1] :]))
    enc2 = to_partner(enc2)
    proj_whole = assemble(proj_found)
    skip_w = [assemble(head), assemble(gather_last(tail))]
    enc_other = (enc0, enc1, enc2)
    skip_parts = [(cut, 0, stride), (stride - cut, cut, stride)]

    skip = project(enc_other, proj_whole, 20)
    dec_out, pre_grad, skip_grad = row_call(
        middle, [dec_rows, skip, out_grad], skip_w, skip_parts, 3, 512, 30
    )
    cuts = [0] + [rows * n // 8 for n in (1, 3, 4, 8)]

    def back(n, value):
        return row_call(
            project_back, [value], [proj_whole], [(1, 0, 1)], 1, 256, 16, start=cuts[n], rows=cuts[n + 1] - cuts[n]
        )[0]

    grad_proj = weight_grad([enc_other], skip_grad)
    grad_proj, skip_grad = together((grad_proj, skip_grad))
    proj_keep, proj_came = pair_send(grad_proj)
    enc0 = back(0, skip_grad)
    proj_keep, proj_came, enc0, pre_grad, skip_grad = together((proj_keep, proj_came, enc0, pre_grad, skip_grad))
    enc0 = to_partner(enc0)
    proj_blocks = pair_sum(proj_keep, proj_came)
    proj_near = scatter_near(proj_blocks)
    skip_keep, skip_send = pair_split(weight_grad([(dec_rows,), (skip,)], pre_grad))
    enc1 = back(1, skip_grad)
    enc0, proj_blocks, proj_near, skip_keep, skip_send, enc1, skip_grad = together(
        (enc0, proj_blocks, proj_near, skip_keep, skip_send, enc1, skip_grad)
    )
    enc1 = to_partner(enc1)
    proj_on = scatter_on(proj_blocks, proj_near)
    proj_one = chip_flip(proj_blocks[1], 1)
    skip_came = core_flip(skip_send)
    enc2 = back(2, skip_grad)
    enc3 = back(3, skip_grad)
    enc1, proj_blocks, proj_on, proj_one, skip_keep, skip_came, enc2, enc3 = together(
        (enc1, proj_blocks, proj_on, proj_one, skip_keep, skip_came, enc2, enc3)
    )
    enc2 = to_partner(enc2)
    proj_sum = to_partner(plus(proj_blocks[0], proj_one, *proj_on).astype(jnp.bfloat16))
    skip_blocks = pair_sum(skip_keep, skip_came)
    skip_near = scatter_near(skip_blocks)
    enc2, proj_sum, skip_blocks, skip_near, enc3, pre_grad = together(
        (enc2, proj_sum, skip_blocks, skip_near, enc3, pre_grad)
    )
    proj_sum = proj_sum.astype(jnp.float32)
    enc3 = to_partner(enc3)
    skip_on = scatter_on(skip_blocks, skip_near)
    skip_one = chip_flip(skip_blocks[1], 1)
    skip_sum = plus(skip_blocks[0], skip_one, *skip_on)
    (dec_grad,) = row_call(upper_back, [pre_grad], skip_w, skip_parts, 1, 256, 20)
    enc_grad = jnp.zeros_like(enc_rows)
    for at, part in zip(cuts, (enc0, enc1, enc2, enc3)):
        enc_grad = lax.dynamic_update_slice(enc_grad, part, (at, 0))

    new_proj = adam_update(w_proj[0], m_proj[0], v_proj[0], proj_sum)
    new_skip = adam_update(w_skip[0], m_skip[0], v_skip[0], skip_sum)
    streams = tuple(value.reshape(1, micro, tokens_here, width) for value in (dec_out, enc_grad, dec_grad))
    return streams + tuple(value[None] for value in new_proj + new_skip)


def solution(mesh):
    tokens = P("section", None, "dp", None)
    weights = P("section", "dp", None)
    return jax.shard_map(
        body,
        mesh=mesh,
        in_specs=(tokens,) * 3 + (weights,) * 6,
        out_specs=(tokens,) * 3 + (weights,) * 6,
        check_vma=False,
    )
```

time: 216 us -> 204 us (0.944)
  Pallas kernels: 0 us -> 48.5 us
  matrix products: 43.3 us -> 0 us
  waiting for transfers between devices: 120 us -> 101 us
  starting transfers between devices: 20.5 us -> 34.8 us
  local copies, waits for them, and re-layouts: 18.3 us -> 9.81 us
  other arithmetic: 13.2 us -> 8.9 us
    pallas_call x0 -> x9, Pallas kernels: none -> 48.5 us  [the longest x6 32.2 us: row_call(): pl.pallas_call(kernel, grid=(rows // tile,), in_specs=[taken] * len(row_a...]
    dot_general x9 -> x0, matrix products: 43.3 us -> none  [the longest x3 16.4 us: matmul(): return jnp.dot(left, right, preferred_element_type=jnp.float32)]
    ppermute x4 -> x9, waiting for transfers between devices: 37.2 us -> 19.4 us  [to_partner(): return lax.ppermute(value, 'section', pairs)]
    ppermute x4 -> x9, starting transfers between devices: 5.18 us -> 12.4 us  [to_partner(): return lax.ppermute(value, 'section', pairs)]
    ppermute x12 -> x15, starting transfers between devices: 12.9 us -> 19.6 us  [to_chips(): lax.ppermute(value, 'dp', [(2 * a + c, 2 * b + c) for a, b in pairs for c...]
    ppermute x12 -> x15, waiting for transfers between devices: 80.1 us -> 73.8 us  [to_chips(): lax.ppermute(value, 'dp', [(2 * a + c, 2 * b + c) for a, b in pairs for c...]
    ppermute x10 -> x14, waiting for transfers between devices: 2.27 us -> 7.75 us  [core_flip(): lax.ppermute(value, 'dp', [(d, d ^ 1) for d in range(lax.axis_size('dp'))])]
    dynamic_update_slice x15 -> x28, local copies, waits for them, and re-layouts: 8.84 us -> 5.25 us  [the longest x12 4.37 us: assemble(): lax.dynamic_update_slice(whole, piece[None, None], (chip ^ k, core, 0, 0))]
  transfers between devices with their start and end apart: 26 -> 38, of which waited for: 12 -> 19; matrix products, arithmetic and copies ran while one was open for 16% -> 7% of each run, Pallas kernels for 0% -> 14%
where the time goes in v2:
time: 204 us
  waiting for transfers between devices  101 us (50%)
  Pallas kernels  48.5 us (24%)
  starting transfers between devices  34.8 us (17%)
  local copies, waits for them, and re-layouts  9.81 us (5%)
  other arithmetic  8.9 us (4%)
    ppermute x15, waiting for transfers between devices, to_chips(): lax.ppermute(value, 'dp', [(2 * a + c, 2 * b + c) for a, b in pairs for c...  73.8 us
    pallas_call x6, Pallas kernels, row_call(): pl.pallas_call(kernel, grid=(rows // tile,), in_specs=[taken] * len(row_a...  32.2 us
    ppermute x15, starting transfers between devices, to_chips(): lax.ppermute(value, 'dp', [(2 * a + c, 2 * b + c) for a, b in pairs for c...  19.6 us
    ppermute x9, waiting for transfers between devices, to_partner(): return lax.ppermute(value, 'section', pairs)  19.4 us
    pallas_call x2, Pallas kernels, weight_grad(): pl.pallas_call(kernel, grid=(len(lefts) * steps,), in_specs=[spec(n, part...  12.8 us
    ppermute x9, starting transfers between devices, to_partner(): return lax.ppermute(value, 'section', pairs)  12.4 us
    ppermute x14, waiting for transfers between devices, core_flip(): lax.ppermute(value, 'dp', [(d, d ^ 1) for d in range(lax.axis_size('dp'))])  7.75 us
    broadcast_in_dim x2, other arithmetic, body(): return streams + tuple((value[None] for value in new_proj + new_skip))  4.83 us
  transfers between devices with their start and end apart: 38, of which 19 were waited for; matrix products, arithmetic and copies ran while one was open for 7% of the time, Pallas kernels for 14%

profile of v2, /device:TPU:0, one launch (start us, length us, event | category | flops | bytes accessed | tf_op | source)
XLA Modules:
  0.0 204.2 jit_solution(15780252454665187952)
XLA Ops:
  1.9 3.0 %collective-permute-start = (bf16[144,1152]{1,0:T(8,128)(2,1)S(1)}, bf16[144,1152]{1,0:T(8,128)(2,1)S(1)}, u32[]{:S(2)}, u32[]{:S(2)}) collective-permute-start(bf16[144,1152]{1,0:T(8,128)(2,1)S(1)} %bitcast_convert_fusion.1), channel_id=1, source_target_pairs={{0,16},{8,24},{16,0},{24,8},{1,17},{9,25},{17,1},{25,9},{2,18},{10... | collective-permute-start | bytes 995336 | tf_op jit(solution)/shard_map/ppermute | solution.py:36
  6.4 1.6 collective-permute-start.1
  8.0 2.6 %collective-permute-start.2 = (bf16[96,1152]{1,0:T(8,128)(2,1)S(1)}, bf16[96,1152]{1,0:T(8,128)(2,1)}, u32[]{:S(2)}, u32[]{:S(2)}) collective-permute-start(bf16[96,1152]{1,0:T(8,128)(2,1)S(1)} %slice.20), channel_id=1, source_target_pairs={{0,4},{1,5},{2,6},{3,7},{4,0},{5,1},{6,2},{7,3},{8,12},{9,13},{10,... | collective-permute-start | bytes 663560 | tf_op jit(solution)/shard_map/ppermute | solution.py:44
  10.8 7.2 %collective-permute-done.1 = bf16[96,1152]{1,0:T(8,128)(2,1)S(1)} collective-permute-done((bf16[96,1152]{1,0:T(8,128)(2,1)S(1)}, bf16[96,1152]{1,0:T(8,128)(2,1)S(1)}, u32[]{:S(2)}, u32[]{:S(2)}) %collective-permute-start.1) | collective-permute-done | bytes 221216 | tf_op jit(solution)/shard_map/ppermute | solution.py:44
  18.0 2.5 %collective-permute-done.2 = bf16[96,1152]{1,0:T(8,128)(2,1)} collective-permute-done((bf16[96,1152]{1,0:T(8,128)(2,1)S(1)}, bf16[96,1152]{1,0:T(8,128)(2,1)}, u32[]{:S(2)}, u32[]{:S(2)}) %collective-permute-start.2) | collective-permute-done | bytes 221216 | tf_op jit(solution)/shard_map/ppermute | solution.py:44
  21.4 2.6 %collective-permute-start.7 = (bf16[192,1152]{1,0:T(8,128)(2,1)S(1)}, bf16[192,1152]{1,0:T(8,128)(2,1)S(1)}, u32[]{:S(2)}, u32[]{:S(2)}) collective-permute-start(bf16[192,1152]{1,0:T(8,128)(2,1)S(1)} %slice.21), channel_id=1, source_target_pairs={{0,4},{1,5},{2,6},{3,7},{4,0},{5,1},{6,2},{7,3},{8,12},{9,13},{10,... | collective-permute-start | bytes 1327112 | tf_op jit(solution)/shard_map/ppermute | solution.py:44
  24.0 1.9 collective-permute-start.5
  26.6 25.8 %collective-permute-done.4 = bf16[144,1152]{1,0:T(8,128)(2,1)S(1)} collective-permute-done((bf16[144,1152]{1,0:T(8,128)(2,1)S(1)}, bf16[144,1152]{1,0:T(8,128)(2,1)S(1)}, u32[]{:S(2)}, u32[]{:S(2)}) %collective-permute-start.4) | collective-permute-done | bytes 331808 | tf_op jit(solution)/shard_map/ppermute | solution.py:44
  52.4 3.9 %collective-permute-done.5 = bf16[144,1152]{1,0:T(8,128)(2,1)} collective-permute-done((bf16[144,1152]{1,0:T(8,128)(2,1)S(1)}, bf16[144,1152]{1,0:T(8,128)(2,1)}, u32[]{:S(2)}, u32[]{:S(2)}) %collective-permute-start.5) | collective-permute-done | bytes 331808 | tf_op jit(solution)/shard_map/ppermute | solution.py:44
  56.5 1.6 collective-permute-start.8
  58.0 1.9 collective-permute-start.10
  60.1 6.5 %collective-permute-done.10 = bf16[96,1152]{1,0:T(8,128)(2,1)} collective-permute-done((bf16[96,1152]{1,0:T(8,128)(2,1)}, bf16[96,1152]{1,0:T(8,128)(2,1)}, u32[]{:S(2)}, u32[]{:S(2)}) %collective-permute-start.10) | collective-permute-done | bytes 221216 | tf_op jit(solution)/shard_map/ppermute | solution.py:44
  74.8 1.5 collective-permute-start.11
  76.6 1.5 collective-permute-done.13
  83.8 6.6 %collective-permute-done.11.refs_2_ = bf16[256,1152]{1,0:T(8,128)(2,1)S(1)} collective-permute-done((bf16[256,1152]{1,0:T(8,128)(2,1)S(1)}, bf16[256,1152]{1,0:T(8,128)(2,1)S(1)}, u32[]{:S(2)}, u32[]{:S(2)}) %collective-permute-start.11) | collective-permute-done | bytes 589856 | tf_op jit(solution)/shard_map/ppermute | solution.py:36
  90.4 3.5 %shard_map.160.refs_1_ = bf16[1024,1152]{1,0:T(8,128)(2,1)S(1)} custom-call(bf16[640,1152]{1,0:T(8,128)(2,1)S(1)} %collective-permute-done.3.refs_0_, bf16[128,1152]{1,0:T(8,128)(2,1)S(1)} %collective-permute-done.8.refs_1_, bf16[256,1152]{1,0:T(8,128)(2,1)S(1)} %collective-permute-done.11.refs_2_, bf16[1152,1152]{1,0:T(8,128)(2,1)S(1)} %bitcast.129), custom_call_target="tpu_custom_call" | custom-call | flops 1000 | bytes 1000 | tf_op jit(solution)/shard_map/pallas_call | solution.py:185
  93.9 15.8 %shard_map.161 = (bf16[1024,1152]{1,0:T(8,128)(2,1)}, bf16[1024,1152]{1,0:T(8,128)(2,1)S(1)}, bf16[1024,1152]{1,0:T(8,128)(2,1)S(1)}) custom-call(bf16[1024,1152]{1,0:T(8,128)(2,1)S(1)} %bitcast.140, bf16[1024,1152]{1,0:T(8,128)(2,1)S(1)} %shard_map.160.refs_1_, bf16[1024,1152]{1,0:T(8,128)(2,1)S(1)} %bitcast.142, bf16[768,1152]{1,0:T(8,128)(2,1)S(1)} %bitcast.137, ...), custom_call_target="tpu_custom_call" | custom-call | flops 1000 | bytes 1000 | tf_op jit(solution)/shard_map/pallas_call | solution.py:145
  109.7 4.6 %shard_map.162 = bf16[1152,1152]{1,0:T(8,128)(2,1)S(1)} custom-call(bf16[640,1152]{1,0:T(8,128)(2,1)S(1)} %collective-permute-done.3.refs_0_, bf16[128,1152]{1,0:T(8,128)(2,1)S(1)} %collective-permute-done.8.refs_1_, bf16[256,1152]{1,0:T(8,128)(2,1)S(1)} %collective-permute-done.11.refs_2_, bf16[1024,1152]{1,0:T(8,128)(2,1)S(1)} %get-tuple-element.122.refs_3_.refs_0_), custom_call_target="tpu_custom_call" | custom-call | flops 1000 | bytes 1000 | tf_op jit(solution)/shard_map/pallas_call | solution.py:239
  115.8 1.9 collective-permute-done.25
  117.7 1.5 collective-permute-start.26
  120.9 8.1 %shard_map.164 = bf16[2304,1152]{1,0:T(8,128)(2,1)S(1)} custom-call(bf16[1024,1152]{1,0:T(8,128)(2,1)S(1)} %bitcast.141, bf16[1024,1152]{1,0:T(8,128)(2,1)S(1)} %shard_map.160.refs_1_, bf16[1024,1152]{1,0:T(8,128)(2,1)S(1)} %get-tuple-element.133.refs_2_.refs_0_), custom_call_target="tpu_custom_call" | custom-call | flops 1000 | bytes 1000 | tf_op jit(solution)/shard_map/pallas_call | solution.py:239
  129.0 2.1 %shard_map.165 = bf16[256,1152]{1,0:T(8,128)(2,1)S(1)} custom-call(bf16[1024,1152]{1,0:T(8,128)(2,1)S(1)} %get-tuple-element.122.refs_3_.refs_0_, bf16[1152,1152]{1,0:T(8,128)(2,1)S(1)} %bitcast.131), custom_call_target="tpu_custom_call" | custom-call | flops 1000 | bytes 1000 | tf_op jit(solution)/shard_map/pallas_call | solution.py:145
  132.3 2.2 %collective-permute-start.29 = (bf16[144,1152]{1,0:T(8,128)(2,1)S(1)}, bf16[144,1152]{1,0:T(8,128)(2,1)S(1)}, u32[]{:S(2)}, u32[]{:S(2)}) collective-permute-start(bf16[144,1152]{1,0:T(8,128)(2,1)S(1)} %add_convert_fusion.4), channel_id=1, source_target_pairs={{0,4},{1,5},{2,6},{3,7},{4,0},{5,1},{6,2},{7,3},{8,12},{9,13},{10,... | collective-permute-start | bytes 995336 | tf_op jit(solution)/shard_map/ppermute | solution.py:44
  136.8 2.6 %shard_map.167 = bf16[512,1152]{1,0:T(8,128)(2,1)S(1)} custom-call(bf16[1024,1152]{1,0:T(8,128)(2,1)S(1)} %get-tuple-element.122.refs_3_.refs_0_, bf16[1152,1152]{1,0:T(8,128)(2,1)S(1)} %bitcast.133), custom_call_target="tpu_custom_call" | custom-call | flops 1000 | bytes 1000 | tf_op jit(solution)/shard_map/pallas_call | solution.py:145
  139.4 11.0 %collective-permute-done.29 = bf16[144,1152]{1,0:T(8,128)(2,1)S(1)} collective-permute-done((bf16[144,1152]{1,0:T(8,128)(2,1)S(1)}, bf16[144,1152]{1,0:T(8,128)(2,1)S(1)}, u32[]{:S(2)}, u32[]{:S(2)}) %collective-permute-start.29) | collective-permute-done | bytes 331808 | tf_op jit(solution)/shard_map/ppermute | solution.py:44
  152.8 1.6 collective-permute-start.33
  155.1 12.8 %collective-permute-done.32 = bf16[128,1152]{1,0:T(8,128)(2,1)S(1)} collective-permute-done((bf16[128,1152]{1,0:T(8,128)(2,1)S(1)}, bf16[128,1152]{1,0:T(8,128)(2,1)S(1)}, u32[]{:S(2)}, u32[]{:S(2)}) %collective-permute-start.32) | collective-permute-done | bytes 294944 | tf_op jit(solution)/shard_map/ppermute | solution.py:36
  167.9 1.5 collective-permute-start.35
  171.7 1.8 fusion.6
  173.5 9.5 %shard_map.168 = bf16[1024,1152]{1,0:T(8,128)(2,1)} custom-call(bf16[1024,1152]{1,0:T(8,128)(2,1)S(1)} %get-tuple-element.133.refs_2_.refs_0_, bf16[768,1152]{1,0:T(8,128)(2,1)S(1)} %bitcast.138, bf16[1536,1152]{1,0:T(8,128)(2,1)S(1)} %bitcast.135), custom_call_target="tpu_custom_call" | custom-call | flops 1000 | bytes 1000 | tf_op jit(solution)/shard_map/pallas_call | solution.py:145
  183.1 16.4 %collective-permute-done.37 = bf16[288,1152]{1,0:T(8,128)(2,1)S(1)} collective-permute-done((bf16[288,1152]{1,0:T(8,128)(2,1)S(1)}, bf16[288,1152]{1,0:T(8,128)(2,1)S(1)}, u32[]{:S(2)}, u32[]{:S(2)}) %collective-permute-start.37) | collective-permute-done | bytes 663584 | tf_op jit(solution)/shard_map/ppermute | solution.py:44
  199.5 3.1 %fusion.8 = (f32[1,288,1152]{2,1,0:T(8,128)}, f32[1,288,1152]{2,1,0:T(8,128)}, f32[1,288,1152]{2,1,0:T(8,128)}) fusion(bf16[288,1152]{1,0:T(8,128)(2,1)S(1)} %collective-permute-done.37, bf16[288,1152]{1,0:T(8,128)(2,1)S(1)} %collective-permute-done.36, bf16[288,1152]{1,0:T(8,128)(2,1)S(1)} %get-tuple-element.135, f32[1,288,1152]{2,1,0:T(8,128)S(1)} %copy-done.6, ...), kind=kLoop, calls=%fused_computation.61 | loop fusion | flops 5971968 | bytes 9953280 | tf_op jit(solution)/shard_map/broadcast_in_dim | solution.py:351
  (138 shorter events, 32.2 us)
Async XLA Ops:
  1.9 18.5 %collective-permute-start = (bf16[144,1152]{1,0:T(8,128)(2,1)S(1)}, bf16[144,1152]{1,0:T(8,128)(2,1)S(1)}, u32[]{:S(2)}, u32[]{:S(2)}) collective-permute-start(bf16[144,1152]{1,0:T(8,128)(2,1)S(1)} %bitcast_convert_fusion.1), channel_id=1, source_target_pairs={{0,16},{8,24},{16,0},{24,8},{1,17},{9,25},{17,1},{25,9},{2,18},{10... | collective-permute-start | bytes 995336 | tf_op jit(solution)/shard_map/ppermute | solution.py:36
  6.4 11.6 %collective-permute-start.1 = (bf16[96,1152]{1,0:T(8,128)(2,1)S(1)}, bf16[96,1152]{1,0:T(8,128)(2,1)S(1)}, u32[]{:S(2)}, u32[]{:S(2)}) collective-permute-start(bf16[96,1152]{1,0:T(8,128)(2,1)S(1)} %slice.20), channel_id=1, source_target_pairs={{0,2},{1,3},{2,0},{3,1},{4,6},{5,7},{6,4},{7,5},{8,10},{9,11},{10,... | collective-permute-start | bytes 663560 | tf_op jit(solution)/shard_map/ppermute | solution.py:44
  8.0 12.4 %collective-permute-start.2 = (bf16[96,1152]{1,0:T(8,128)(2,1)S(1)}, bf16[96,1152]{1,0:T(8,128)(2,1)}, u32[]{:S(2)}, u32[]{:S(2)}) collective-permute-start(bf16[96,1152]{1,0:T(8,128)(2,1)S(1)} %slice.20), channel_id=1, source_target_pairs={{0,4},{1,5},{2,6},{3,7},{4,0},{5,1},{6,2},{7,3},{8,12},{9,13},{10,... | collective-permute-start | bytes 663560 | tf_op jit(solution)/shard_map/ppermute | solution.py:44
  20.4 35.9 %collective-permute-start.3 = (bf16[640,1152]{1,0:T(8,128)(2,1)S(1)}, bf16[640,1152]{1,0:T(8,128)(2,1)S(1)}, u32[]{:S(2)}, u32[]{:S(2)}) collective-permute-start(bf16[640,1152]{1,0:T(8,128)(2,1)S(1)} %slice.22), channel_id=1, source_target_pairs={{0,16},{8,24},{16,0},{24,8},{1,17},{9,25},{17,1},{25,9},{2,18},{10... | collective-permute-start | bytes 4423688 | tf_op jit(solution)/shard_map/ppermute | solution.py:36
  20.9 35.4 %collective-permute-start.6 = (bf16[192,1152]{1,0:T(8,128)(2,1)S(1)}, bf16[192,1152]{1,0:T(8,128)(2,1)S(1)}, u32[]{:S(2)}, u32[]{:S(2)}) collective-permute-start(bf16[192,1152]{1,0:T(8,128)(2,1)S(1)} %slice.21), channel_id=1, source_target_pairs={{0,2},{1,3},{2,0},{3,1},{4,6},{5,7},{6,4},{7,5},{8,10},{9,11},{10,... | collective-permute-start | bytes 1327112 | tf_op jit(solution)/shard_map/ppermute | solution.py:44
  21.4 35.0 %collective-permute-start.7 = (bf16[192,1152]{1,0:T(8,128)(2,1)S(1)}, bf16[192,1152]{1,0:T(8,128)(2,1)S(1)}, u32[]{:S(2)}, u32[]{:S(2)}) collective-permute-start(bf16[192,1152]{1,0:T(8,128)(2,1)S(1)} %slice.21), channel_id=1, source_target_pairs={{0,4},{1,5},{2,6},{3,7},{4,0},{5,1},{6,2},{7,3},{8,12},{9,13},{10,... | collective-permute-start | bytes 1327112 | tf_op jit(solution)/shard_map/ppermute | solution.py:44
  24.0 28.5 %collective-permute-start.4 = (bf16[144,1152]{1,0:T(8,128)(2,1)S(1)}, bf16[144,1152]{1,0:T(8,128)(2,1)S(1)}, u32[]{:S(2)}, u32[]{:S(2)}) collective-permute-start(bf16[144,1152]{1,0:T(8,128)(2,1)S(1)} %collective-permute-done), channel_id=1, source_target_pairs={{0,2},{1,3},{2,0},{3,1},{4,6},{5,7},{6,4},{7,5},{8,10},{9,11},{10,... | collective-permute-start | bytes 995336 | tf_op jit(solution)/shard_map/ppermute | solution.py:44
  24.0 32.4 %collective-permute-start.5 = (bf16[144,1152]{1,0:T(8,128)(2,1)S(1)}, bf16[144,1152]{1,0:T(8,128)(2,1)}, u32[]{:S(2)}, u32[]{:S(2)}) collective-permute-start(bf16[144,1152]{1,0:T(8,128)(2,1)S(1)} %collective-permute-done), channel_id=1, source_target_pairs={{0,4},{1,5},{2,6},{3,7},{4,0},{5,1},{6,2},{7,3},{8,12},{9,13},{10,... | collective-permute-start | bytes 995336 | tf_op jit(solution)/shard_map/ppermute | solution.py:44
  56.4 10.3 %collective-permute-start.9 = (bf16[144,1152]{1,0:T(8,128)(2,1)}, bf16[144,1152]{1,0:T(8,128)(2,1)}, u32[]{:S(2)}, u32[]{:S(2)}) collective-permute-start(bf16[144,1152]{1,0:T(8,128)(2,1)} %collective-permute-done.5), channel_id=1, source_target_pairs={{0,2},{1,3},{2,0},{3,1},{4,6},{5,7},{6,4},{7,5},{8,10},{9,11},{10,... | collective-permute-start | bytes 995336 | tf_op jit(solution)/shard_map/ppermute | solution.py:44
  56.5 10.2 %collective-permute-start.8 = (bf16[128,1152]{1,0:T(8,128)(2,1)}, bf16[128,1152]{1,0:T(8,128)(2,1)S(1)}, u32[]{:S(2)}, u32[]{:S(2)}) collective-permute-start(bf16[128,1152]{1,0:T(8,128)(2,1)} %slice.23), channel_id=1, source_target_pairs={{0,16},{8,24},{16,0},{24,8},{1,17},{9,25},{17,1},{25,9},{2,18},{10... | collective-permute-start | bytes 884744 | tf_op jit(solution)/shard_map/ppermute | solution.py:36
  58.0 8.6 %collective-permute-start.10 = (bf16[96,1152]{1,0:T(8,128)(2,1)}, bf16[96,1152]{1,0:T(8,128)(2,1)}, u32[]{:S(2)}, u32[]{:S(2)}) collective-permute-start(bf16[96,1152]{1,0:T(8,128)(2,1)} %collective-permute-done.2), channel_id=1, source_target_pairs={{0,2},{1,3},{2,0},{3,1},{4,6},{5,7},{6,4},{7,5},{8,10},{9,11},{10,... | collective-permute-start | bytes 663560 | tf_op jit(solution)/shard_map/ppermute | solution.py:44
  66.6 17.0 %collective-permute-start.22 = (bf16[192,1152]{1,0:T(8,128)(2,1)S(1)}, bf16[192,1152]{1,0:T(8,128)(2,1)S(1)}, u32[]{:S(2)}, u32[]{:S(2)}) collective-permute-start(bf16[192,1152]{1,0:T(8,128)(2,1)S(1)} %collective-permute-done.7), channel_id=1, source_target_pairs={{0,1},{1,0},{2,3},{3,2},{4,5},{5,4},{6,7},{7,6},{8,9},{9,8},{10,11... | collective-permute-start | bytes 1327112 | tf_op jit(solution)/shard_map/ppermute | solution.py:52
  66.6 15.3 %collective-permute-start.23 = (bf16[192,1152]{1,0:T(8,128)(2,1)S(1)}, bf16[192,1152]{1,0:T(8,128)(2,1)S(1)}, u32[]{:S(2)}, u32[]{:S(2)}) collective-permute-start(bf16[192,1152]{1,0:T(8,128)(2,1)S(1)} %collective-permute-done.7), channel_id=1, source_target_pairs={{0,2},{1,3},{2,0},{3,1},{4,6},{5,7},{6,4},{7,5},{8,10},{9,11},{10,... | collective-permute-start | bytes 1327112 | tf_op jit(solution)/shard_map/ppermute | solution.py:44
  67.6 8.7 %collective-permute-start.12 = (bf16[144,1152]{1,0:T(8,128)(2,1)}, bf16[144,1152]{1,0:T(8,128)(2,1)S(1)}, u32[]{:S(2)}, u32[]{:S(2)}) collective-permute-start(bf16[144,1152]{1,0:T(8,128)(2,1)} %copy-done.12), channel_id=1, source_target_pairs={{0,1},{1,0},{2,3},{3,2},{4,5},{5,4},{6,7},{7,6},{8,9},{9,8},{10,11... | collective-permute-start | bytes 995336 | tf_op jit(solution)/shard_map/ppermute | solution.py:52
  68.1 14.2 %collective-permute-start.20 = (bf16[192,1152]{1,0:T(8,128)(2,1)S(1)}, bf16[192,1152]{1,0:T(8,128)(2,1)S(1)}, u32[]{:S(2)}, u32[]{:S(2)}) collective-permute-start(bf16[192,1152]{1,0:T(8,128)(2,1)S(1)} %slice.21), channel_id=1, source_target_pairs={{0,1},{1,0},{2,3},{3,2},{4,5},{5,4},{6,7},{7,6},{8,9},{9,8},{10,11... | collective-permute-start | bytes 1327112 | tf_op jit(solution)/shard_map/ppermute | solution.py:52
  74.8 15.6 %collective-permute-start.11 = (bf16[256,1152]{1,0:T(8,128)(2,1)S(1)}, bf16[256,1152]{1,0:T(8,128)(2,1)S(1)}, u32[]{:S(2)}, u32[]{:S(2)}) collective-permute-start(bf16[256,1152]{1,0:T(8,128)(2,1)S(1)} %slice.24), channel_id=1, source_target_pairs={{0,16},{8,24},{16,0},{24,8},{1,17},{9,25},{17,1},{25,9},{2,18},{10... | collective-permute-start | bytes 1769480 | tf_op jit(solution)/shard_map/ppermute | solution.py:36
  78.0 1.8 collective-permute-start.14
  79.9 1.8 collective-permute-start.15
  81.9 11.9 %collective-permute-start.24 = (bf16[192,1152]{1,0:T(8,128)(2,1)S(1)}, bf16[192,1152]{1,0:T(8,128)(2,1)S(1)}, u32[]{:S(2)}, u32[]{:S(2)}) collective-permute-start(bf16[192,1152]{1,0:T(8,128)(2,1)S(1)} %collective-permute-done.23), channel_id=1, source_target_pairs={{0,1},{1,0},{2,3},{3,2},{4,5},{5,4},{6,7},{7,6},{8,9},{9,8},{10,11... | collective-permute-start | bytes 1327112 | tf_op jit(solution)/shard_map/ppermute | solution.py:52
  114.6 3.1 %collective-permute-start.25 = (bf16[4,144,1152]{2,1,0:T(8,128)(2,1)S(1)}, bf16[4,144,1152]{2,1,0:T(8,128)(2,1)S(1)}, u32[]{:S(2)}, u32[]{:S(2)}) collective-permute-start(bf16[4,144,1152]{2,1,0:T(8,128)(2,1)S(1)} %get-tuple-element.148), channel_id=1, source_target_pairs={{0,1},{1,0},{2,3},{3,2},{4,5},{5,4},{6,7},{7,6},{8,9},{9,8},{10,11... | collective-permute-start | bytes 3981320 | tf_op jit(solution)/shard_map/ppermute | solution.py:52
  117.7 13.8 %collective-permute-start.26 = (bf16[128,1152]{1,0:T(8,128)(2,1)S(1)}, bf16[128,1152]{1,0:T(8,128)(2,1)S(1)}, u32[]{:S(2)}, u32[]{:S(2)}) collective-permute-start(bf16[128,1152]{1,0:T(8,128)(2,1)S(1)} %shard_map.163), channel_id=1, source_target_pairs={{0,16},{8,24},{16,0},{24,8},{1,17},{9,25},{17,1},{25,9},{2,18},{10... | collective-permute-start | bytes 884744 | tf_op jit(solution)/shard_map/ppermute | solution.py:36
  119.7 11.9 %collective-permute-start.27 = (bf16[144,1152]{1,0:T(8,128)(2,1)S(1)}, bf16[144,1152]{1,0:T(8,128)(2,1)S(1)}, u32[]{:S(2)}, u32[]{:S(2)}) collective-permute-start(bf16[144,1152]{1,0:T(8,128)(2,1)S(1)} %get-tuple-element.150), channel_id=1, source_target_pairs={{0,2},{1,3},{2,0},{3,1},{4,6},{5,7},{6,4},{7,5},{8,10},{9,11},{10,... | collective-permute-start | bytes 995336 | tf_op jit(solution)/shard_map/ppermute | solution.py:44
  131.6 19.3 %collective-permute-start.31 = (bf16[4,288,1152]{2,1,0:T(8,128)(2,1)S(1)}, bf16[4,288,1152]{2,1,0:T(8,128)(2,1)S(1)}, u32[]{:S(2)}, u32[]{:S(2)}) collective-permute-start(bf16[4,288,1152]{2,1,0:T(8,128)(2,1)S(1)} %get-tuple-element.121), channel_id=1, source_target_pairs={{0,1},{1,0},{2,3},{3,2},{4,5},{5,4},{6,7},{7,6},{8,9},{9,8},{10,11... | collective-permute-start | bytes 7962632 | tf_op jit(solution)/shard_map/ppermute | solution.py:52
  131.7 19.2 %collective-permute-start.28 = (bf16[256,1152]{1,0:T(8,128)(2,1)S(1)}, bf16[256,1152]{1,0:T(8,128)(2,1)S(1)}, u32[]{:S(2)}, u32[]{:S(2)}) collective-permute-start(bf16[256,1152]{1,0:T(8,128)(2,1)S(1)} %shard_map.165), channel_id=1, source_target_pairs={{0,16},{8,24},{16,0},{24,8},{1,17},{9,25},{17,1},{25,9},{2,18},{10... | collective-permute-start | bytes 1769480 | tf_op jit(solution)/shard_map/ppermute | solution.py:36
  132.3 18.0 %collective-permute-start.29 = (bf16[144,1152]{1,0:T(8,128)(2,1)S(1)}, bf16[144,1152]{1,0:T(8,128)(2,1)S(1)}, u32[]{:S(2)}, u32[]{:S(2)}) collective-permute-start(bf16[144,1152]{1,0:T(8,128)(2,1)S(1)} %add_convert_fusion.4), channel_id=1, source_target_pairs={{0,4},{1,5},{2,6},{3,7},{4,0},{5,1},{6,2},{7,3},{8,12},{9,13},{10,... | collective-permute-start | bytes 995336 | tf_op jit(solution)/shard_map/ppermute | solution.py:44
  134.6 16.3 %collective-permute-start.30 = (bf16[144,1152]{1,0:T(8,128)(2,1)S(1)}, bf16[144,1152]{1,0:T(8,128)(2,1)S(1)}, u32[]{:S(2)}, u32[]{:S(2)}) collective-permute-start(bf16[144,1152]{1,0:T(8,128)(2,1)S(1)} %get-tuple-element.117), channel_id=1, source_target_pairs={{0,2},{1,3},{2,0},{3,1},{4,6},{5,7},{6,4},{7,5},{8,10},{9,11},{10,... | collective-permute-start | bytes 995336 | tf_op jit(solution)/shard_map/ppermute | solution.py:44
  151.8 16.1 %collective-permute-start.34 = (bf16[288,1152]{1,0:T(8,128)(2,1)S(1)}, bf16[288,1152]{1,0:T(8,128)(2,1)S(1)}, u32[]{:S(2)}, u32[]{:S(2)}) collective-permute-start(bf16[288,1152]{1,0:T(8,128)(2,1)S(1)} %get-tuple-element.144), channel_id=1, source_target_pairs={{0,2},{1,3},{2,0},{3,1},{4,6},{5,7},{6,4},{7,5},{8,10},{9,11},{10,... | collective-permute-start | bytes 1990664 | tf_op jit(solution)/shard_map/ppermute | solution.py:44
  152.8 15.1 %collective-permute-start.33 = (bf16[144,1152]{1,0:T(8,128)(2,1)S(1)}, bf16[144,1152]{1,0:T(8,128)(2,1)S(1)}, u32[]{:S(2)}, u32[]{:S(2)}) collective-permute-start(bf16[144,1152]{1,0:T(8,128)(2,1)S(1)} %add_convert_fusion.3), channel_id=1, source_target_pairs={{0,16},{8,24},{16,0},{24,8},{1,17},{9,25},{17,1},{25,9},{2,18},{10... | collective-permute-start | bytes 995336 | tf_op jit(solution)/shard_map/ppermute | solution.py:36
  154.3 13.6 %collective-permute-start.32 = (bf16[128,1152]{1,0:T(8,128)(2,1)S(1)}, bf16[128,1152]{1,0:T(8,128)(2,1)S(1)}, u32[]{:S(2)}, u32[]{:S(2)}) collective-permute-start(bf16[128,1152]{1,0:T(8,128)(2,1)S(1)} %shard_map.166), channel_id=1, source_target_pairs={{0,16},{8,24},{16,0},{24,8},{1,17},{9,25},{17,1},{25,9},{2,18},{10... | collective-permute-start | bytes 884744 | tf_op jit(solution)/shard_map/ppermute | solution.py:36
  167.9 34.7 %collective-permute-start.35 = (bf16[512,1152]{1,0:T(8,128)(2,1)S(1)}, bf16[512,1152]{1,0:T(8,128)(2,1)S(1)}, u32[]{:S(2)}, u32[]{:S(2)}) collective-permute-start(bf16[512,1152]{1,0:T(8,128)(2,1)S(1)} %shard_map.167), channel_id=1, source_target_pairs={{0,16},{8,24},{16,0},{24,8},{1,17},{9,25},{17,1},{25,9},{2,18},{10... | collective-permute-start | bytes 3538952 | tf_op jit(solution)/shard_map/ppermute | solution.py:36
  169.6 29.9 %collective-permute-start.37 = (bf16[288,1152]{1,0:T(8,128)(2,1)S(1)}, bf16[288,1152]{1,0:T(8,128)(2,1)S(1)}, u32[]{:S(2)}, u32[]{:S(2)}) collective-permute-start(bf16[288,1152]{1,0:T(8,128)(2,1)S(1)} %add_convert_fusion.2), channel_id=1, source_target_pairs={{0,4},{1,5},{2,6},{3,7},{4,0},{5,1},{6,2},{7,3},{8,12},{9,13},{10,... | collective-permute-start | bytes 1990664 | tf_op jit(solution)/shard_map/ppermute | solution.py:44
  170.9 28.6 %collective-permute-start.36 = (bf16[288,1152]{1,0:T(8,128)(2,1)S(1)}, bf16[288,1152]{1,0:T(8,128)(2,1)S(1)}, u32[]{:S(2)}, u32[]{:S(2)}) collective-permute-start(bf16[288,1152]{1,0:T(8,128)(2,1)S(1)} %get-tuple-element.136), channel_id=1, source_target_pairs={{0,2},{1,3},{2,0},{3,1},{4,6},{5,7},{6,4},{7,5},{8,10},{9,11},{10,... | collective-permute-start | bytes 1990664 | tf_op jit(solution)/shard_map/ppermute | solution.py:44
  (24 other events, 277.6 us)

commit v3 on v2

--- a/solution.py
+++ b/solution.py
@@ -63,9 +63,7 @@
 
 
 def gather_last(found):
-    for k in range(2, chip_count(), 2):
-        found[k + 1] = chip_flip(found[k], 1)
-    return [found[k] for k in range(chip_count())]
+    return {k + 1: chip_flip(found[k], 1) for k in range(2, chip_count(), 2)}
 
 
 def plus(*terms):
@@ -89,27 +87,32 @@
     return [chip_flip(held[2**n], 2**n) for n in range(1, len(blocks).bit_length() - 1)]
 
 
-def assemble(found):
+def assemble(found, whole=None):
     place = lax.axis_index("dp")
     chip, core = place // 2, place % 2
-    rows, width = found[0].shape
-    whole = jnp.zeros((chip_count(), 2, rows, width), found[0].dtype)
-    for k, piece in enumerate(found):
+    rows, width = found[min(found)].shape
+    if whole is None:
+        whole = jnp.zeros((2 * chip_count() * rows, width), found[0].dtype)
+    whole = whole.reshape(chip_count(), 2, rows, width)
+    for k, piece in found.items():
         whole = lax.dynamic_update_slice(whole, piece[None, None], (chip ^ k, core, 0, 0))
         whole = lax.dynamic_update_slice(whole, core_flip(piece)[None, None], (chip ^ k, 1 - core, 0, 0))
     return whole.reshape(-1, width)
 
 
-def interleave(parts, refs, target, sems):
+def interleave(parts, refs, target, sems, half):
     copies = []
     for (rows, start, stride), ref in zip(parts, refs):
         if rows == stride:
             copies.append(pltpu.make_async_copy(ref, target, sems.at[len(copies)]))
             continue
-        for d in range(ref.shape[0] // rows):
+        count = ref.shape[0] // rows
+        taken = range(count) if half is None else range(half * count // 2, (half + 1) * count // 2)
+        for d in taken:
+            to = (d - taken[0]) * stride + start
             copies.append(
                 pltpu.make_async_copy(
-                    ref.at[pl.ds(d * rows, rows)], target.at[pl.ds(d * stride + start, rows)], sems.at[len(copies)]
+                    ref.at[pl.ds(d * rows, rows)], target.at[pl.ds(to, rows)], sems.at[len(copies)]
                 )
             )
     for copy in copies:
@@ -122,7 +125,7 @@
     return sum(1 if rows == stride else w.shape[0] // rows for w, (rows, _, stride) in zip(weights, parts))
 
 
-def row_call(compute, row_arrays, weights, parts, out_count, tile_rows, vmem_mib, start=0, rows=None):
+def row_call(compute, row_arrays, weights, parts, out_count, tile_rows, vmem_mib, start=0, rows=None, out_type=jnp.bfloat16, half=None):
     width = row_arrays[0].shape[1]
     rows = rows or row_arrays[0].shape[0]
     tile = math.gcd(math.gcd(rows, start), tile_rows)
@@ -136,7 +139,7 @@
 
         @pl.when(pl.program_id(0) == 0)
         def _():
-            interleave(parts, weight_refs, whole, sems)
+            interleave(parts, weight_refs, whole, sems, half)
 
         compute(ins, whole, outs)
 
@@ -147,9 +150,9 @@
         grid=(rows // tile,),
         in_specs=[taken] * len(row_arrays) + [pl.BlockSpec(memory_space=pl.ANY)] * len(weights),
         out_specs=[block] * out_count,
-        out_shape=[jax.ShapeDtypeStruct((rows, width), jnp.bfloat16)] * out_count,
+        out_shape=[jax.ShapeDtypeStruct((rows, width), out_type)] * out_count,
         scratch_shapes=[
-            pltpu.VMEM((sum(w.shape[0] for w in weights), width), jnp.bfloat16),
+            pltpu.VMEM((sum(w.shape[0] for w in weights) // (1 if half is None else 2), width), jnp.bfloat16),
             pltpu.SemaphoreType.DMA((count,)),
         ],
         compiler_params=pltpu.CompilerParams(vmem_limit_bytes=vmem_mib * 2**20),
@@ -194,23 +197,22 @@
     outs[0][...] = dot_nt(ins[0][...], whole[...]).astype(jnp.bfloat16)
 
 
-def upper_back(ins, whole, outs):
-    width = ins[0].shape[1]
-    outs[0][...] = dot_nt(ins[0][...], whole[:width]).astype(jnp.bfloat16)
+def decoder_part(ins, whole, outs):
+    outs[0][...] = dot_nn(ins[0][...], whole[...])
 
 
 def middle(ins, whole, outs):
-    dec, skip, out_grad = ins
-    rows, width = dec.shape
+    from_dec, skip, out_grad = ins
+    rows, width = skip.shape
     part = math.gcd(rows, 256)
     for at in range(0, rows, part):
         here = slice(at, at + part)
-        preact = dot_nn(dec[here], whole[:width]) + dot_nn(skip[here], whole[width:])
+        preact = from_dec[here] + dot_nn(skip[here], whole[...])
         activated, gelu_slope = gelu_parts(preact)
         outs[0][here] = activated.astype(jnp.bfloat16)
         pre_grad = (out_grad[here].astype(jnp.float32) * gelu_slope).astype(jnp.bfloat16)
         outs[1][here] = pre_grad
-        outs[2][here] = dot_nt(pre_grad, whole[width:]).astype(jnp.bfloat16)
+        outs[2][here] = dot_nt(pre_grad, whole[...]).astype(jnp.bfloat16)
 
 
 def weight_grad(lefts, right):
@@ -274,7 +276,7 @@
     out_grad = cotangent[0].reshape(rows, width)
     together = lax.optimization_barrier
 
-    enc_cuts = [rows * n // 8 for n in (5, 6)]
+    enc_cuts = [rows * n // 8 for n in (5, 7)]
     proj_half, skip_half = w_proj[0].astype(jnp.bfloat16), w_skip[0].astype(jnp.bfloat16)
     stride = skip_half.shape[0]
     cut = stride // 48 * 16
@@ -286,18 +288,24 @@
     tail = gather_first(tail)
     enc0, proj_found, tail, head, enc1 = together((enc0, proj_found, tail, head, enc_rows[enc_cuts[0] : enc_cuts[1]]))
     enc1 = to_partner(enc1)
-    proj_found = gather_last(proj_found)
-    head = gather_last(head)
-    enc1, proj_found, tail, head, enc2 = together((enc1, proj_found, tail, head, enc_rows[enc_cuts[1] :]))
+    skip_w = [assemble(head), assemble(tail)]
+    skip_last = [gather_last(head), gather_last(tail)]
+    enc1, proj_found, skip_w, skip_last, enc2 = together(
+        (enc1, proj_found, skip_w, skip_last, enc_rows[enc_cuts[1] :])
+    )
     enc2 = to_partner(enc2)
+    proj_last = gather_last(proj_found)
     proj_whole = assemble(proj_found)
-    skip_w = [assemble(head), assemble(gather_last(tail))]
+    skip_w = [assemble(last, whole) for last, whole in zip(skip_last, skip_w)]
+    skip_parts = [(cut, 0, stride), (stride - cut, cut, stride)]
+    (from_dec,) = row_call(decoder_part, [dec_rows], skip_w, skip_parts, 1, 256, 20, out_type=jnp.float32, half=0)
+    enc2, proj_last, proj_whole, from_dec, skip_w = together((enc2, proj_last, proj_whole, from_dec, skip_w))
+    proj_whole = assemble(proj_last, proj_whole)
     enc_other = (enc0, enc1, enc2)
-    skip_parts = [(cut, 0, stride), (stride - cut, cut, stride)]
 
     skip = project(enc_other, proj_whole, 20)
     dec_out, pre_grad, skip_grad = row_call(
-        middle, [dec_rows, skip, out_grad], skip_w, skip_parts, 3, 512, 30
+        middle, [from_dec, skip, out_grad], skip_w, skip_parts, 3, 512, 30, half=1
     )
     cuts = [0] + [rows * n // 8 for n in (1, 3, 4, 8)]
 
@@ -310,12 +318,14 @@
     grad_proj, skip_grad = together((grad_proj, skip_grad))
     proj_keep, proj_came = pair_send(grad_proj)
     enc0 = back(0, skip_grad)
-    proj_keep, proj_came, enc0, pre_grad, skip_grad = together((proj_keep, proj_came, enc0, pre_grad, skip_grad))
+    enc1 = back(1, skip_grad)
+    proj_keep, proj_came, enc0, enc1, pre_grad, skip_grad = together(
+        (proj_keep, proj_came, enc0, enc1, pre_grad, skip_grad)
+    )
     enc0 = to_partner(enc0)
     proj_blocks = pair_sum(proj_keep, proj_came)
     proj_near = scatter_near(proj_blocks)
     skip_keep, skip_send = pair_split(weight_grad([(dec_rows,), (skip,)], pre_grad))
-    enc1 = back(1, skip_grad)
     enc0, proj_blocks, proj_near, skip_keep, skip_send, enc1, skip_grad = together(
         (enc0, proj_blocks, proj_near, skip_keep, skip_send, enc1, skip_grad)
     )
@@ -340,7 +350,7 @@
     skip_on = scatter_on(skip_blocks, skip_near)
     skip_one = chip_flip(skip_blocks[1], 1)
     skip_sum = plus(skip_blocks[0], skip_one, *skip_on)
-    (dec_grad,) = row_call(upper_back, [pre_grad], skip_w, skip_parts, 1, 256, 20)
+    (dec_grad,) = row_call(project_back, [pre_grad], skip_w, skip_parts, 1, 256, 20, half=0)
     enc_grad = jnp.zeros_like(enc_rows)
     for at, part in zip(cuts, (enc0, enc1, enc2, enc3)):
         enc_grad = lax.dynamic_update_slice(enc_grad, part, (at, 0))

time: 204 us -> 200 us (0.980)
  waiting for transfers between devices: 101 us -> 92.6 us
  local copies, waits for them, and re-layouts: 9.81 us -> 13.4 us
    ppermute x14, waiting for transfers between devices: 7.75 us -> 3.38 us  [core_flip(): lax.ppermute(value, 'dp', [(d, d ^ 1) for d in range(lax.axis_size('dp'))])]
    ppermute x15, waiting for transfers between devices: 73.8 us -> 71.7 us  [to_chips(): lax.ppermute(value, 'dp', [(2 * a + c, 2 * b + c) for a, b in pairs for c...]
    pallas_call x6 -> x7, Pallas kernels: 32.2 us -> 31.3 us  [row_call(): pl.pallas_call(kernel, grid=(rows // tile,), in_specs=[taken] * len(row_a...]
  transfers between devices with their start and end apart: 38 -> 38, of which waited for: 19 -> 13; matrix products, arithmetic and copies ran while one was open for 7% -> 9% of each run, Pallas kernels for 14% -> 14%
where the time goes in v3:
time: 200 us; the launch traced here: 199 us
  waiting for transfers between devices  92.6 us (46%)
  Pallas kernels  47.6 us (24%)
  starting transfers between devices  35.6 us (18%)
  local copies, waits for them, and re-layouts  13.4 us (7%)
  other arithmetic  8.97 us (4%)
    ppermute x15, waiting for transfers between devices, to_chips(): lax.ppermute(value, 'dp', [(2 * a + c, 2 * b + c) for a, b in pairs for c...  71.7 us
    pallas_call x7, Pallas kernels, row_call(): pl.pallas_call(kernel, grid=(rows // tile,), in_specs=[taken] * len(row_a...  31.3 us
    ppermute x15, starting transfers between devices, to_chips(): lax.ppermute(value, 'dp', [(2 * a + c, 2 * b + c) for a, b in pairs for c...  20.9 us
    ppermute x9, waiting for transfers between devices, to_partner(): return lax.ppermute(value, 'section', pairs)  17.5 us
    pallas_call x2, Pallas kernels, weight_grad(): pl.pallas_call(kernel, grid=(len(lefts) * steps,), in_specs=[spec(n, part...  12.8 us
    ppermute x9, starting transfers between devices, to_partner(): return lax.ppermute(value, 'section', pairs)  11.7 us
    dynamic_update_slice x12, local copies, waits for them, and re-layouts, assemble(): lax.dynamic_update_slice(whole, piece[None, None], (chip ^ k, core, 0, 0))  5.44 us
    broadcast_in_dim x2, other arithmetic, body(): return streams + tuple((value[None] for value in new_proj + new_skip))  4.84 us
  transfers between devices with their start and end apart: 38, of which 13 were waited for; matrix products, arithmetic and copies ran while one was open for 9% of the time, Pallas kernels for 14%

profile of v3, /device:TPU:0, one launch (start us, length us, event | category | flops | bytes accessed | tf_op | source)
XLA Modules:
  0.0 199.3 jit_solution(12246556891839824898)
XLA Ops:
  1.9 3.0 %collective-permute-start = (bf16[144,1152]{1,0:T(8,128)(2,1)S(1)}, bf16[144,1152]{1,0:T(8,128)(2,1)}, u32[]{:S(2)}, u32[]{:S(2)}) collective-permute-start(bf16[144,1152]{1,0:T(8,128)(2,1)S(1)} %bitcast_convert_fusion.1), channel_id=1, source_target_pairs={{0,16},{8,24},{16,0},{24,8},{1,17},{9,25},{17,1},{25,9},{2,18},{10... | collective-permute-start | bytes 995336 | tf_op jit(solution)/shard_map/ppermute | solution.py:36
  6.4 2.7 %collective-permute-start.2 = (bf16[96,1152]{1,0:T(8,128)(2,1)S(1)}, bf16[96,1152]{1,0:T(8,128)(2,1)S(1)}, u32[]{:S(2)}, u32[]{:S(2)}) collective-permute-start(bf16[96,1152]{1,0:T(8,128)(2,1)S(1)} %slice.20), channel_id=1, source_target_pairs={{0,4},{1,5},{2,6},{3,7},{4,0},{5,1},{6,2},{7,3},{8,12},{9,13},{10,... | collective-permute-start | bytes 663560 | tf_op jit(solution)/shard_map/ppermute | solution.py:44
  9.1 1.6 collective-permute-start.1
  10.8 8.3 %collective-permute-done.2 = bf16[96,1152]{1,0:T(8,128)(2,1)S(1)} collective-permute-done((bf16[96,1152]{1,0:T(8,128)(2,1)S(1)}, bf16[96,1152]{1,0:T(8,128)(2,1)S(1)}, u32[]{:S(2)}, u32[]{:S(2)}) %collective-permute-start.2) | collective-permute-done | bytes 221216 | tf_op jit(solution)/shard_map/ppermute | solution.py:44
  21.1 2.5 %collective-permute-start.6 = (bf16[192,1152]{1,0:T(8,128)(2,1)S(1)}, bf16[192,1152]{1,0:T(8,128)(2,1)}, u32[]{:S(2)}, u32[]{:S(2)}) collective-permute-start(bf16[192,1152]{1,0:T(8,128)(2,1)S(1)} %slice.21), channel_id=1, source_target_pairs={{0,2},{1,3},{2,0},{3,1},{4,6},{5,7},{6,4},{7,5},{8,10},{9,11},{10,... | collective-permute-start | bytes 1327112 | tf_op jit(solution)/shard_map/ppermute | solution.py:44
  24.7 1.7 slice.24
  26.4 1.9 slice.23
  28.3 26.9 %collective-permute-done.5 = bf16[144,1152]{1,0:T(8,128)(2,1)} collective-permute-done((bf16[144,1152]{1,0:T(8,128)(2,1)}, bf16[144,1152]{1,0:T(8,128)(2,1)}, u32[]{:S(2)}, u32[]{:S(2)}) %collective-permute-start.5) | collective-permute-done | bytes 331808 | tf_op jit(solution)/shard_map/ppermute | solution.py:44
  57.6 1.8 collective-permute-start.16
  60.2 1.6 collective-permute-start.8
  64.2 6.8 %collective-permute-done.16 = bf16[192,1152]{1,0:T(8,128)(2,1)S(1)} collective-permute-done((bf16[192,1152]{1,0:T(8,128)(2,1)}, bf16[192,1152]{1,0:T(8,128)(2,1)S(1)}, u32[]{:S(2)}, u32[]{:S(2)}) %collective-permute-start.16) | collective-permute-done | bytes 442400 | tf_op jit(solution)/shard_map/ppermute | solution.py:44
  70.9 4.6 %collective-permute-done.8.refs_1_ = bf16[256,1152]{1,0:T(8,128)(2,1)S(1)} collective-permute-done((bf16[256,1152]{1,0:T(8,128)(2,1)S(1)}, bf16[256,1152]{1,0:T(8,128)(2,1)S(1)}, u32[]{:S(2)}, u32[]{:S(2)}) %collective-permute-start.8) | collective-permute-done | bytes 589856 | tf_op jit(solution)/shard_map/ppermute | solution.py:36
  79.1 1.5 collective-permute-start.17
  83.8 6.5 %shard_map.160.refs_0_ = f32[1024,1152]{1,0:T(8,128)S(1)} custom-call(bf16[1024,1152]{1,0:T(8,128)(2,1)S(1)} %bitcast.148, bf16[768,1152]{1,0:T(8,128)(2,1)S(1)} %bitcast.143, bf16[1536,1152]{1,0:T(8,128)(2,1)S(1)} %bitcast.140), custom_call_target="tpu_custom_call" | custom-call | flops 1000 | bytes 1000 | tf_op jit(solution)/shard_map/pallas_call | solution.py:148
  90.6 1.5 collective-permute-done.24
  92.1 3.5 %shard_map.161.refs_1_ = bf16[1024,1152]{1,0:T(8,128)(2,1)S(1)} custom-call(bf16[640,1152]{1,0:T(8,128)(2,1)S(1)} %collective-permute-done.3.refs_0_, bf16[256,1152]{1,0:T(8,128)(2,1)S(1)} %collective-permute-done.8.refs_1_, bf16[128,1152]{1,0:T(8,128)(2,1)S(1)} %collective-permute-done.17.refs_2_, bf16[1152,1152]{1,0:T(8,128)(2,1)S(1)} %bitcast.135), custom_call_target="tpu_custom_call" | custom-call | flops 1000 | bytes 1000 | tf_op jit(solution)/shard_map/pallas_call | solution.py:188
  95.6 10.6 %shard_map.162 = (bf16[1024,1152]{1,0:T(8,128)(2,1)}, bf16[1024,1152]{1,0:T(8,128)(2,1)S(1)}, bf16[1024,1152]{1,0:T(8,128)(2,1)S(1)}) custom-call(f32[1024,1152]{1,0:T(8,128)S(1)} %shard_map.160.refs_0_, bf16[1024,1152]{1,0:T(8,128)(2,1)S(1)} %shard_map.161.refs_1_, bf16[1024,1152]{1,0:T(8,128)(2,1)S(1)} %bitcast.150, bf16[768,1152]{1,0:T(8,128)(2,1)S(1)} %bitcast.144, ...), custom_call_target="tpu_custom_call" | custom-call | flops 1000 | bytes 1000 | tf_op jit(solution)/shard_map/pallas_call | solution.py:148
  106.3 4.6 %shard_map.163 = bf16[1152,1152]{1,0:T(8,128)(2,1)S(1)} custom-call(bf16[640,1152]{1,0:T(8,128)(2,1)S(1)} %collective-permute-done.3.refs_0_, bf16[256,1152]{1,0:T(8,128)(2,1)S(1)} %collective-permute-done.8.refs_1_, bf16[128,1152]{1,0:T(8,128)(2,1)S(1)} %collective-permute-done.17.refs_2_, bf16[1024,1152]{1,0:T(8,128)(2,1)S(1)} %get-tuple-element.128.refs_3_.refs_0_), custom_call_target="tpu_custom_call" | custom-call | flops 1000 | bytes 1000 | tf_op jit(solution)/shard_map/pallas_call | solution.py:241
  112.5 2.1 %shard_map.165 = bf16[256,1152]{1,0:T(8,128)(2,1)S(1)} custom-call(bf16[1024,1152]{1,0:T(8,128)(2,1)S(1)} %get-tuple-element.128.refs_3_.refs_0_, bf16[1152,1152]{1,0:T(8,128)(2,1)S(1)} %bitcast.137), custom_call_target="tpu_custom_call" | custom-call | flops 1000 | bytes 1000 | tf_op jit(solution)/shard_map/pallas_call | solution.py:148
  115.6 1.5 collective-permute-start.27
  117.1 8.1 %shard_map.166 = bf16[2304,1152]{1,0:T(8,128)(2,1)S(1)} custom-call(bf16[1024,1152]{1,0:T(8,128)(2,1)S(1)} %bitcast.149, bf16[1024,1152]{1,0:T(8,128)(2,1)S(1)} %shard_map.161.refs_1_, bf16[1024,1152]{1,0:T(8,128)(2,1)S(1)} %get-tuple-element.139.refs_2_.refs_0_), custom_call_target="tpu_custom_call" | custom-call | flops 1000 | bytes 1000 | tf_op jit(solution)/shard_map/pallas_call | solution.py:241
  125.8 1.6 collective-permute-start.28
  127.5 3.2 %collective-permute-start.29 = (bf16[144,1152]{1,0:T(8,128)(2,1)S(1)}, bf16[144,1152]{1,0:T(8,128)(2,1)S(1)}, u32[]{:S(2)}, u32[]{:S(2)}) collective-permute-start(bf16[144,1152]{1,0:T(8,128)(2,1)S(1)} %add_convert_fusion.4), channel_id=1, source_target_pairs={{0,4},{1,5},{2,6},{3,7},{4,0},{5,1},{6,2},{7,3},{8,12},{9,13},{10,... | collective-permute-start | bytes 995336 | tf_op jit(solution)/shard_map/ppermute | solution.py:44
  132.8 2.4 %shard_map.168 = bf16[512,1152]{1,0:T(8,128)(2,1)S(1)} custom-call(bf16[1024,1152]{1,0:T(8,128)(2,1)S(1)} %get-tuple-element.128.refs_3_.refs_0_, bf16[1152,1152]{1,0:T(8,128)(2,1)S(1)} %bitcast.139), custom_call_target="tpu_custom_call" | custom-call | flops 1000 | bytes 1000 | tf_op jit(solution)/shard_map/pallas_call | solution.py:148
  135.2 11.0 %collective-permute-done.29 = bf16[144,1152]{1,0:T(8,128)(2,1)S(1)} collective-permute-done((bf16[144,1152]{1,0:T(8,128)(2,1)S(1)}, bf16[144,1152]{1,0:T(8,128)(2,1)S(1)}, u32[]{:S(2)}, u32[]{:S(2)}) %collective-permute-start.29) | collective-permute-done | bytes 331808 | tf_op jit(solution)/shard_map/ppermute | solution.py:44
  151.3 12.9 %collective-permute-done.32 = bf16[128,1152]{1,0:T(8,128)(2,1)S(1)} collective-permute-done((bf16[128,1152]{1,0:T(8,128)(2,1)S(1)}, bf16[128,1152]{1,0:T(8,128)(2,1)S(1)}, u32[]{:S(2)}, u32[]{:S(2)}) %collective-permute-start.32) | collective-permute-done | bytes 294944 | tf_op jit(solution)/shard_map/ppermute | solution.py:36
  164.4 1.8 collective-permute-start.37
  167.8 1.8 fusion.6
  169.6 7.4 %shard_map.169 = bf16[1024,1152]{1,0:T(8,128)(2,1)} custom-call(bf16[1024,1152]{1,0:T(8,128)(2,1)S(1)} %get-tuple-element.139.refs_2_.refs_0_, bf16[768,1152]{1,0:T(8,128)(2,1)S(1)} %bitcast.145, bf16[1536,1152]{1,0:T(8,128)(2,1)S(1)} %bitcast.142), custom_call_target="tpu_custom_call" | custom-call | flops 1000 | bytes 1000 | tf_op jit(solution)/shard_map/pallas_call | solution.py:148
  177.0 17.6 %collective-permute-done.37 = bf16[288,1152]{1,0:T(8,128)(2,1)S(1)} collective-permute-done((bf16[288,1152]{1,0:T(8,128)(2,1)S(1)}, bf16[288,1152]{1,0:T(8,128)(2,1)S(1)}, u32[]{:S(2)}, u32[]{:S(2)}) %collective-permute-start.37) | collective-permute-done | bytes 663584 | tf_op jit(solution)/shard_map/ppermute | solution.py:44
  194.6 3.1 %fusion.8 = (f32[1,288,1152]{2,1,0:T(8,128)}, f32[1,288,1152]{2,1,0:T(8,128)}, f32[1,288,1152]{2,1,0:T(8,128)}) fusion(bf16[288,1152]{1,0:T(8,128)(2,1)S(1)} %collective-permute-done.37, bf16[288,1152]{1,0:T(8,128)(2,1)S(1)} %collective-permute-done.36, bf16[288,1152]{1,0:T(8,128)(2,1)S(1)} %get-tuple-element.141, f32[1,288,1152]{2,1,0:T(8,128)S(1)} %copy-done.6, ...), kind=kLoop, calls=%fused_computation.61 | loop fusion | flops 5971968 | bytes 9953280 | tf_op jit(solution)/shard_map/broadcast_in_dim | solution.py:361
  197.9 1.4 copy-done.5
  (139 shorter events, 30.7 us)
Async XLA Ops:
  1.9 17.4 %collective-permute-start = (bf16[144,1152]{1,0:T(8,128)(2,1)S(1)}, bf16[144,1152]{1,0:T(8,128)(2,1)}, u32[]{:S(2)}, u32[]{:S(2)}) collective-permute-start(bf16[144,1152]{1,0:T(8,128)(2,1)S(1)} %bitcast_convert_fusion.1), channel_id=1, source_target_pairs={{0,16},{8,24},{16,0},{24,8},{1,17},{9,25},{17,1},{25,9},{2,18},{10... | collective-permute-start | bytes 995336 | tf_op jit(solution)/shard_map/ppermute | solution.py:36
  6.4 12.7 %collective-permute-start.2 = (bf16[96,1152]{1,0:T(8,128)(2,1)S(1)}, bf16[96,1152]{1,0:T(8,128)(2,1)S(1)}, u32[]{:S(2)}, u32[]{:S(2)}) collective-permute-start(bf16[96,1152]{1,0:T(8,128)(2,1)S(1)} %slice.20), channel_id=1, source_target_pairs={{0,4},{1,5},{2,6},{3,7},{4,0},{5,1},{6,2},{7,3},{8,12},{9,13},{10,... | collective-permute-start | bytes 663560 | tf_op jit(solution)/shard_map/ppermute | solution.py:44
  9.1 10.2 %collective-permute-start.1 = (bf16[96,1152]{1,0:T(8,128)(2,1)S(1)}, bf16[96,1152]{1,0:T(8,128)(2,1)S(1)}, u32[]{:S(2)}, u32[]{:S(2)}) collective-permute-start(bf16[96,1152]{1,0:T(8,128)(2,1)S(1)} %slice.20), channel_id=1, source_target_pairs={{0,2},{1,3},{2,0},{3,1},{4,6},{5,7},{6,4},{7,5},{8,10},{9,11},{10,... | collective-permute-start | bytes 663560 | tf_op jit(solution)/shard_map/ppermute | solution.py:44
  19.3 35.9 %collective-permute-start.3 = (bf16[640,1152]{1,0:T(8,128)(2,1)S(1)}, bf16[640,1152]{1,0:T(8,128)(2,1)S(1)}, u32[]{:S(2)}, u32[]{:S(2)}) collective-permute-start(bf16[640,1152]{1,0:T(8,128)(2,1)S(1)} %slice.22), channel_id=1, source_target_pairs={{0,16},{8,24},{16,0},{24,8},{1,17},{9,25},{17,1},{25,9},{2,18},{10... | collective-permute-start | bytes 4423688 | tf_op jit(solution)/shard_map/ppermute | solution.py:36
  19.8 35.5 %collective-permute-start.7 = (bf16[192,1152]{1,0:T(8,128)(2,1)S(1)}, bf16[192,1152]{1,0:T(8,128)(2,1)}, u32[]{:S(2)}, u32[]{:S(2)}) collective-permute-start(bf16[192,1152]{1,0:T(8,128)(2,1)S(1)} %slice.21), channel_id=1, source_target_pairs={{0,4},{1,5},{2,6},{3,7},{4,0},{5,1},{6,2},{7,3},{8,12},{9,13},{10,... | collective-permute-start | bytes 1327112 | tf_op jit(solution)/shard_map/ppermute | solution.py:44
  21.1 34.1 %collective-permute-start.6 = (bf16[192,1152]{1,0:T(8,128)(2,1)S(1)}, bf16[192,1152]{1,0:T(8,128)(2,1)}, u32[]{:S(2)}, u32[]{:S(2)}) collective-permute-start(bf16[192,1152]{1,0:T(8,128)(2,1)S(1)} %slice.21), channel_id=1, source_target_pairs={{0,2},{1,3},{2,0},{3,1},{4,6},{5,7},{6,4},{7,5},{8,10},{9,11},{10,... | collective-permute-start | bytes 1327112 | tf_op jit(solution)/shard_map/ppermute | solution.py:44
  23.6 31.6 %collective-permute-start.5 = (bf16[144,1152]{1,0:T(8,128)(2,1)}, bf16[144,1152]{1,0:T(8,128)(2,1)}, u32[]{:S(2)}, u32[]{:S(2)}) collective-permute-start(bf16[144,1152]{1,0:T(8,128)(2,1)} %collective-permute-done), channel_id=1, source_target_pairs={{0,4},{1,5},{2,6},{3,7},{4,0},{5,1},{6,2},{7,3},{8,12},{9,13},{10,... | collective-permute-start | bytes 995336 | tf_op jit(solution)/shard_map/ppermute | solution.py:44
  24.2 31.1 %collective-permute-start.4 = (bf16[144,1152]{1,0:T(8,128)(2,1)}, bf16[144,1152]{1,0:T(8,128)(2,1)}, u32[]{:S(2)}, u32[]{:S(2)}) collective-permute-start(bf16[144,1152]{1,0:T(8,128)(2,1)} %collective-permute-done), channel_id=1, source_target_pairs={{0,2},{1,3},{2,0},{3,1},{4,6},{5,7},{6,4},{7,5},{8,10},{9,11},{10,... | collective-permute-start | bytes 995336 | tf_op jit(solution)/shard_map/ppermute | solution.py:44
  55.2 8.9 %collective-permute-start.15 = (bf16[96,1152]{1,0:T(8,128)(2,1)}, bf16[96,1152]{1,0:T(8,128)(2,1)S(1)}, u32[]{:S(2)}, u32[]{:S(2)}) collective-permute-start(bf16[96,1152]{1,0:T(8,128)(2,1)} %copy-done.14), channel_id=1, source_target_pairs={{0,2},{1,3},{2,0},{3,1},{4,6},{5,7},{6,4},{7,5},{8,10},{9,11},{10,... | collective-permute-start | bytes 663560 | tf_op jit(solution)/shard_map/ppermute | solution.py:44
  55.6 4.0 %collective-permute-start.11 = (bf16[96,1152]{1,0:T(8,128)(2,1)}, bf16[96,1152]{1,0:T(8,128)(2,1)S(1)}, u32[]{:S(2)}, u32[]{:S(2)}) collective-permute-start(bf16[96,1152]{1,0:T(8,128)(2,1)} %copy-done.14), channel_id=1, source_target_pairs={{0,1},{1,0},{2,3},{3,2},{4,5},{5,4},{6,7},{7,6},{8,9},{9,8},{10,11... | collective-permute-start | bytes 663560 | tf_op jit(solution)/shard_map/ppermute | solution.py:52
  56.1 4.1 %collective-permute-start.12 = (bf16[192,1152]{1,0:T(8,128)(2,1)S(1)}, bf16[192,1152]{1,0:T(8,128)(2,1)S(1)}, u32[]{:S(2)}, u32[]{:S(2)}) collective-permute-start(bf16[192,1152]{1,0:T(8,128)(2,1)S(1)} %slice.21), channel_id=1, source_target_pairs={{0,1},{1,0},{2,3},{3,2},{4,5},{5,4},{6,7},{7,6},{8,9},{9,8},{10,11... | collective-permute-start | bytes 1327112 | tf_op jit(solution)/shard_map/ppermute | solution.py:52
  57.6 13.3 %collective-permute-start.16 = (bf16[192,1152]{1,0:T(8,128)(2,1)}, bf16[192,1152]{1,0:T(8,128)(2,1)S(1)}, u32[]{:S(2)}, u32[]{:S(2)}) collective-permute-start(bf16[192,1152]{1,0:T(8,128)(2,1)} %collective-permute-done.7), channel_id=1, source_target_pairs={{0,2},{1,3},{2,0},{3,1},{4,6},{5,7},{6,4},{7,5},{8,10},{9,11},{10,... | collective-permute-start | bytes 1327112 | tf_op jit(solution)/shard_map/ppermute | solution.py:44
  59.4 4.6 %collective-permute-start.14 = (bf16[192,1152]{1,0:T(8,128)(2,1)}, bf16[192,1152]{1,0:T(8,128)(2,1)S(1)}, u32[]{:S(2)}, u32[]{:S(2)}) collective-permute-start(bf16[192,1152]{1,0:T(8,128)(2,1)} %collective-permute-done.7), channel_id=1, source_target_pairs={{0,1},{1,0},{2,3},{3,2},{4,5},{5,4},{6,7},{7,6},{8,9},{9,8},{10,11... | collective-permute-start | bytes 1327112 | tf_op jit(solution)/shard_map/ppermute | solution.py:52
  60.2 15.3 %collective-permute-start.8 = (bf16[256,1152]{1,0:T(8,128)(2,1)S(1)}, bf16[256,1152]{1,0:T(8,128)(2,1)S(1)}, u32[]{:S(2)}, u32[]{:S(2)}) collective-permute-start(bf16[256,1152]{1,0:T(8,128)(2,1)S(1)} %copy-done.12), channel_id=1, source_target_pairs={{0,16},{8,24},{16,0},{24,8},{1,17},{9,25},{17,1},{25,9},{2,18},{10... | collective-permute-start | bytes 1769480 | tf_op jit(solution)/shard_map/ppermute | solution.py:36
  75.5 8.1 %collective-permute-start.21 = (bf16[144,1152]{1,0:T(8,128)(2,1)}, bf16[144,1152]{1,0:T(8,128)(2,1)S(1)}, u32[]{:S(2)}, u32[]{:S(2)}) collective-permute-start(bf16[144,1152]{1,0:T(8,128)(2,1)} %collective-permute-done.5), channel_id=1, source_target_pairs={{0,1},{1,0},{2,3},{3,2},{4,5},{5,4},{6,7},{7,6},{8,9},{9,8},{10,11... | collective-permute-start | bytes 995336 | tf_op jit(solution)/shard_map/ppermute | solution.py:52
  75.5 14.8 %collective-permute-start.18 = (bf16[144,1152]{1,0:T(8,128)(2,1)}, bf16[144,1152]{1,0:T(8,128)(2,1)S(1)}, u32[]{:S(2)}, u32[]{:S(2)}) collective-permute-start(bf16[144,1152]{1,0:T(8,128)(2,1)} %collective-permute-done.5), channel_id=1, source_target_pairs={{0,2},{1,3},{2,0},{3,1},{4,6},{5,7},{6,4},{7,5},{8,10},{9,11},{10,... | collective-permute-start | bytes 995336 | tf_op jit(solution)/shard_map/ppermute | solution.py:44
  76.1 4.6 %collective-permute-start.19 = (bf16[144,1152]{1,0:T(8,128)(2,1)}, bf16[144,1152]{1,0:T(8,128)(2,1)S(1)}, u32[]{:S(2)}, u32[]{:S(2)}) collective-permute-start(bf16[144,1152]{1,0:T(8,128)(2,1)} %collective-permute-done), channel_id=1, source_target_pairs={{0,1},{1,0},{2,3},{3,2},{4,5},{5,4},{6,7},{7,6},{8,9},{9,8},{10,11... | collective-permute-start | bytes 995336 | tf_op jit(solution)/shard_map/ppermute | solution.py:52
  77.9 5.8 %collective-permute-start.23 = (bf16[192,1152]{1,0:T(8,128)(2,1)S(1)}, bf16[192,1152]{1,0:T(8,128)(2,1)S(1)}, u32[]{:S(2)}, u32[]{:S(2)}) collective-permute-start(bf16[192,1152]{1,0:T(8,128)(2,1)S(1)} %collective-permute-done.16), channel_id=1, source_target_pairs={{0,1},{1,0},{2,3},{3,2},{4,5},{5,4},{6,7},{7,6},{8,9},{9,8},{10,11... | collective-permute-start | bytes 1327112 | tf_op jit(solution)/shard_map/ppermute | solution.py:52
  79.1 11.2 %collective-permute-start.17 = (bf16[128,1152]{1,0:T(8,128)(2,1)S(1)}, bf16[128,1152]{1,0:T(8,128)(2,1)S(1)}, u32[]{:S(2)}, u32[]{:S(2)}) collective-permute-start(bf16[128,1152]{1,0:T(8,128)(2,1)S(1)} %copy-done.13), channel_id=1, source_target_pairs={{0,16},{8,24},{16,0},{24,8},{1,17},{9,25},{17,1},{25,9},{2,18},{10... | collective-permute-start | bytes 884744 | tf_op jit(solution)/shard_map/ppermute | solution.py:36
  111.2 3.4 %collective-permute-start.25 = (bf16[4,144,1152]{2,1,0:T(8,128)(2,1)S(1)}, bf16[4,144,1152]{2,1,0:T(8,128)(2,1)S(1)}, u32[]{:S(2)}, u32[]{:S(2)}) collective-permute-start(bf16[4,144,1152]{2,1,0:T(8,128)(2,1)S(1)} %get-tuple-element.154), channel_id=1, source_target_pairs={{0,1},{1,0},{2,3},{3,2},{4,5},{5,4},{6,7},{7,6},{8,9},{9,8},{10,11... | collective-permute-start | bytes 3981320 | tf_op jit(solution)/shard_map/ppermute | solution.py:52
  114.6 11.1 %collective-permute-start.26 = (bf16[128,1152]{1,0:T(8,128)(2,1)S(1)}, bf16[128,1152]{1,0:T(8,128)(2,1)S(1)}, u32[]{:S(2)}, u32[]{:S(2)}) collective-permute-start(bf16[128,1152]{1,0:T(8,128)(2,1)S(1)} %shard_map.164), channel_id=1, source_target_pairs={{0,16},{8,24},{16,0},{24,8},{1,17},{9,25},{17,1},{25,9},{2,18},{10... | collective-permute-start | bytes 884744 | tf_op jit(solution)/shard_map/ppermute | solution.py:36
  115.6 10.1 %collective-permute-start.27 = (bf16[144,1152]{1,0:T(8,128)(2,1)S(1)}, bf16[144,1152]{1,0:T(8,128)(2,1)S(1)}, u32[]{:S(2)}, u32[]{:S(2)}) collective-permute-start(bf16[144,1152]{1,0:T(8,128)(2,1)S(1)} %get-tuple-element.156), channel_id=1, source_target_pairs={{0,2},{1,3},{2,0},{3,1},{4,6},{5,7},{6,4},{7,5},{8,10},{9,11},{10,... | collective-permute-start | bytes 995336 | tf_op jit(solution)/shard_map/ppermute | solution.py:44
  125.7 21.4 %collective-permute-start.31 = (bf16[4,288,1152]{2,1,0:T(8,128)(2,1)S(1)}, bf16[4,288,1152]{2,1,0:T(8,128)(2,1)S(1)}, u32[]{:S(2)}, u32[]{:S(2)}) collective-permute-start(bf16[4,288,1152]{2,1,0:T(8,128)(2,1)S(1)} %get-tuple-element.127), channel_id=1, source_target_pairs={{0,1},{1,0},{2,3},{3,2},{4,5},{5,4},{6,7},{7,6},{8,9},{9,8},{10,11... | collective-permute-start | bytes 7962632 | tf_op jit(solution)/shard_map/ppermute | solution.py:52
  125.8 21.3 %collective-permute-start.28 = (bf16[256,1152]{1,0:T(8,128)(2,1)S(1)}, bf16[256,1152]{1,0:T(8,128)(2,1)S(1)}, u32[]{:S(2)}, u32[]{:S(2)}) collective-permute-start(bf16[256,1152]{1,0:T(8,128)(2,1)S(1)} %shard_map.165), channel_id=1, source_target_pairs={{0,16},{8,24},{16,0},{24,8},{1,17},{9,25},{17,1},{25,9},{2,18},{10... | collective-permute-start | bytes 1769480 | tf_op jit(solution)/shard_map/ppermute | solution.py:36
  127.5 18.6 %collective-permute-start.29 = (bf16[144,1152]{1,0:T(8,128)(2,1)S(1)}, bf16[144,1152]{1,0:T(8,128)(2,1)S(1)}, u32[]{:S(2)}, u32[]{:S(2)}) collective-permute-start(bf16[144,1152]{1,0:T(8,128)(2,1)S(1)} %add_convert_fusion.4), channel_id=1, source_target_pairs={{0,4},{1,5},{2,6},{3,7},{4,0},{5,1},{6,2},{7,3},{8,12},{9,13},{10,... | collective-permute-start | bytes 995336 | tf_op jit(solution)/shard_map/ppermute | solution.py:44
  130.7 16.4 %collective-permute-start.30 = (bf16[144,1152]{1,0:T(8,128)(2,1)S(1)}, bf16[144,1152]{1,0:T(8,128)(2,1)S(1)}, u32[]{:S(2)}, u32[]{:S(2)}) collective-permute-start(bf16[144,1152]{1,0:T(8,128)(2,1)S(1)} %get-tuple-element.123), channel_id=1, source_target_pairs={{0,2},{1,3},{2,0},{3,1},{4,6},{5,7},{6,4},{7,5},{8,10},{9,11},{10,... | collective-permute-start | bytes 995336 | tf_op jit(solution)/shard_map/ppermute | solution.py:44
  148.1 16.2 %collective-permute-start.34 = (bf16[288,1152]{1,0:T(8,128)(2,1)S(1)}, bf16[288,1152]{1,0:T(8,128)(2,1)S(1)}, u32[]{:S(2)}, u32[]{:S(2)}) collective-permute-start(bf16[288,1152]{1,0:T(8,128)(2,1)S(1)} %get-tuple-element.150), channel_id=1, source_target_pairs={{0,2},{1,3},{2,0},{3,1},{4,6},{5,7},{6,4},{7,5},{8,10},{9,11},{10,... | collective-permute-start | bytes 1990664 | tf_op jit(solution)/shard_map/ppermute | solution.py:44
  149.0 15.2 %collective-permute-start.33 = (bf16[144,1152]{1,0:T(8,128)(2,1)S(1)}, bf16[144,1152]{1,0:T(8,128)(2,1)S(1)}, u32[]{:S(2)}, u32[]{:S(2)}) collective-permute-start(bf16[144,1152]{1,0:T(8,128)(2,1)S(1)} %add_convert_fusion.3), channel_id=1, source_target_pairs={{0,16},{8,24},{16,0},{24,8},{1,17},{9,25},{17,1},{25,9},{2,18},{10... | collective-permute-start | bytes 995336 | tf_op jit(solution)/shard_map/ppermute | solution.py:36
  149.9 14.3 %collective-permute-start.32 = (bf16[128,1152]{1,0:T(8,128)(2,1)S(1)}, bf16[128,1152]{1,0:T(8,128)(2,1)S(1)}, u32[]{:S(2)}, u32[]{:S(2)}) collective-permute-start(bf16[128,1152]{1,0:T(8,128)(2,1)S(1)} %shard_map.167), channel_id=1, source_target_pairs={{0,16},{8,24},{16,0},{24,8},{1,17},{9,25},{17,1},{25,9},{2,18},{10... | collective-permute-start | bytes 884744 | tf_op jit(solution)/shard_map/ppermute | solution.py:36
  164.4 30.2 %collective-permute-start.37 = (bf16[288,1152]{1,0:T(8,128)(2,1)S(1)}, bf16[288,1152]{1,0:T(8,128)(2,1)S(1)}, u32[]{:S(2)}, u32[]{:S(2)}) collective-permute-start(bf16[288,1152]{1,0:T(8,128)(2,1)S(1)} %add_convert_fusion.2), channel_id=1, source_target_pairs={{0,4},{1,5},{2,6},{3,7},{4,0},{5,1},{6,2},{7,3},{8,12},{9,13},{10,... | collective-permute-start | bytes 1990664 | tf_op jit(solution)/shard_map/ppermute | solution.py:44
  166.2 28.4 %collective-permute-start.36 = (bf16[288,1152]{1,0:T(8,128)(2,1)S(1)}, bf16[288,1152]{1,0:T(8,128)(2,1)S(1)}, u32[]{:S(2)}, u32[]{:S(2)}) collective-permute-start(bf16[288,1152]{1,0:T(8,128)(2,1)S(1)} %get-tuple-element.142), channel_id=1, source_target_pairs={{0,2},{1,3},{2,0},{3,1},{4,6},{5,7},{6,4},{7,5},{8,10},{9,11},{10,... | collective-permute-start | bytes 1990664 | tf_op jit(solution)/shard_map/ppermute | solution.py:44
  167.0 30.7 %collective-permute-start.35 = (bf16[512,1152]{1,0:T(8,128)(2,1)S(1)}, bf16[512,1152]{1,0:T(8,128)(2,1)S(1)}, u32[]{:S(2)}, u32[]{:S(2)}) collective-permute-start(bf16[512,1152]{1,0:T(8,128)(2,1)S(1)} %shard_map.168), channel_id=1, source_target_pairs={{0,16},{8,24},{16,0},{24,8},{1,17},{9,25},{17,1},{25,9},{2,18},{10... | collective-permute-start | bytes 3538952 | tf_op jit(solution)/shard_map/ppermute | solution.py:36
  (24 other events, 237.6 us)

commit v4 on v3

--- a/solution.py
+++ b/solution.py
@@ -349,11 +349,12 @@
     enc3 = to_partner(enc3)
     skip_on = scatter_on(skip_blocks, skip_near)
     skip_one = chip_flip(skip_blocks[1], 1)
-    skip_sum = plus(skip_blocks[0], skip_one, *skip_on)
     (dec_grad,) = row_call(project_back, [pre_grad], skip_w, skip_parts, 1, 256, 20, half=0)
     enc_grad = jnp.zeros_like(enc_rows)
     for at, part in zip(cuts, (enc0, enc1, enc2, enc3)):
         enc_grad = lax.dynamic_update_slice(enc_grad, part, (at, 0))
+    enc_grad, skip_one = together((enc_grad, skip_one))
+    skip_sum = plus(skip_blocks[0], skip_one, *skip_on)
 
     new_proj = adam_update(w_proj[0], m_proj[0], v_proj[0], proj_sum)
     new_skip = adam_update(w_skip[0], m_skip[0], v_skip[0], skip_sum)

time: 200 us -> 199 us (level)
    ppermute x9, waiting for transfers between devices: 17.5 us -> 30.8 us  [to_partner(): return lax.ppermute(value, 'section', pairs)]
    ppermute x15, waiting for transfers between devices: 71.7 us -> 58.8 us  [to_chips(): lax.ppermute(value, 'dp', [(2 * a + c, 2 * b + c) for a, b in pairs for c...]
  transfers between devices with their start and end apart: 38 -> 38, of which waited for: 13 -> 15; matrix products, arithmetic and copies ran while one was open for 9% -> 8% of each run, Pallas kernels for 14% -> 14%
where the time goes in v4:
time: 199 us; the launch traced here: 198 us
  waiting for transfers between devices  92.9 us (47%)
  Pallas kernels  47.5 us (24%)
  starting transfers between devices  35.6 us (18%)
  local copies, waits for them, and re-layouts  12 us (6%)
  other arithmetic  8.93 us (4%)
    ppermute x15, waiting for transfers between devices, to_chips(): lax.ppermute(value, 'dp', [(2 * a + c, 2 * b + c) for a, b in pairs for c...  58.8 us
    pallas_call x7, Pallas kernels, row_call(): pl.pallas_call(kernel, grid=(rows // tile,), in_specs=[taken] * len(row_a...  31.2 us
    ppermute x9, waiting for transfers between devices, to_partner(): return lax.ppermute(value, 'section', pairs)  30.8 us
    ppermute x15, starting transfers between devices, to_chips(): lax.ppermute(value, 'dp', [(2 * a + c, 2 * b + c) for a, b in pairs for c...  20.9 us
    pallas_call x2, Pallas kernels, weight_grad(): pl.pallas_call(kernel, grid=(len(lefts) * steps,), in_specs=[spec(n, part...  12.8 us
    ppermute x9, starting transfers between devices, to_partner(): return lax.ppermute(value, 'section', pairs)  11.7 us
    dynamic_update_slice x12, local copies, waits for them, and re-layouts, assemble(): lax.dynamic_update_slice(whole, piece[None, None], (chip ^ k, core, 0, 0))  5.44 us
    broadcast_in_dim x2, other arithmetic, body(): return streams + tuple((value[None] for value in new_proj + new_skip))  4.83 us
  transfers between devices with their start and end apart: 38, of which 15 were waited for; matrix products, arithmetic and copies ran while one was open for 8% of the time, Pallas kernels for 14%

profile of v4, /device:TPU:0, one launch (start us, length us, event | category | flops | bytes accessed | tf_op | source)
XLA Modules:
  0.0 198.2 jit_solution(6942589080913138156)
XLA Ops:
  1.9 3.0 %collective-permute-start = (bf16[144,1152]{1,0:T(8,128)(2,1)S(1)}, bf16[144,1152]{1,0:T(8,128)(2,1)}, u32[]{:S(2)}, u32[]{:S(2)}) collective-permute-start(bf16[144,1152]{1,0:T(8,128)(2,1)S(1)} %bitcast_convert_fusion.1), channel_id=1, source_target_pairs={{0,16},{8,24},{16,0},{24,8},{1,17},{9,25},{17,1},{25,9},{2,18},{10... | collective-permute-start | bytes 995336 | tf_op jit(solution)/shard_map/ppermute | solution.py:36
  6.4 2.7 %collective-permute-start.2 = (bf16[96,1152]{1,0:T(8,128)(2,1)S(1)}, bf16[96,1152]{1,0:T(8,128)(2,1)S(1)}, u32[]{:S(2)}, u32[]{:S(2)}) collective-permute-start(bf16[96,1152]{1,0:T(8,128)(2,1)S(1)} %slice.20), channel_id=1, source_target_pairs={{0,4},{1,5},{2,6},{3,7},{4,0},{5,1},{6,2},{7,3},{8,12},{9,13},{10,... | collective-permute-start | bytes 663560 | tf_op jit(solution)/shard_map/ppermute | solution.py:44
  9.1 1.6 collective-permute-start.1
  10.8 8.3 %collective-permute-done.2 = bf16[96,1152]{1,0:T(8,128)(2,1)S(1)} collective-permute-done((bf16[96,1152]{1,0:T(8,128)(2,1)S(1)}, bf16[96,1152]{1,0:T(8,128)(2,1)S(1)}, u32[]{:S(2)}, u32[]{:S(2)}) %collective-permute-start.2) | collective-permute-done | bytes 221216 | tf_op jit(solution)/shard_map/ppermute | solution.py:44
  21.1 2.5 %collective-permute-start.6 = (bf16[192,1152]{1,0:T(8,128)(2,1)S(1)}, bf16[192,1152]{1,0:T(8,128)(2,1)}, u32[]{:S(2)}, u32[]{:S(2)}) collective-permute-start(bf16[192,1152]{1,0:T(8,128)(2,1)S(1)} %slice.21), channel_id=1, source_target_pairs={{0,2},{1,3},{2,0},{3,1},{4,6},{5,7},{6,4},{7,5},{8,10},{9,11},{10,... | collective-permute-start | bytes 1327112 | tf_op jit(solution)/shard_map/ppermute | solution.py:44
  24.7 1.7 slice.24
  26.4 1.9 slice.23
  28.3 26.9 %collective-permute-done.5 = bf16[144,1152]{1,0:T(8,128)(2,1)} collective-permute-done((bf16[144,1152]{1,0:T(8,128)(2,1)}, bf16[144,1152]{1,0:T(8,128)(2,1)}, u32[]{:S(2)}, u32[]{:S(2)}) %collective-permute-start.5) | collective-permute-done | bytes 331808 | tf_op jit(solution)/shard_map/ppermute | solution.py:44
  57.6 1.8 collective-permute-start.16
  60.2 1.6 collective-permute-start.8
  64.2 6.8 %collective-permute-done.16 = bf16[192,1152]{1,0:T(8,128)(2,1)S(1)} collective-permute-done((bf16[192,1152]{1,0:T(8,128)(2,1)}, bf16[192,1152]{1,0:T(8,128)(2,1)S(1)}, u32[]{:S(2)}, u32[]{:S(2)}) %collective-permute-start.16) | collective-permute-done | bytes 442400 | tf_op jit(solution)/shard_map/ppermute | solution.py:44
  70.9 4.6 %collective-permute-done.8.refs_1_ = bf16[256,1152]{1,0:T(8,128)(2,1)S(1)} collective-permute-done((bf16[256,1152]{1,0:T(8,128)(2,1)S(1)}, bf16[256,1152]{1,0:T(8,128)(2,1)S(1)}, u32[]{:S(2)}, u32[]{:S(2)}) %collective-permute-start.8) | collective-permute-done | bytes 589856 | tf_op jit(solution)/shard_map/ppermute | solution.py:36
  79.1 1.5 collective-permute-start.17
  83.8 6.5 %shard_map.160.refs_0_ = f32[1024,1152]{1,0:T(8,128)S(1)} custom-call(bf16[1024,1152]{1,0:T(8,128)(2,1)S(1)} %bitcast.148, bf16[768,1152]{1,0:T(8,128)(2,1)S(1)} %bitcast.143, bf16[1536,1152]{1,0:T(8,128)(2,1)S(1)} %bitcast.140), custom_call_target="tpu_custom_call" | custom-call | flops 1000 | bytes 1000 | tf_op jit(solution)/shard_map/pallas_call | solution.py:148
  92.1 3.5 %shard_map.161.refs_1_ = bf16[1024,1152]{1,0:T(8,128)(2,1)S(1)} custom-call(bf16[640,1152]{1,0:T(8,128)(2,1)S(1)} %collective-permute-done.3.refs_0_, bf16[256,1152]{1,0:T(8,128)(2,1)S(1)} %collective-permute-done.8.refs_1_, bf16[128,1152]{1,0:T(8,128)(2,1)S(1)} %collective-permute-done.17.refs_2_, bf16[1152,1152]{1,0:T(8,128)(2,1)S(1)} %bitcast.135), custom_call_target="tpu_custom_call" | custom-call | flops 1000 | bytes 1000 | tf_op jit(solution)/shard_map/pallas_call | solution.py:188
  95.6 10.6 %shard_map.162 = (bf16[1024,1152]{1,0:T(8,128)(2,1)}, bf16[1024,1152]{1,0:T(8,128)(2,1)S(1)}, bf16[1024,1152]{1,0:T(8,128)(2,1)S(1)}) custom-call(f32[1024,1152]{1,0:T(8,128)S(1)} %shard_map.160.refs_0_, bf16[1024,1152]{1,0:T(8,128)(2,1)S(1)} %shard_map.161.refs_1_, bf16[1024,1152]{1,0:T(8,128)(2,1)S(1)} %bitcast.150, bf16[768,1152]{1,0:T(8,128)(2,1)S(1)} %bitcast.144, ...), custom_call_target="tpu_custom_call" | custom-call | flops 1000 | bytes 1000 | tf_op jit(solution)/shard_map/pallas_call | solution.py:148
  106.3 4.6 %shard_map.163 = bf16[1152,1152]{1,0:T(8,128)(2,1)S(1)} custom-call(bf16[640,1152]{1,0:T(8,128)(2,1)S(1)} %collective-permute-done.3.refs_0_, bf16[256,1152]{1,0:T(8,128)(2,1)S(1)} %collective-permute-done.8.refs_1_, bf16[128,1152]{1,0:T(8,128)(2,1)S(1)} %collective-permute-done.17.refs_2_, bf16[1024,1152]{1,0:T(8,128)(2,1)S(1)} %get-tuple-element.130.refs_3_.refs_0_), custom_call_target="tpu_custom_call" | custom-call | flops 1000 | bytes 1000 | tf_op jit(solution)/shard_map/pallas_call | solution.py:241
  112.5 2.1 %shard_map.165 = bf16[256,1152]{1,0:T(8,128)(2,1)S(1)} custom-call(bf16[1024,1152]{1,0:T(8,128)(2,1)S(1)} %get-tuple-element.130.refs_3_.refs_0_, bf16[1152,1152]{1,0:T(8,128)(2,1)S(1)} %bitcast.137), custom_call_target="tpu_custom_call" | custom-call | flops 1000 | bytes 1000 | tf_op jit(solution)/shard_map/pallas_call | solution.py:148
  115.6 1.5 collective-permute-start.27
  117.1 8.1 %shard_map.166 = bf16[2304,1152]{1,0:T(8,128)(2,1)S(1)} custom-call(bf16[1024,1152]{1,0:T(8,128)(2,1)S(1)} %bitcast.149, bf16[1024,1152]{1,0:T(8,128)(2,1)S(1)} %shard_map.161.refs_1_, bf16[1024,1152]{1,0:T(8,128)(2,1)S(1)} %get-tuple-element.143.refs_2_.refs_0_), custom_call_target="tpu_custom_call" | custom-call | flops 1000 | bytes 1000 | tf_op jit(solution)/shard_map/pallas_call | solution.py:241
  125.8 1.6 collective-permute-start.28
  127.5 3.2 %collective-permute-start.29 = (bf16[144,1152]{1,0:T(8,128)(2,1)S(1)}, bf16[144,1152]{1,0:T(8,128)(2,1)S(1)}, u32[]{:S(2)}, u32[]{:S(2)}) collective-permute-start(bf16[144,1152]{1,0:T(8,128)(2,1)S(1)} %add_convert_fusion.4), channel_id=1, source_target_pairs={{0,4},{1,5},{2,6},{3,7},{4,0},{5,1},{6,2},{7,3},{8,12},{9,13},{10,... | collective-permute-start | bytes 995336 | tf_op jit(solution)/shard_map/ppermute | solution.py:44
  132.8 2.4 %shard_map.168 = bf16[512,1152]{1,0:T(8,128)(2,1)S(1)} custom-call(bf16[1024,1152]{1,0:T(8,128)(2,1)S(1)} %get-tuple-element.130.refs_3_.refs_0_, bf16[1152,1152]{1,0:T(8,128)(2,1)S(1)} %bitcast.139), custom_call_target="tpu_custom_call" | custom-call | flops 1000 | bytes 1000 | tf_op jit(solution)/shard_map/pallas_call | solution.py:148
  135.2 11.0 %collective-permute-done.29 = bf16[144,1152]{1,0:T(8,128)(2,1)S(1)} collective-permute-done((bf16[144,1152]{1,0:T(8,128)(2,1)S(1)}, bf16[144,1152]{1,0:T(8,128)(2,1)S(1)}, u32[]{:S(2)}, u32[]{:S(2)}) %collective-permute-start.29) | collective-permute-done | bytes 331808 | tf_op jit(solution)/shard_map/ppermute | solution.py:44
  151.3 12.9 %collective-permute-done.32 = bf16[128,1152]{1,0:T(8,128)(2,1)S(1)} collective-permute-done((bf16[128,1152]{1,0:T(8,128)(2,1)S(1)}, bf16[128,1152]{1,0:T(8,128)(2,1)S(1)}, u32[]{:S(2)}, u32[]{:S(2)}) %collective-permute-start.32) | collective-permute-done | bytes 294944 | tf_op jit(solution)/shard_map/ppermute | solution.py:36
  165.2 1.8 collective-permute-start.37
  167.8 1.8 fusion.6
  169.6 7.3 %shard_map.169 = bf16[1024,1152]{1,0:T(8,128)(2,1)} custom-call(bf16[1024,1152]{1,0:T(8,128)(2,1)S(1)} %get-tuple-element.143.refs_2_.refs_0_, bf16[768,1152]{1,0:T(8,128)(2,1)S(1)} %bitcast.145, bf16[1536,1152]{1,0:T(8,128)(2,1)S(1)} %bitcast.142), custom_call_target="tpu_custom_call" | custom-call | flops 1000 | bytes 1000 | tf_op jit(solution)/shard_map/pallas_call | solution.py:148
  177.0 13.3 %collective-permute-done.35 = bf16[512,1152]{1,0:T(8,128)(2,1)S(1)} collective-permute-done((bf16[512,1152]{1,0:T(8,128)(2,1)S(1)}, bf16[512,1152]{1,0:T(8,128)(2,1)S(1)}, u32[]{:S(2)}, u32[]{:S(2)}) %collective-permute-start.35) | collective-permute-done | bytes 1179680 | tf_op jit(solution)/shard_map/ppermute | solution.py:36
  190.5 3.0 %collective-permute-done.36 = bf16[288,1152]{1,0:T(8,128)(2,1)S(1)} collective-permute-done((bf16[288,1152]{1,0:T(8,128)(2,1)S(1)}, bf16[288,1152]{1,0:T(8,128)(2,1)S(1)}, u32[]{:S(2)}, u32[]{:S(2)}) %collective-permute-start.36) | collective-permute-done | bytes 663584 | tf_op jit(solution)/shard_map/ppermute | solution.py:44
  193.5 1.6 collective-permute-done.37
  195.1 3.1 %fusion.8 = (f32[1,288,1152]{2,1,0:T(8,128)}, f32[1,288,1152]{2,1,0:T(8,128)}, f32[1,288,1152]{2,1,0:T(8,128)}) fusion(bf16[288,1152]{1,0:T(8,128)(2,1)S(1)} %collective-permute-done.37, bf16[288,1152]{1,0:T(8,128)(2,1)S(1)} %collective-permute-done.36, bf16[288,1152]{1,0:T(8,128)(2,1)S(1)} %get-tuple-element.145, f32[1,288,1152]{2,1,0:T(8,128)S(1)} %copy-done.6, ...), kind=kLoop, calls=%fused_computation.61 | loop fusion | flops 5971968 | bytes 9953280 | tf_op jit(solution)/shard_map/broadcast_in_dim | solution.py:362
  (139 shorter events, 32.1 us)
Async XLA Ops:
  1.9 17.4 %collective-permute-start = (bf16[144,1152]{1,0:T(8,128)(2,1)S(1)}, bf16[144,1152]{1,0:T(8,128)(2,1)}, u32[]{:S(2)}, u32[]{:S(2)}) collective-permute-start(bf16[144,1152]{1,0:T(8,128)(2,1)S(1)} %bitcast_convert_fusion.1), channel_id=1, source_target_pairs={{0,16},{8,24},{16,0},{24,8},{1,17},{9,25},{17,1},{25,9},{2,18},{10... | collective-permute-start | bytes 995336 | tf_op jit(solution)/shard_map/ppermute | solution.py:36
  6.4 12.7 %collective-permute-start.2 = (bf16[96,1152]{1,0:T(8,128)(2,1)S(1)}, bf16[96,1152]{1,0:T(8,128)(2,1)S(1)}, u32[]{:S(2)}, u32[]{:S(2)}) collective-permute-start(bf16[96,1152]{1,0:T(8,128)(2,1)S(1)} %slice.20), channel_id=1, source_target_pairs={{0,4},{1,5},{2,6},{3,7},{4,0},{5,1},{6,2},{7,3},{8,12},{9,13},{10,... | collective-permute-start | bytes 663560 | tf_op jit(solution)/shard_map/ppermute | solution.py:44
  9.1 10.2 %collective-permute-start.1 = (bf16[96,1152]{1,0:T(8,128)(2,1)S(1)}, bf16[96,1152]{1,0:T(8,128)(2,1)S(1)}, u32[]{:S(2)}, u32[]{:S(2)}) collective-permute-start(bf16[96,1152]{1,0:T(8,128)(2,1)S(1)} %slice.20), channel_id=1, source_target_pairs={{0,2},{1,3},{2,0},{3,1},{4,6},{5,7},{6,4},{7,5},{8,10},{9,11},{10,... | collective-permute-start | bytes 663560 | tf_op jit(solution)/shard_map/ppermute | solution.py:44
  19.3 35.9 %collective-permute-start.3 = (bf16[640,1152]{1,0:T(8,128)(2,1)S(1)}, bf16[640,1152]{1,0:T(8,128)(2,1)S(1)}, u32[]{:S(2)}, u32[]{:S(2)}) collective-permute-start(bf16[640,1152]{1,0:T(8,128)(2,1)S(1)} %slice.22), channel_id=1, source_target_pairs={{0,16},{8,24},{16,0},{24,8},{1,17},{9,25},{17,1},{25,9},{2,18},{10... | collective-permute-start | bytes 4423688 | tf_op jit(solution)/shard_map/ppermute | solution.py:36
  19.8 35.5 %collective-permute-start.7 = (bf16[192,1152]{1,0:T(8,128)(2,1)S(1)}, bf16[192,1152]{1,0:T(8,128)(2,1)}, u32[]{:S(2)}, u32[]{:S(2)}) collective-permute-start(bf16[192,1152]{1,0:T(8,128)(2,1)S(1)} %slice.21), channel_id=1, source_target_pairs={{0,4},{1,5},{2,6},{3,7},{4,0},{5,1},{6,2},{7,3},{8,12},{9,13},{10,... | collective-permute-start | bytes 1327112 | tf_op jit(solution)/shard_map/ppermute | solution.py:44
  21.1 34.1 %collective-permute-start.6 = (bf16[192,1152]{1,0:T(8,128)(2,1)S(1)}, bf16[192,1152]{1,0:T(8,128)(2,1)}, u32[]{:S(2)}, u32[]{:S(2)}) collective-permute-start(bf16[192,1152]{1,0:T(8,128)(2,1)S(1)} %slice.21), channel_id=1, source_target_pairs={{0,2},{1,3},{2,0},{3,1},{4,6},{5,7},{6,4},{7,5},{8,10},{9,11},{10,... | collective-permute-start | bytes 1327112 | tf_op jit(solution)/shard_map/ppermute | solution.py:44
  23.6 31.6 %collective-permute-start.5 = (bf16[144,1152]{1,0:T(8,128)(2,1)}, bf16[144,1152]{1,0:T(8,128)(2,1)}, u32[]{:S(2)}, u32[]{:S(2)}) collective-permute-start(bf16[144,1152]{1,0:T(8,128)(2,1)} %collective-permute-done), channel_id=1, source_target_pairs={{0,4},{1,5},{2,6},{3,7},{4,0},{5,1},{6,2},{7,3},{8,12},{9,13},{10,... | collective-permute-start | bytes 995336 | tf_op jit(solution)/shard_map/ppermute | solution.py:44
  24.2 31.1 %collective-permute-start.4 = (bf16[144,1152]{1,0:T(8,128)(2,1)}, bf16[144,1152]{1,0:T(8,128)(2,1)}, u32[]{:S(2)}, u32[]{:S(2)}) collective-permute-start(bf16[144,1152]{1,0:T(8,128)(2,1)} %collective-permute-done), channel_id=1, source_target_pairs={{0,2},{1,3},{2,0},{3,1},{4,6},{5,7},{6,4},{7,5},{8,10},{9,11},{10,... | collective-permute-start | bytes 995336 | tf_op jit(solution)/shard_map/ppermute | solution.py:44
  55.2 8.9 %collective-permute-start.15 = (bf16[96,1152]{1,0:T(8,128)(2,1)}, bf16[96,1152]{1,0:T(8,128)(2,1)S(1)}, u32[]{:S(2)}, u32[]{:S(2)}) collective-permute-start(bf16[96,1152]{1,0:T(8,128)(2,1)} %copy-done.14), channel_id=1, source_target_pairs={{0,2},{1,3},{2,0},{3,1},{4,6},{5,7},{6,4},{7,5},{8,10},{9,11},{10,... | collective-permute-start | bytes 663560 | tf_op jit(solution)/shard_map/ppermute | solution.py:44
  55.6 4.0 %collective-permute-start.11 = (bf16[96,1152]{1,0:T(8,128)(2,1)}, bf16[96,1152]{1,0:T(8,128)(2,1)S(1)}, u32[]{:S(2)}, u32[]{:S(2)}) collective-permute-start(bf16[96,1152]{1,0:T(8,128)(2,1)} %copy-done.14), channel_id=1, source_target_pairs={{0,1},{1,0},{2,3},{3,2},{4,5},{5,4},{6,7},{7,6},{8,9},{9,8},{10,11... | collective-permute-start | bytes 663560 | tf_op jit(solution)/shard_map/ppermute | solution.py:52
  56.1 4.1 %collective-permute-start.12 = (bf16[192,1152]{1,0:T(8,128)(2,1)S(1)}, bf16[192,1152]{1,0:T(8,128)(2,1)S(1)}, u32[]{:S(2)}, u32[]{:S(2)}) collective-permute-start(bf16[192,1152]{1,0:T(8,128)(2,1)S(1)} %slice.21), channel_id=1, source_target_pairs={{0,1},{1,0},{2,3},{3,2},{4,5},{5,4},{6,7},{7,6},{8,9},{9,8},{10,11... | collective-permute-start | bytes 1327112 | tf_op jit(solution)/shard_map/ppermute | solution.py:52
  57.6 13.3 %collective-permute-start.16 = (bf16[192,1152]{1,0:T(8,128)(2,1)}, bf16[192,1152]{1,0:T(8,128)(2,1)S(1)}, u32[]{:S(2)}, u32[]{:S(2)}) collective-permute-start(bf16[192,1152]{1,0:T(8,128)(2,1)} %collective-permute-done.7), channel_id=1, source_target_pairs={{0,2},{1,3},{2,0},{3,1},{4,6},{5,7},{6,4},{7,5},{8,10},{9,11},{10,... | collective-permute-start | bytes 1327112 | tf_op jit(solution)/shard_map/ppermute | solution.py:44
  59.4 4.6 %collective-permute-start.14 = (bf16[192,1152]{1,0:T(8,128)(2,1)}, bf16[192,1152]{1,0:T(8,128)(2,1)S(1)}, u32[]{:S(2)}, u32[]{:S(2)}) collective-permute-start(bf16[192,1152]{1,0:T(8,128)(2,1)} %collective-permute-done.7), channel_id=1, source_target_pairs={{0,1},{1,0},{2,3},{3,2},{4,5},{5,4},{6,7},{7,6},{8,9},{9,8},{10,11... | collective-permute-start | bytes 1327112 | tf_op jit(solution)/shard_map/ppermute | solution.py:52
  60.2 15.3 %collective-permute-start.8 = (bf16[256,1152]{1,0:T(8,128)(2,1)S(1)}, bf16[256,1152]{1,0:T(8,128)(2,1)S(1)}, u32[]{:S(2)}, u32[]{:S(2)}) collective-permute-start(bf16[256,1152]{1,0:T(8,128)(2,1)S(1)} %copy-done.12), channel_id=1, source_target_pairs={{0,16},{8,24},{16,0},{24,8},{1,17},{9,25},{17,1},{25,9},{2,18},{10... | collective-permute-start | bytes 1769480 | tf_op jit(solution)/shard_map/ppermute | solution.py:36
  75.5 8.1 %collective-permute-start.21 = (bf16[144,1152]{1,0:T(8,128)(2,1)}, bf16[144,1152]{1,0:T(8,128)(2,1)S(1)}, u32[]{:S(2)}, u32[]{:S(2)}) collective-permute-start(bf16[144,1152]{1,0:T(8,128)(2,1)} %collective-permute-done.5), channel_id=1, source_target_pairs={{0,1},{1,0},{2,3},{3,2},{4,5},{5,4},{6,7},{7,6},{8,9},{9,8},{10,11... | collective-permute-start | bytes 995336 | tf_op jit(solution)/shard_map/ppermute | solution.py:52
  75.5 14.8 %collective-permute-start.18 = (bf16[144,1152]{1,0:T(8,128)(2,1)}, bf16[144,1152]{1,0:T(8,128)(2,1)S(1)}, u32[]{:S(2)}, u32[]{:S(2)}) collective-permute-start(bf16[144,1152]{1,0:T(8,128)(2,1)} %collective-permute-done.5), channel_id=1, source_target_pairs={{0,2},{1,3},{2,0},{3,1},{4,6},{5,7},{6,4},{7,5},{8,10},{9,11},{10,... | collective-permute-start | bytes 995336 | tf_op jit(solution)/shard_map/ppermute | solution.py:44
  76.1 4.6 %collective-permute-start.19 = (bf16[144,1152]{1,0:T(8,128)(2,1)}, bf16[144,1152]{1,0:T(8,128)(2,1)S(1)}, u32[]{:S(2)}, u32[]{:S(2)}) collective-permute-start(bf16[144,1152]{1,0:T(8,128)(2,1)} %collective-permute-done), channel_id=1, source_target_pairs={{0,1},{1,0},{2,3},{3,2},{4,5},{5,4},{6,7},{7,6},{8,9},{9,8},{10,11... | collective-permute-start | bytes 995336 | tf_op jit(solution)/shard_map/ppermute | solution.py:52
  77.9 5.8 %collective-permute-start.23 = (bf16[192,1152]{1,0:T(8,128)(2,1)S(1)}, bf16[192,1152]{1,0:T(8,128)(2,1)S(1)}, u32[]{:S(2)}, u32[]{:S(2)}) collective-permute-start(bf16[192,1152]{1,0:T(8,128)(2,1)S(1)} %collective-permute-done.16), channel_id=1, source_target_pairs={{0,1},{1,0},{2,3},{3,2},{4,5},{5,4},{6,7},{7,6},{8,9},{9,8},{10,11... | collective-permute-start | bytes 1327112 | tf_op jit(solution)/shard_map/ppermute | solution.py:52
  79.1 11.2 %collective-permute-start.17 = (bf16[128,1152]{1,0:T(8,128)(2,1)S(1)}, bf16[128,1152]{1,0:T(8,128)(2,1)S(1)}, u32[]{:S(2)}, u32[]{:S(2)}) collective-permute-start(bf16[128,1152]{1,0:T(8,128)(2,1)S(1)} %copy-done.13), channel_id=1, source_target_pairs={{0,16},{8,24},{16,0},{24,8},{1,17},{9,25},{17,1},{25,9},{2,18},{10... | collective-permute-start | bytes 884744 | tf_op jit(solution)/shard_map/ppermute | solution.py:36
  111.2 3.4 %collective-permute-start.25 = (bf16[4,144,1152]{2,1,0:T(8,128)(2,1)S(1)}, bf16[4,144,1152]{2,1,0:T(8,128)(2,1)S(1)}, u32[]{:S(2)}, u32[]{:S(2)}) collective-permute-start(bf16[4,144,1152]{2,1,0:T(8,128)(2,1)S(1)} %get-tuple-element.158), channel_id=1, source_target_pairs={{0,1},{1,0},{2,3},{3,2},{4,5},{5,4},{6,7},{7,6},{8,9},{9,8},{10,11... | collective-permute-start | bytes 3981320 | tf_op jit(solution)/shard_map/ppermute | solution.py:52
  114.6 11.1 %collective-permute-start.26 = (bf16[128,1152]{1,0:T(8,128)(2,1)S(1)}, bf16[128,1152]{1,0:T(8,128)(2,1)S(1)}, u32[]{:S(2)}, u32[]{:S(2)}) collective-permute-start(bf16[128,1152]{1,0:T(8,128)(2,1)S(1)} %shard_map.164), channel_id=1, source_target_pairs={{0,16},{8,24},{16,0},{24,8},{1,17},{9,25},{17,1},{25,9},{2,18},{10... | collective-permute-start | bytes 884744 | tf_op jit(solution)/shard_map/ppermute | solution.py:36
  115.6 10.1 %collective-permute-start.27 = (bf16[144,1152]{1,0:T(8,128)(2,1)S(1)}, bf16[144,1152]{1,0:T(8,128)(2,1)S(1)}, u32[]{:S(2)}, u32[]{:S(2)}) collective-permute-start(bf16[144,1152]{1,0:T(8,128)(2,1)S(1)} %get-tuple-element.160), channel_id=1, source_target_pairs={{0,2},{1,3},{2,0},{3,1},{4,6},{5,7},{6,4},{7,5},{8,10},{9,11},{10,... | collective-permute-start | bytes 995336 | tf_op jit(solution)/shard_map/ppermute | solution.py:44
  125.7 21.4 %collective-permute-start.31 = (bf16[4,288,1152]{2,1,0:T(8,128)(2,1)S(1)}, bf16[4,288,1152]{2,1,0:T(8,128)(2,1)S(1)}, u32[]{:S(2)}, u32[]{:S(2)}) collective-permute-start(bf16[4,288,1152]{2,1,0:T(8,128)(2,1)S(1)} %get-tuple-element.129), channel_id=1, source_target_pairs={{0,1},{1,0},{2,3},{3,2},{4,5},{5,4},{6,7},{7,6},{8,9},{9,8},{10,11... | collective-permute-start | bytes 7962632 | tf_op jit(solution)/shard_map/ppermute | solution.py:52
  125.8 21.3 %collective-permute-start.28 = (bf16[256,1152]{1,0:T(8,128)(2,1)S(1)}, bf16[256,1152]{1,0:T(8,128)(2,1)S(1)}, u32[]{:S(2)}, u32[]{:S(2)}) collective-permute-start(bf16[256,1152]{1,0:T(8,128)(2,1)S(1)} %shard_map.165), channel_id=1, source_target_pairs={{0,16},{8,24},{16,0},{24,8},{1,17},{9,25},{17,1},{25,9},{2,18},{10... | collective-permute-start | bytes 1769480 | tf_op jit(solution)/shard_map/ppermute | solution.py:36
  127.5 18.6 %collective-permute-start.29 = (bf16[144,1152]{1,0:T(8,128)(2,1)S(1)}, bf16[144,1152]{1,0:T(8,128)(2,1)S(1)}, u32[]{:S(2)}, u32[]{:S(2)}) collective-permute-start(bf16[144,1152]{1,0:T(8,128)(2,1)S(1)} %add_convert_fusion.4), channel_id=1, source_target_pairs={{0,4},{1,5},{2,6},{3,7},{4,0},{5,1},{6,2},{7,3},{8,12},{9,13},{10,... | collective-permute-start | bytes 995336 | tf_op jit(solution)/shard_map/ppermute | solution.py:44
  130.7 16.4 %collective-permute-start.30 = (bf16[144,1152]{1,0:T(8,128)(2,1)S(1)}, bf16[144,1152]{1,0:T(8,128)(2,1)S(1)}, u32[]{:S(2)}, u32[]{:S(2)}) collective-permute-start(bf16[144,1152]{1,0:T(8,128)(2,1)S(1)} %get-tuple-element.125), channel_id=1, source_target_pairs={{0,2},{1,3},{2,0},{3,1},{4,6},{5,7},{6,4},{7,5},{8,10},{9,11},{10,... | collective-permute-start | bytes 995336 | tf_op jit(solution)/shard_map/ppermute | solution.py:44
  148.1 16.2 %collective-permute-start.34 = (bf16[288,1152]{1,0:T(8,128)(2,1)S(1)}, bf16[288,1152]{1,0:T(8,128)(2,1)S(1)}, u32[]{:S(2)}, u32[]{:S(2)}) collective-permute-start(bf16[288,1152]{1,0:T(8,128)(2,1)S(1)} %get-tuple-element.154), channel_id=1, source_target_pairs={{0,2},{1,3},{2,0},{3,1},{4,6},{5,7},{6,4},{7,5},{8,10},{9,11},{10,... | collective-permute-start | bytes 1990664 | tf_op jit(solution)/shard_map/ppermute | solution.py:44
  149.0 15.2 %collective-permute-start.33 = (bf16[144,1152]{1,0:T(8,128)(2,1)S(1)}, bf16[144,1152]{1,0:T(8,128)(2,1)S(1)}, u32[]{:S(2)}, u32[]{:S(2)}) collective-permute-start(bf16[144,1152]{1,0:T(8,128)(2,1)S(1)} %add_convert_fusion.3), channel_id=1, source_target_pairs={{0,16},{8,24},{16,0},{24,8},{1,17},{9,25},{17,1},{25,9},{2,18},{10... | collective-permute-start | bytes 995336 | tf_op jit(solution)/shard_map/ppermute | solution.py:36
  149.9 14.3 %collective-permute-start.32 = (bf16[128,1152]{1,0:T(8,128)(2,1)S(1)}, bf16[128,1152]{1,0:T(8,128)(2,1)S(1)}, u32[]{:S(2)}, u32[]{:S(2)}) collective-permute-start(bf16[128,1152]{1,0:T(8,128)(2,1)S(1)} %shard_map.167), channel_id=1, source_target_pairs={{0,16},{8,24},{16,0},{24,8},{1,17},{9,25},{17,1},{25,9},{2,18},{10... | collective-permute-start | bytes 884744 | tf_op jit(solution)/shard_map/ppermute | solution.py:36
  164.2 26.1 %collective-permute-start.35 = (bf16[512,1152]{1,0:T(8,128)(2,1)S(1)}, bf16[512,1152]{1,0:T(8,128)(2,1)S(1)}, u32[]{:S(2)}, u32[]{:S(2)}) collective-permute-start(bf16[512,1152]{1,0:T(8,128)(2,1)S(1)} %shard_map.168), channel_id=1, source_target_pairs={{0,16},{8,24},{16,0},{24,8},{1,17},{9,25},{17,1},{25,9},{2,18},{10... | collective-permute-start | bytes 3538952 | tf_op jit(solution)/shard_map/ppermute | solution.py:36
  165.2 29.9 %collective-permute-start.37 = (bf16[288,1152]{1,0:T(8,128)(2,1)S(1)}, bf16[288,1152]{1,0:T(8,128)(2,1)S(1)}, u32[]{:S(2)}, u32[]{:S(2)}) collective-permute-start(bf16[288,1152]{1,0:T(8,128)(2,1)S(1)} %add_convert_fusion.2), channel_id=1, source_target_pairs={{0,4},{1,5},{2,6},{3,7},{4,0},{5,1},{6,2},{7,3},{8,12},{9,13},{10,... | collective-permute-start | bytes 1990664 | tf_op jit(solution)/shard_map/ppermute | solution.py:44
  167.0 26.5 %collective-permute-start.36 = (bf16[288,1152]{1,0:T(8,128)(2,1)S(1)}, bf16[288,1152]{1,0:T(8,128)(2,1)S(1)}, u32[]{:S(2)}, u32[]{:S(2)}) collective-permute-start(bf16[288,1152]{1,0:T(8,128)(2,1)S(1)} %get-tuple-element.141), channel_id=1, source_target_pairs={{0,2},{1,3},{2,0},{3,1},{4,6},{5,7},{6,4},{7,5},{8,10},{9,11},{10,... | collective-permute-start | bytes 1990664 | tf_op jit(solution)/shard_map/ppermute | solution.py:44
  (24 other events, 230.7 us)

commit v5 on v4

--- a/solution.py
+++ b/solution.py
@@ -298,7 +298,7 @@
     proj_whole = assemble(proj_found)
     skip_w = [assemble(last, whole) for last, whole in zip(skip_last, skip_w)]
     skip_parts = [(cut, 0, stride), (stride - cut, cut, stride)]
-    (from_dec,) = row_call(decoder_part, [dec_rows], skip_w, skip_parts, 1, 256, 20, out_type=jnp.float32, half=0)
+    (from_dec,) = row_call(decoder_part, [dec_rows], skip_w, skip_parts, 1, 512, 20, out_type=jnp.float32, half=0)
     enc2, proj_last, proj_whole, from_dec, skip_w = together((enc2, proj_last, proj_whole, from_dec, skip_w))
     proj_whole = assemble(proj_last, proj_whole)
     enc_other = (enc0, enc1, enc2)

time: 199 us -> 198 us (level)
  no operation moved by 1% of the time
where the time goes in v5:
time: 198 us
  waiting for transfers between devices  92.9 us (47%)
  Pallas kernels  47.2 us (24%)
  starting transfers between devices  35.6 us (18%)
  local copies, waits for them, and re-layouts  12 us (6%)
  other arithmetic  8.93 us (5%)
    ppermute x15, waiting for transfers between devices, to_chips(): lax.ppermute(value, 'dp', [(2 * a + c, 2 * b + c) for a, b in pairs for c...  58.8 us
    pallas_call x7, Pallas kernels, row_call(): pl.pallas_call(kernel, grid=(rows // tile,), in_specs=[taken] * len(row_a...  30.9 us
    ppermute x9, waiting for transfers between devices, to_partner(): return lax.ppermute(value, 'section', pairs)  30.8 us
    ppermute x15, starting transfers between devices, to_chips(): lax.ppermute(value, 'dp', [(2 * a + c, 2 * b + c) for a, b in pairs for c...  20.9 us
    pallas_call x2, Pallas kernels, weight_grad(): pl.pallas_call(kernel, grid=(len(lefts) * steps,), in_specs=[spec(n, part...  12.8 us
    ppermute x9, starting transfers between devices, to_partner(): return lax.ppermute(value, 'section', pairs)  11.7 us
    dynamic_update_slice x12, local copies, waits for them, and re-layouts, assemble(): lax.dynamic_update_slice(whole, piece[None, None], (chip ^ k, core, 0, 0))  5.44 us
    broadcast_in_dim x2, other arithmetic, body(): return streams + tuple((value[None] for value in new_proj + new_skip))  4.83 us
  transfers between devices with their start and end apart: 38, of which 15 were waited for; matrix products, arithmetic and copies ran while one was open for 8% of the time, Pallas kernels for 14%

profile of v5, /device:TPU:0, one launch (start us, length us, event | category | flops | bytes accessed | tf_op | source)
XLA Modules:
  0.0 197.9 jit_solution(8497146558377691572)
XLA Ops:
  1.9 3.0 %collective-permute-start = (bf16[144,1152]{1,0:T(8,128)(2,1)S(1)}, bf16[144,1152]{1,0:T(8,128)(2,1)}, u32[]{:S(2)}, u32[]{:S(2)}) collective-permute-start(bf16[144,1152]{1,0:T(8,128)(2,1)S(1)} %bitcast_convert_fusion.1), channel_id=1, source_target_pairs={{0,16},{8,24},{16,0},{24,8},{1,17},{9,25},{17,1},{25,9},{2,18},{10... | collective-permute-start | bytes 995336 | tf_op jit(solution)/shard_map/ppermute | solution.py:36
  6.4 2.7 %collective-permute-start.2 = (bf16[96,1152]{1,0:T(8,128)(2,1)S(1)}, bf16[96,1152]{1,0:T(8,128)(2,1)S(1)}, u32[]{:S(2)}, u32[]{:S(2)}) collective-permute-start(bf16[96,1152]{1,0:T(8,128)(2,1)S(1)} %slice.20), channel_id=1, source_target_pairs={{0,4},{1,5},{2,6},{3,7},{4,0},{5,1},{6,2},{7,3},{8,12},{9,13},{10,... | collective-permute-start | bytes 663560 | tf_op jit(solution)/shard_map/ppermute | solution.py:44
  9.1 1.6 collective-permute-start.1
  10.8 8.3 %collective-permute-done.2 = bf16[96,1152]{1,0:T(8,128)(2,1)S(1)} collective-permute-done((bf16[96,1152]{1,0:T(8,128)(2,1)S(1)}, bf16[96,1152]{1,0:T(8,128)(2,1)S(1)}, u32[]{:S(2)}, u32[]{:S(2)}) %collective-permute-start.2) | collective-permute-done | bytes 221216 | tf_op jit(solution)/shard_map/ppermute | solution.py:44
  21.1 2.5 %collective-permute-start.6 = (bf16[192,1152]{1,0:T(8,128)(2,1)S(1)}, bf16[192,1152]{1,0:T(8,128)(2,1)}, u32[]{:S(2)}, u32[]{:S(2)}) collective-permute-start(bf16[192,1152]{1,0:T(8,128)(2,1)S(1)} %slice.21), channel_id=1, source_target_pairs={{0,2},{1,3},{2,0},{3,1},{4,6},{5,7},{6,4},{7,5},{8,10},{9,11},{10,... | collective-permute-start | bytes 1327112 | tf_op jit(solution)/shard_map/ppermute | solution.py:44
  24.7 1.7 slice.24
  26.4 1.9 slice.23
  28.3 26.9 %collective-permute-done.5 = bf16[144,1152]{1,0:T(8,128)(2,1)} collective-permute-done((bf16[144,1152]{1,0:T(8,128)(2,1)}, bf16[144,1152]{1,0:T(8,128)(2,1)}, u32[]{:S(2)}, u32[]{:S(2)}) %collective-permute-start.5) | collective-permute-done | bytes 331808 | tf_op jit(solution)/shard_map/ppermute | solution.py:44
  57.6 1.8 collective-permute-start.16
  60.2 1.6 collective-permute-start.8
  64.2 6.8 %collective-permute-done.16 = bf16[192,1152]{1,0:T(8,128)(2,1)S(1)} collective-permute-done((bf16[192,1152]{1,0:T(8,128)(2,1)}, bf16[192,1152]{1,0:T(8,128)(2,1)S(1)}, u32[]{:S(2)}, u32[]{:S(2)}) %collective-permute-start.16) | collective-permute-done | bytes 442400 | tf_op jit(solution)/shard_map/ppermute | solution.py:44
  70.9 4.6 %collective-permute-done.8.refs_1_ = bf16[256,1152]{1,0:T(8,128)(2,1)S(1)} collective-permute-done((bf16[256,1152]{1,0:T(8,128)(2,1)S(1)}, bf16[256,1152]{1,0:T(8,128)(2,1)S(1)}, u32[]{:S(2)}, u32[]{:S(2)}) %collective-permute-start.8) | collective-permute-done | bytes 589856 | tf_op jit(solution)/shard_map/ppermute | solution.py:36
  79.1 1.5 collective-permute-start.17
  83.8 6.2 %shard_map.160.refs_0_ = f32[1024,1152]{1,0:T(8,128)S(1)} custom-call(bf16[1024,1152]{1,0:T(8,128)(2,1)S(1)} %bitcast.148, bf16[768,1152]{1,0:T(8,128)(2,1)S(1)} %bitcast.143, bf16[1536,1152]{1,0:T(8,128)(2,1)S(1)} %bitcast.140), custom_call_target="tpu_custom_call" | custom-call | flops 1000 | bytes 1000 | tf_op jit(solution)/shard_map/pallas_call | solution.py:148
  91.8 3.5 %shard_map.161.refs_1_ = bf16[1024,1152]{1,0:T(8,128)(2,1)S(1)} custom-call(bf16[640,1152]{1,0:T(8,128)(2,1)S(1)} %collective-permute-done.3.refs_0_, bf16[256,1152]{1,0:T(8,128)(2,1)S(1)} %collective-permute-done.8.refs_1_, bf16[128,1152]{1,0:T(8,128)(2,1)S(1)} %collective-permute-done.17.refs_2_, bf16[1152,1152]{1,0:T(8,128)(2,1)S(1)} %bitcast.135), custom_call_target="tpu_custom_call" | custom-call | flops 1000 | bytes 1000 | tf_op jit(solution)/shard_map/pallas_call | solution.py:188
  95.3 10.6 %shard_map.162 = (bf16[1024,1152]{1,0:T(8,128)(2,1)}, bf16[1024,1152]{1,0:T(8,128)(2,1)S(1)}, bf16[1024,1152]{1,0:T(8,128)(2,1)S(1)}) custom-call(f32[1024,1152]{1,0:T(8,128)S(1)} %shard_map.160.refs_0_, bf16[1024,1152]{1,0:T(8,128)(2,1)S(1)} %shard_map.161.refs_1_, bf16[1024,1152]{1,0:T(8,128)(2,1)S(1)} %bitcast.150, bf16[768,1152]{1,0:T(8,128)(2,1)S(1)} %bitcast.144, ...), custom_call_target="tpu_custom_call" | custom-call | flops 1000 | bytes 1000 | tf_op jit(solution)/shard_map/pallas_call | solution.py:148
  105.9 4.6 %shard_map.163 = bf16[1152,1152]{1,0:T(8,128)(2,1)S(1)} custom-call(bf16[640,1152]{1,0:T(8,128)(2,1)S(1)} %collective-permute-done.3.refs_0_, bf16[256,1152]{1,0:T(8,128)(2,1)S(1)} %collective-permute-done.8.refs_1_, bf16[128,1152]{1,0:T(8,128)(2,1)S(1)} %collective-permute-done.17.refs_2_, bf16[1024,1152]{1,0:T(8,128)(2,1)S(1)} %get-tuple-element.130.refs_3_.refs_0_), custom_call_target="tpu_custom_call" | custom-call | flops 1000 | bytes 1000 | tf_op jit(solution)/shard_map/pallas_call | solution.py:241
  112.2 2.1 %shard_map.165 = bf16[256,1152]{1,0:T(8,128)(2,1)S(1)} custom-call(bf16[1024,1152]{1,0:T(8,128)(2,1)S(1)} %get-tuple-element.130.refs_3_.refs_0_, bf16[1152,1152]{1,0:T(8,128)(2,1)S(1)} %bitcast.137), custom_call_target="tpu_custom_call" | custom-call | flops 1000 | bytes 1000 | tf_op jit(solution)/shard_map/pallas_call | solution.py:148
  115.3 1.5 collective-permute-start.27
  116.8 8.1 %shard_map.166 = bf16[2304,1152]{1,0:T(8,128)(2,1)S(1)} custom-call(bf16[1024,1152]{1,0:T(8,128)(2,1)S(1)} %bitcast.149, bf16[1024,1152]{1,0:T(8,128)(2,1)S(1)} %shard_map.161.refs_1_, bf16[1024,1152]{1,0:T(8,128)(2,1)S(1)} %get-tuple-element.143.refs_2_.refs_0_), custom_call_target="tpu_custom_call" | custom-call | flops 1000 | bytes 1000 | tf_op jit(solution)/shard_map/pallas_call | solution.py:241
  125.5 1.6 collective-permute-start.28
  127.2 3.2 %collective-permute-start.29 = (bf16[144,1152]{1,0:T(8,128)(2,1)S(1)}, bf16[144,1152]{1,0:T(8,128)(2,1)S(1)}, u32[]{:S(2)}, u32[]{:S(2)}) collective-permute-start(bf16[144,1152]{1,0:T(8,128)(2,1)S(1)} %add_convert_fusion.4), channel_id=1, source_target_pairs={{0,4},{1,5},{2,6},{3,7},{4,0},{5,1},{6,2},{7,3},{8,12},{9,13},{10,... | collective-permute-start | bytes 995336 | tf_op jit(solution)/shard_map/ppermute | solution.py:44
  132.5 2.4 %shard_map.168 = bf16[512,1152]{1,0:T(8,128)(2,1)S(1)} custom-call(bf16[1024,1152]{1,0:T(8,128)(2,1)S(1)} %get-tuple-element.130.refs_3_.refs_0_, bf16[1152,1152]{1,0:T(8,128)(2,1)S(1)} %bitcast.139), custom_call_target="tpu_custom_call" | custom-call | flops 1000 | bytes 1000 | tf_op jit(solution)/shard_map/pallas_call | solution.py:148
  134.8 11.0 %collective-permute-done.29 = bf16[144,1152]{1,0:T(8,128)(2,1)S(1)} collective-permute-done((bf16[144,1152]{1,0:T(8,128)(2,1)S(1)}, bf16[144,1152]{1,0:T(8,128)(2,1)S(1)}, u32[]{:S(2)}, u32[]{:S(2)}) %collective-permute-start.29) | collective-permute-done | bytes 331808 | tf_op jit(solution)/shard_map/ppermute | solution.py:44
  151.0 12.9 %collective-permute-done.32 = bf16[128,1152]{1,0:T(8,128)(2,1)S(1)} collective-permute-done((bf16[128,1152]{1,0:T(8,128)(2,1)S(1)}, bf16[128,1152]{1,0:T(8,128)(2,1)S(1)}, u32[]{:S(2)}, u32[]{:S(2)}) %collective-permute-start.32) | collective-permute-done | bytes 294944 | tf_op jit(solution)/shard_map/ppermute | solution.py:36
  164.9 1.8 collective-permute-start.37
  167.5 1.8 fusion.6
  169.3 7.3 %shard_map.169 = bf16[1024,1152]{1,0:T(8,128)(2,1)} custom-call(bf16[1024,1152]{1,0:T(8,128)(2,1)S(1)} %get-tuple-element.143.refs_2_.refs_0_, bf16[768,1152]{1,0:T(8,128)(2,1)S(1)} %bitcast.145, bf16[1536,1152]{1,0:T(8,128)(2,1)S(1)} %bitcast.142), custom_call_target="tpu_custom_call" | custom-call | flops 1000 | bytes 1000 | tf_op jit(solution)/shard_map/pallas_call | solution.py:148
  176.7 13.3 %collective-permute-done.35 = bf16[512,1152]{1,0:T(8,128)(2,1)S(1)} collective-permute-done((bf16[512,1152]{1,0:T(8,128)(2,1)S(1)}, bf16[512,1152]{1,0:T(8,128)(2,1)S(1)}, u32[]{:S(2)}, u32[]{:S(2)}) %collective-permute-start.35) | collective-permute-done | bytes 1179680 | tf_op jit(solution)/shard_map/ppermute | solution.py:36
  190.2 3.1 %collective-permute-done.36 = bf16[288,1152]{1,0:T(8,128)(2,1)S(1)} collective-permute-done((bf16[288,1152]{1,0:T(8,128)(2,1)S(1)}, bf16[288,1152]{1,0:T(8,128)(2,1)S(1)}, u32[]{:S(2)}, u32[]{:S(2)}) %collective-permute-start.36) | collective-permute-done | bytes 663584 | tf_op jit(solution)/shard_map/ppermute | solution.py:44
  193.2 1.6 collective-permute-done.37
  194.8 3.1 %fusion.8 = (f32[1,288,1152]{2,1,0:T(8,128)}, f32[1,288,1152]{2,1,0:T(8,128)}, f32[1,288,1152]{2,1,0:T(8,128)}) fusion(bf16[288,1152]{1,0:T(8,128)(2,1)S(1)} %collective-permute-done.37, bf16[288,1152]{1,0:T(8,128)(2,1)S(1)} %collective-permute-done.36, bf16[288,1152]{1,0:T(8,128)(2,1)S(1)} %get-tuple-element.145, f32[1,288,1152]{2,1,0:T(8,128)S(1)} %copy-done.6, ...), kind=kLoop, calls=%fused_computation.61 | loop fusion | flops 5971968 | bytes 9953280 | tf_op jit(solution)/shard_map/broadcast_in_dim | solution.py:362
  (139 shorter events, 32.1 us)
Async XLA Ops:
  1.9 17.4 %collective-permute-start = (bf16[144,1152]{1,0:T(8,128)(2,1)S(1)}, bf16[144,1152]{1,0:T(8,128)(2,1)}, u32[]{:S(2)}, u32[]{:S(2)}) collective-permute-start(bf16[144,1152]{1,0:T(8,128)(2,1)S(1)} %bitcast_convert_fusion.1), channel_id=1, source_target_pairs={{0,16},{8,24},{16,0},{24,8},{1,17},{9,25},{17,1},{25,9},{2,18},{10... | collective-permute-start | bytes 995336 | tf_op jit(solution)/shard_map/ppermute | solution.py:36
  6.4 12.7 %collective-permute-start.2 = (bf16[96,1152]{1,0:T(8,128)(2,1)S(1)}, bf16[96,1152]{1,0:T(8,128)(2,1)S(1)}, u32[]{:S(2)}, u32[]{:S(2)}) collective-permute-start(bf16[96,1152]{1,0:T(8,128)(2,1)S(1)} %slice.20), channel_id=1, source_target_pairs={{0,4},{1,5},{2,6},{3,7},{4,0},{5,1},{6,2},{7,3},{8,12},{9,13},{10,... | collective-permute-start | bytes 663560 | tf_op jit(solution)/shard_map/ppermute | solution.py:44
  9.1 10.2 %collective-permute-start.1 = (bf16[96,1152]{1,0:T(8,128)(2,1)S(1)}, bf16[96,1152]{1,0:T(8,128)(2,1)S(1)}, u32[]{:S(2)}, u32[]{:S(2)}) collective-permute-start(bf16[96,1152]{1,0:T(8,128)(2,1)S(1)} %slice.20), channel_id=1, source_target_pairs={{0,2},{1,3},{2,0},{3,1},{4,6},{5,7},{6,4},{7,5},{8,10},{9,11},{10,... | collective-permute-start | bytes 663560 | tf_op jit(solution)/shard_map/ppermute | solution.py:44
  19.3 35.9 %collective-permute-start.3 = (bf16[640,1152]{1,0:T(8,128)(2,1)S(1)}, bf16[640,1152]{1,0:T(8,128)(2,1)S(1)}, u32[]{:S(2)}, u32[]{:S(2)}) collective-permute-start(bf16[640,1152]{1,0:T(8,128)(2,1)S(1)} %slice.22), channel_id=1, source_target_pairs={{0,16},{8,24},{16,0},{24,8},{1,17},{9,25},{17,1},{25,9},{2,18},{10... | collective-permute-start | bytes 4423688 | tf_op jit(solution)/shard_map/ppermute | solution.py:36
  19.8 35.5 %collective-permute-start.7 = (bf16[192,1152]{1,0:T(8,128)(2,1)S(1)}, bf16[192,1152]{1,0:T(8,128)(2,1)}, u32[]{:S(2)}, u32[]{:S(2)}) collective-permute-start(bf16[192,1152]{1,0:T(8,128)(2,1)S(1)} %slice.21), channel_id=1, source_target_pairs={{0,4},{1,5},{2,6},{3,7},{4,0},{5,1},{6,2},{7,3},{8,12},{9,13},{10,... | collective-permute-start | bytes 1327112 | tf_op jit(solution)/shard_map/ppermute | solution.py:44
  21.1 34.1 %collective-permute-start.6 = (bf16[192,1152]{1,0:T(8,128)(2,1)S(1)}, bf16[192,1152]{1,0:T(8,128)(2,1)}, u32[]{:S(2)}, u32[]{:S(2)}) collective-permute-start(bf16[192,1152]{1,0:T(8,128)(2,1)S(1)} %slice.21), channel_id=1, source_target_pairs={{0,2},{1,3},{2,0},{3,1},{4,6},{5,7},{6,4},{7,5},{8,10},{9,11},{10,... | collective-permute-start | bytes 1327112 | tf_op jit(solution)/shard_map/ppermute | solution.py:44
  23.6 31.6 %collective-permute-start.5 = (bf16[144,1152]{1,0:T(8,128)(2,1)}, bf16[144,1152]{1,0:T(8,128)(2,1)}, u32[]{:S(2)}, u32[]{:S(2)}) collective-permute-start(bf16[144,1152]{1,0:T(8,128)(2,1)} %collective-permute-done), channel_id=1, source_target_pairs={{0,4},{1,5},{2,6},{3,7},{4,0},{5,1},{6,2},{7,3},{8,12},{9,13},{10,... | collective-permute-start | bytes 995336 | tf_op jit(solution)/shard_map/ppermute | solution.py:44
  24.2 31.1 %collective-permute-start.4 = (bf16[144,1152]{1,0:T(8,128)(2,1)}, bf16[144,1152]{1,0:T(8,128)(2,1)}, u32[]{:S(2)}, u32[]{:S(2)}) collective-permute-start(bf16[144,1152]{1,0:T(8,128)(2,1)} %collective-permute-done), channel_id=1, source_target_pairs={{0,2},{1,3},{2,0},{3,1},{4,6},{5,7},{6,4},{7,5},{8,10},{9,11},{10,... | collective-permute-start | bytes 995336 | tf_op jit(solution)/shard_map/ppermute | solution.py:44
  55.2 8.9 %collective-permute-start.15 = (bf16[96,1152]{1,0:T(8,128)(2,1)}, bf16[96,1152]{1,0:T(8,128)(2,1)S(1)}, u32[]{:S(2)}, u32[]{:S(2)}) collective-permute-start(bf16[96,1152]{1,0:T(8,128)(2,1)} %copy-done.14), channel_id=1, source_target_pairs={{0,2},{1,3},{2,0},{3,1},{4,6},{5,7},{6,4},{7,5},{8,10},{9,11},{10,... | collective-permute-start | bytes 663560 | tf_op jit(solution)/shard_map/ppermute | solution.py:44
  55.6 4.0 %collective-permute-start.11 = (bf16[96,1152]{1,0:T(8,128)(2,1)}, bf16[96,1152]{1,0:T(8,128)(2,1)S(1)}, u32[]{:S(2)}, u32[]{:S(2)}) collective-permute-start(bf16[96,1152]{1,0:T(8,128)(2,1)} %copy-done.14), channel_id=1, source_target_pairs={{0,1},{1,0},{2,3},{3,2},{4,5},{5,4},{6,7},{7,6},{8,9},{9,8},{10,11... | collective-permute-start | bytes 663560 | tf_op jit(solution)/shard_map/ppermute | solution.py:52
  56.1 4.1 %collective-permute-start.12 = (bf16[192,1152]{1,0:T(8,128)(2,1)S(1)}, bf16[192,1152]{1,0:T(8,128)(2,1)S(1)}, u32[]{:S(2)}, u32[]{:S(2)}) collective-permute-start(bf16[192,1152]{1,0:T(8,128)(2,1)S(1)} %slice.21), channel_id=1, source_target_pairs={{0,1},{1,0},{2,3},{3,2},{4,5},{5,4},{6,7},{7,6},{8,9},{9,8},{10,11... | collective-permute-start | bytes 1327112 | tf_op jit(solution)/shard_map/ppermute | solution.py:52
  57.6 13.3 %collective-permute-start.16 = (bf16[192,1152]{1,0:T(8,128)(2,1)}, bf16[192,1152]{1,0:T(8,128)(2,1)S(1)}, u32[]{:S(2)}, u32[]{:S(2)}) collective-permute-start(bf16[192,1152]{1,0:T(8,128)(2,1)} %collective-permute-done.7), channel_id=1, source_target_pairs={{0,2},{1,3},{2,0},{3,1},{4,6},{5,7},{6,4},{7,5},{8,10},{9,11},{10,... | collective-permute-start | bytes 1327112 | tf_op jit(solution)/shard_map/ppermute | solution.py:44
  59.4 4.6 %collective-permute-start.14 = (bf16[192,1152]{1,0:T(8,128)(2,1)}, bf16[192,1152]{1,0:T(8,128)(2,1)S(1)}, u32[]{:S(2)}, u32[]{:S(2)}) collective-permute-start(bf16[192,1152]{1,0:T(8,128)(2,1)} %collective-permute-done.7), channel_id=1, source_target_pairs={{0,1},{1,0},{2,3},{3,2},{4,5},{5,4},{6,7},{7,6},{8,9},{9,8},{10,11... | collective-permute-start | bytes 1327112 | tf_op jit(solution)/shard_map/ppermute | solution.py:52
  60.2 15.3 %collective-permute-start.8 = (bf16[256,1152]{1,0:T(8,128)(2,1)S(1)}, bf16[256,1152]{1,0:T(8,128)(2,1)S(1)}, u32[]{:S(2)}, u32[]{:S(2)}) collective-permute-start(bf16[256,1152]{1,0:T(8,128)(2,1)S(1)} %copy-done.12), channel_id=1, source_target_pairs={{0,16},{8,24},{16,0},{24,8},{1,17},{9,25},{17,1},{25,9},{2,18},{10... | collective-permute-start | bytes 1769480 | tf_op jit(solution)/shard_map/ppermute | solution.py:36
  75.5 8.1 %collective-permute-start.21 = (bf16[144,1152]{1,0:T(8,128)(2,1)}, bf16[144,1152]{1,0:T(8,128)(2,1)S(1)}, u32[]{:S(2)}, u32[]{:S(2)}) collective-permute-start(bf16[144,1152]{1,0:T(8,128)(2,1)} %collective-permute-done.5), channel_id=1, source_target_pairs={{0,1},{1,0},{2,3},{3,2},{4,5},{5,4},{6,7},{7,6},{8,9},{9,8},{10,11... | collective-permute-start | bytes 995336 | tf_op jit(solution)/shard_map/ppermute | solution.py:52
  75.5 14.5 %collective-permute-start.18 = (bf16[144,1152]{1,0:T(8,128)(2,1)}, bf16[144,1152]{1,0:T(8,128)(2,1)S(1)}, u32[]{:S(2)}, u32[]{:S(2)}) collective-permute-start(bf16[144,1152]{1,0:T(8,128)(2,1)} %collective-permute-done.5), channel_id=1, source_target_pairs={{0,2},{1,3},{2,0},{3,1},{4,6},{5,7},{6,4},{7,5},{8,10},{9,11},{10,... | collective-permute-start | bytes 995336 | tf_op jit(solution)/shard_map/ppermute | solution.py:44
  76.1 4.6 %collective-permute-start.19 = (bf16[144,1152]{1,0:T(8,128)(2,1)}, bf16[144,1152]{1,0:T(8,128)(2,1)S(1)}, u32[]{:S(2)}, u32[]{:S(2)}) collective-permute-start(bf16[144,1152]{1,0:T(8,128)(2,1)} %collective-permute-done), channel_id=1, source_target_pairs={{0,1},{1,0},{2,3},{3,2},{4,5},{5,4},{6,7},{7,6},{8,9},{9,8},{10,11... | collective-permute-start | bytes 995336 | tf_op jit(solution)/shard_map/ppermute | solution.py:52
  77.9 5.8 %collective-permute-start.23 = (bf16[192,1152]{1,0:T(8,128)(2,1)S(1)}, bf16[192,1152]{1,0:T(8,128)(2,1)S(1)}, u32[]{:S(2)}, u32[]{:S(2)}) collective-permute-start(bf16[192,1152]{1,0:T(8,128)(2,1)S(1)} %collective-permute-done.16), channel_id=1, source_target_pairs={{0,1},{1,0},{2,3},{3,2},{4,5},{5,4},{6,7},{7,6},{8,9},{9,8},{10,11... | collective-permute-start | bytes 1327112 | tf_op jit(solution)/shard_map/ppermute | solution.py:52
  79.1 10.9 %collective-permute-start.17 = (bf16[128,1152]{1,0:T(8,128)(2,1)S(1)}, bf16[128,1152]{1,0:T(8,128)(2,1)S(1)}, u32[]{:S(2)}, u32[]{:S(2)}) collective-permute-start(bf16[128,1152]{1,0:T(8,128)(2,1)S(1)} %copy-done.13), channel_id=1, source_target_pairs={{0,16},{8,24},{16,0},{24,8},{1,17},{9,25},{17,1},{25,9},{2,18},{10... | collective-permute-start | bytes 884744 | tf_op jit(solution)/shard_map/ppermute | solution.py:36
  110.9 3.4 %collective-permute-start.25 = (bf16[4,144,1152]{2,1,0:T(8,128)(2,1)S(1)}, bf16[4,144,1152]{2,1,0:T(8,128)(2,1)S(1)}, u32[]{:S(2)}, u32[]{:S(2)}) collective-permute-start(bf16[4,144,1152]{2,1,0:T(8,128)(2,1)S(1)} %get-tuple-element.158), channel_id=1, source_target_pairs={{0,1},{1,0},{2,3},{3,2},{4,5},{5,4},{6,7},{7,6},{8,9},{9,8},{10,11... | collective-permute-start | bytes 3981320 | tf_op jit(solution)/shard_map/ppermute | solution.py:52
  114.3 11.1 %collective-permute-start.26 = (bf16[128,1152]{1,0:T(8,128)(2,1)S(1)}, bf16[128,1152]{1,0:T(8,128)(2,1)S(1)}, u32[]{:S(2)}, u32[]{:S(2)}) collective-permute-start(bf16[128,1152]{1,0:T(8,128)(2,1)S(1)} %shard_map.164), channel_id=1, source_target_pairs={{0,16},{8,24},{16,0},{24,8},{1,17},{9,25},{17,1},{25,9},{2,18},{10... | collective-permute-start | bytes 884744 | tf_op jit(solution)/shard_map/ppermute | solution.py:36
  115.3 10.1 %collective-permute-start.27 = (bf16[144,1152]{1,0:T(8,128)(2,1)S(1)}, bf16[144,1152]{1,0:T(8,128)(2,1)S(1)}, u32[]{:S(2)}, u32[]{:S(2)}) collective-permute-start(bf16[144,1152]{1,0:T(8,128)(2,1)S(1)} %get-tuple-element.160), channel_id=1, source_target_pairs={{0,2},{1,3},{2,0},{3,1},{4,6},{5,7},{6,4},{7,5},{8,10},{9,11},{10,... | collective-permute-start | bytes 995336 | tf_op jit(solution)/shard_map/ppermute | solution.py:44
  125.4 21.4 %collective-permute-start.31 = (bf16[4,288,1152]{2,1,0:T(8,128)(2,1)S(1)}, bf16[4,288,1152]{2,1,0:T(8,128)(2,1)S(1)}, u32[]{:S(2)}, u32[]{:S(2)}) collective-permute-start(bf16[4,288,1152]{2,1,0:T(8,128)(2,1)S(1)} %get-tuple-element.129), channel_id=1, source_target_pairs={{0,1},{1,0},{2,3},{3,2},{4,5},{5,4},{6,7},{7,6},{8,9},{9,8},{10,11... | collective-permute-start | bytes 7962632 | tf_op jit(solution)/shard_map/ppermute | solution.py:52
  125.5 21.3 %collective-permute-start.28 = (bf16[256,1152]{1,0:T(8,128)(2,1)S(1)}, bf16[256,1152]{1,0:T(8,128)(2,1)S(1)}, u32[]{:S(2)}, u32[]{:S(2)}) collective-permute-start(bf16[256,1152]{1,0:T(8,128)(2,1)S(1)} %shard_map.165), channel_id=1, source_target_pairs={{0,16},{8,24},{16,0},{24,8},{1,17},{9,25},{17,1},{25,9},{2,18},{10... | collective-permute-start | bytes 1769480 | tf_op jit(solution)/shard_map/ppermute | solution.py:36
  127.2 18.6 %collective-permute-start.29 = (bf16[144,1152]{1,0:T(8,128)(2,1)S(1)}, bf16[144,1152]{1,0:T(8,128)(2,1)S(1)}, u32[]{:S(2)}, u32[]{:S(2)}) collective-permute-start(bf16[144,1152]{1,0:T(8,128)(2,1)S(1)} %add_convert_fusion.4), channel_id=1, source_target_pairs={{0,4},{1,5},{2,6},{3,7},{4,0},{5,1},{6,2},{7,3},{8,12},{9,13},{10,... | collective-permute-start | bytes 995336 | tf_op jit(solution)/shard_map/ppermute | solution.py:44
  130.4 16.4 %collective-permute-start.30 = (bf16[144,1152]{1,0:T(8,128)(2,1)S(1)}, bf16[144,1152]{1,0:T(8,128)(2,1)S(1)}, u32[]{:S(2)}, u32[]{:S(2)}) collective-permute-start(bf16[144,1152]{1,0:T(8,128)(2,1)S(1)} %get-tuple-element.125), channel_id=1, source_target_pairs={{0,2},{1,3},{2,0},{3,1},{4,6},{5,7},{6,4},{7,5},{8,10},{9,11},{10,... | collective-permute-start | bytes 995336 | tf_op jit(solution)/shard_map/ppermute | solution.py:44
  147.7 16.2 %collective-permute-start.34 = (bf16[288,1152]{1,0:T(8,128)(2,1)S(1)}, bf16[288,1152]{1,0:T(8,128)(2,1)S(1)}, u32[]{:S(2)}, u32[]{:S(2)}) collective-permute-start(bf16[288,1152]{1,0:T(8,128)(2,1)S(1)} %get-tuple-element.154), channel_id=1, source_target_pairs={{0,2},{1,3},{2,0},{3,1},{4,6},{5,7},{6,4},{7,5},{8,10},{9,11},{10,... | collective-permute-start | bytes 1990664 | tf_op jit(solution)/shard_map/ppermute | solution.py:44
  148.7 15.2 %collective-permute-start.33 = (bf16[144,1152]{1,0:T(8,128)(2,1)S(1)}, bf16[144,1152]{1,0:T(8,128)(2,1)S(1)}, u32[]{:S(2)}, u32[]{:S(2)}) collective-permute-start(bf16[144,1152]{1,0:T(8,128)(2,1)S(1)} %add_convert_fusion.3), channel_id=1, source_target_pairs={{0,16},{8,24},{16,0},{24,8},{1,17},{9,25},{17,1},{25,9},{2,18},{10... | collective-permute-start | bytes 995336 | tf_op jit(solution)/shard_map/ppermute | solution.py:36
  149.5 14.3 %collective-permute-start.32 = (bf16[128,1152]{1,0:T(8,128)(2,1)S(1)}, bf16[128,1152]{1,0:T(8,128)(2,1)S(1)}, u32[]{:S(2)}, u32[]{:S(2)}) collective-permute-start(bf16[128,1152]{1,0:T(8,128)(2,1)S(1)} %shard_map.167), channel_id=1, source_target_pairs={{0,16},{8,24},{16,0},{24,8},{1,17},{9,25},{17,1},{25,9},{2,18},{10... | collective-permute-start | bytes 884744 | tf_op jit(solution)/shard_map/ppermute | solution.py:36
  163.9 26.1 %collective-permute-start.35 = (bf16[512,1152]{1,0:T(8,128)(2,1)S(1)}, bf16[512,1152]{1,0:T(8,128)(2,1)S(1)}, u32[]{:S(2)}, u32[]{:S(2)}) collective-permute-start(bf16[512,1152]{1,0:T(8,128)(2,1)S(1)} %shard_map.168), channel_id=1, source_target_pairs={{0,16},{8,24},{16,0},{24,8},{1,17},{9,25},{17,1},{25,9},{2,18},{10... | collective-permute-start | bytes 3538952 | tf_op jit(solution)/shard_map/ppermute | solution.py:36
  164.9 29.9 %collective-permute-start.37 = (bf16[288,1152]{1,0:T(8,128)(2,1)S(1)}, bf16[288,1152]{1,0:T(8,128)(2,1)S(1)}, u32[]{:S(2)}, u32[]{:S(2)}) collective-permute-start(bf16[288,1152]{1,0:T(8,128)(2,1)S(1)} %add_convert_fusion.2), channel_id=1, source_target_pairs={{0,4},{1,5},{2,6},{3,7},{4,0},{5,1},{6,2},{7,3},{8,12},{9,13},{10,... | collective-permute-start | bytes 1990664 | tf_op jit(solution)/shard_map/ppermute | solution.py:44
  166.7 26.5 %collective-permute-start.36 = (bf16[288,1152]{1,0:T(8,128)(2,1)S(1)}, bf16[288,1152]{1,0:T(8,128)(2,1)S(1)}, u32[]{:S(2)}, u32[]{:S(2)}) collective-permute-start(bf16[288,1152]{1,0:T(8,128)(2,1)S(1)} %get-tuple-element.141), channel_id=1, source_target_pairs={{0,2},{1,3},{2,0},{3,1},{4,6},{5,7},{6,4},{7,5},{8,10},{9,11},{10,... | collective-permute-start | bytes 1990664 | tf_op jit(solution)/shard_map/ppermute | solution.py:44
  (24 other events, 230.7 us)
